TPU v7x, 128 devices: a whole 4x4x4 slice. The times are simulated.
128 devices in a mesh: grp: 8 (over x, core), seq: 16 (over y, z).
Axes of the slice: x: 4, y: 4, z: 4, core: 2. Of those that a mesh axis runs over, the one named last changes fastest.
Arguments:
- queries: bfloat16 [16384, 4096], P(('grp', 'seq')), may hold values from -6 to 6
- key_rows: bfloat16 [16384, 4096], P(('grp', 'seq')), may hold values from -6 to 6
- value_rows: bfloat16 [16384, 4096], P(('grp', 'seq')), may hold values from -6 to 6
- gate_logits: bfloat16 [16384, 4096], P(('grp', 'seq')), may hold values from -6 to 6
- residual_in: bfloat16 [16384, 4096], P(('grp', 'seq')), may hold values from -6 to 6
- decay_rate: float32 [16384, 32], P(('grp', 'seq')), may hold values from 0 to 1, as said below
- attention_gain: float32 [4096], replicated, may hold values from 0.25 to 1.75
- expert_gain: float32 [4096], replicated, may hold values from 0.25 to 1.75
- expert_index: int32 [16384, 2], P(('grp', 'seq')), may hold values from 0 to 15, all different within a row; in each aligned block of 128 rows (0 to 127, 128 to 255, ...) at most 16 rows name the same one
- router_weight: float32 [16384, 2], P(('grp', 'seq')), may hold values from 0.1 to 0.9
- gate_up_weight: bfloat16 [16, 4096, 2, 4608], P('seq', None, None, 'grp'), may hold values from -0.09375 to 0.09375
- down_weight: bfloat16 [16, 4608, 4096], P('seq', 'grp'), may hold values from -0.09375 to 0.09375
Outputs:
- layer_output: bfloat16 [16384, 4096], P(('grp', 'seq'))
Inputs may be any that keep to these rules, and one draw needn't show every extreme that they name: `expert_index`: each expert is named by exactly 16 of the 128 rows of one device; a row names 2 different experts. `decay_rate`: nonnegative rates.
All inputs are finite; a program needn't handle non-finite values.
Results may differ from a plain program's by a relative error of at most 0.02.
Values may be sent and summed in bfloat16 or wider, within the bound.
No kernel may reach another device: no remote copies, remote signals or barrier semaphores. Data moves between devices by JAX's collectives and lax.ppermute only.
A program may use at most 576 MiB of HBM per device.

v0:
```python
import jax
import jax.numpy as jnp
from jax import lax
from jax.sharding import PartitionSpec as P


def prefix(value, axis, join, neutral):
    count, mine = (lax.axis_size(axis), lax.axis_index(axis))
    pieces = jax.tree.map(lambda part: lax.all_gather(part, axis), value)
    so_far = jax.tree.map(
        lambda part, zero: jnp.full_like(part, 0) + jnp.asarray(zero, part.dtype), value, neutral
    )

    def prefix_lap(position, so_far):
        longer = join(so_far, jax.tree.map(lambda part: part[position], pieces))
        return jax.tree.map(lambda new, old: jnp.where(position < mine, new, old), longer, so_far)

    return lax.fori_loop(0, count - 1, prefix_lap, so_far)


def shortened(shard):
    return jax.tree.map(lambda a: a.astype(jnp.bfloat16) if a.dtype == jnp.float32 else a, shard)


def from_root(block, axis, owner):
    block = jnp.where(lax.axis_index(axis) == owner, block, jnp.zeros_like(block))
    return lax.psum(block, axis)


def carried_in(shard, axis, combine, identity):
    devices, here = (lax.axis_size(axis), lax.axis_index(axis))
    everything = jax.tree.map(
        lambda part, kind: lax.all_gather(part.astype(kind), axis),
        shard,
        jax.tree.map(lambda a: jnp.bfloat16 if a.dtype == jnp.float32 else a.dtype, shard),
    )
    start = jax.tree.map(
        lambda part, zero: jnp.broadcast_to(jnp.asarray(zero, part.dtype), part.shape),
        shard,
        identity,
    )

    def carried_lap(k, before):
        reached = k < here
        new = combine(
            before, jax.tree.map(lambda part, own: part[k].astype(own.dtype), everything, shard)
        )
        return jax.tree.map(lambda a, b: jnp.where(reached, a, b), new, before)

    return lax.fori_loop(0, devices, carried_lap, start)


def link_states(earlier, later):
    decay_early, state_early = earlier
    decay_late, state_late = later
    return (decay_early * decay_late, decay_late[:, None, None] * state_early + state_late)


def block_terms(query_heads, key_heads, value_heads, rates):
    token_count = rates.shape[0]
    running = jnp.cumsum(rates, axis=0)
    running_rows = running.T
    spacing = running_rows[:, :, None] - running_rows[:, None, :]
    positions = lax.iota(jnp.int32, token_count)
    causal = (positions[:, None] >= positions[None, :])[None]
    fading = jnp.where(causal, jnp.exp(-jnp.where(causal, spacing, 0.0)), 0.0)
    scores = jnp.einsum("thd,shd->hts", query_heads, key_heads, preferred_element_type=jnp.float32)
    weights = (scores * fading).astype(jnp.bfloat16)
    local_out = jnp.einsum("hts,shd->thd", weights, value_heads, preferred_element_type=jnp.float32)
    block_end = running[-1]
    key_faded = (
        key_heads.astype(jnp.float32) * jnp.exp(-(block_end[None, :] - running))[:, :, None]
    ).astype(jnp.bfloat16)
    local_state = jnp.einsum(
        "thd,the->hde", key_faded, value_heads, preferred_element_type=jnp.float32
    )
    return (local_out, local_state, jnp.exp(-block_end), running)


def body(
    queries,
    key_rows,
    value_rows,
    gate_logits,
    residual_in,
    decay_rate,
    attention_gain,
    expert_gain,
    expert_index,
    router_weight,
    gate_up_weight,
    down_weight,
):
    token_count, model_width = queries.shape
    head_count = decay_rate.shape[1]
    head_size = model_width // head_count
    query_heads = queries.reshape(token_count, head_count, head_size)
    key_heads = key_rows.reshape(token_count, head_count, head_size)
    value_heads = value_rows.reshape(token_count, head_count, head_size)
    local_out, local_state, block_keep, running = block_terms(
        query_heads, key_heads, value_heads, decay_rate
    )
    own_terms = (block_keep, local_state)
    identity = (jnp.ones_like(block_keep), jnp.zeros_like(local_state))
    within_group = prefix(own_terms, "seq", link_states, identity)
    through_self = link_states(within_group, own_terms)
    group_whole = (
        from_root(shortened(through_self[0]), "seq", lax.axis_size("seq") - 1),
        from_root(shortened(through_self[1]), "seq", lax.axis_size("seq") - 1),
    )
    before_group = carried_in(group_whole, "grp", link_states, identity)
    incoming = link_states(before_group, within_group)[1]
    carried_low = incoming.astype(jnp.bfloat16)
    carried_out = jnp.exp(-running)[:, :, None] * jnp.einsum(
        "thd,hde->the", query_heads, carried_low, preferred_element_type=jnp.float32
    )
    attention = (local_out + carried_out).reshape(token_count, model_width)
    inv_norm = lax.rsqrt(jnp.mean(attention * attention, axis=1, keepdims=True) + 1e-05)
    stream = (
        residual_in.astype(jnp.float32)
        + attention * inv_norm * attention_gain * jax.nn.sigmoid(gate_logits.astype(jnp.float32))
    ).astype(jnp.bfloat16)
    stream_wide = stream.astype(jnp.float32)
    inv_stream = lax.rsqrt(jnp.mean(stream_wide * stream_wide, axis=1, keepdims=True) + 1e-05)
    expert_input = (stream_wide * inv_stream * expert_gain).astype(jnp.bfloat16)
    choices_each = expert_index.shape[1]
    expert_count = lax.axis_size("seq")
    assigned = token_count * choices_each
    slot_count = assigned // expert_count
    flat_choice = expert_index.reshape(assigned)
    one_hot = (flat_choice[:, None] == lax.iota(jnp.int32, expert_count)[None, :]).astype(jnp.int32)
    before = jnp.cumsum(one_hot, axis=0) - one_hot
    slot_index = jnp.sum(before * one_hot, axis=1)
    position = (flat_choice * slot_count + slot_index).reshape(token_count, choices_each)
    targets = lax.iota(jnp.int32, assigned)
    chosen = position[None, :, :] == targets[:, None, None]
    selector = jnp.any(chosen, axis=2).astype(jnp.bfloat16)
    binned = jnp.dot(selector, expert_input, preferred_element_type=jnp.float32).astype(
        jnp.bfloat16
    )
    binned = binned.reshape(expert_count, slot_count, model_width)
    received = lax.all_to_all(binned, "seq", split_axis=0, concat_axis=0, tiled=True)
    arrived = received.reshape(expert_count * slot_count, model_width)
    hidden_width = down_weight.shape[1]
    gate_up = gate_up_weight[0].reshape(model_width, 2 * hidden_width)
    down_local = down_weight[0]
    block_rows = lax.all_gather(arrived, "grp", axis=0, tiled=True)
    pair = jnp.dot(block_rows, gate_up, preferred_element_type=jnp.float32).reshape(
        block_rows.shape[0], 2, hidden_width
    )
    hidden = (jax.nn.silu(pair[:, 0]) * pair[:, 1]).astype(jnp.bfloat16)
    block_rows = hidden
    summed = lax.psum_scatter(
        jnp.dot(block_rows, down_local, preferred_element_type=jnp.float32).astype(jnp.bfloat16),
        "grp",
        scatter_dimension=0,
        tiled=True,
    )
    returned = lax.all_to_all(
        summed.reshape(expert_count, slot_count, model_width),
        "seq",
        split_axis=0,
        concat_axis=0,
        tiled=True,
    )
    flat_returned = returned.reshape(assigned, model_width)
    picked = flat_returned[position]
    expert_mix = jnp.sum(router_weight[:, :, None] * picked.astype(jnp.float32), axis=1)
    return (stream_wide + expert_mix).astype(jnp.bfloat16)


def solution(mesh):
    return jax.shard_map(
        body,
        mesh=mesh,
        in_specs=(
            P(("grp", "seq"), None),
            P(("grp", "seq"), None),
            P(("grp", "seq"), None),
            P(("grp", "seq"), None),
            P(("grp", "seq"), None),
            P(("grp", "seq"), None),
            P(),
            P(),
            P(("grp", "seq"), None),
            P(("grp", "seq"), None),
            P("seq", None, None, "grp"),
            P("seq", "grp", None),
        ),
        out_specs=P(("grp", "seq"), None),
        check_vma=False,
    )
```

profile of v0, /device:TPU:0, one launch (start us, length us, event | category | flops | bytes accessed | tf_op | source)
XLA Modules:
  0.0 733.7 jit_solution(1627167585009449755)
XLA Ops:
  7.8 1.6 copy.103
  9.4 1.8 fusion.15
  11.3 22.2 %all-gather.1 = f32[16,1,32]{2,1,0:T(1,128)S(1)} all-gather(f32[1,1,32]{2,1,0:T(1,128)S(1)} %get-tuple-element.282), channel_id=1, replica_groups=mesh['grp'=8,'seq'=16] {'seq'}, dimensions={0}, use_global_device_ids=true | all-gather | bytes 2176 | tf_op jit(solution)/shard_map/all_gather | solution.py:9
  33.5 177.6 %all-gather.11.cloned.1.call-done = f32[512,128,128]{2,1,0:T(8,128)} async-done(((f32[32,128,128]{2,1,0:T(8,128)}), f32[512,128,128]{2,1,0:T(8,128)}) %all-gather.11.cloned.1.call-update) | async-done | bytes 33554448 | tf_op jit(solution)/shard_map/all_gather | solution.py:9
  211.1 32.1 %while.30 = (s32[]{:T(128)}, f32[32]{0:T(128)S(1)}, f32[32,128,128]{2,1,0:T(8,128)S(1)}, s32[]{:T(128)}, f32[16,32]{1,0:T(8,128)S(1)}, /*index=5*/f32[16,32,128,128]{3,2,1,0:T(8,128)}, s32[]{:T(128)}, s32[]{:T(128)}) while((s32[]{:T(128)}, f32[32]{0:T(128)S(1)}, f32[32,128,128]{2,1,0:T(8,128)S(1)}, s32[]{:T(128)}, ...), condition=%wide.region_2.3_spmd.clone, body=%wide.region_1.2_spmd.clone.sunk | while | flops 2097252 | bytes 6292211 | solution.py:18
  211.1 2.1 fusion.53
  213.2 2.1 fusion.53
  215.3 2.1 fusion.53
  217.5 2.1 fusion.53
  219.6 2.1 fusion.53
  221.8 2.1 fusion.53
  223.9 2.1 fusion.53
  226.1 2.1 fusion.53
  228.2 2.1 fusion.53
  230.3 2.1 fusion.53
  232.5 2.1 fusion.53
  234.6 2.1 fusion.53
  236.8 2.1 fusion.53
  238.9 2.1 fusion.53
  241.1 2.1 fusion.53
  243.2 2.9 fusion.17
  246.2 86.9 %all-reduce.2.cloned.1.call-done = bf16[1,32,128,128]{3,2,1,0:T(8,128)(2,1)} async-done(((bf16[1,32,128,128]{3,2,1,0:T(8,128)(2,1)}), bf16[1,32,128,128]{3,2,1,0:T(8,128)(2,1)}) %all-reduce.2.cloned.1.call-update) | async-done | bytes 1048592 | tf_op jit(solution)/shard_map/psum | solution.py:27
  334.8 4.1 fusion.14
  339.0 38.1 %psum.14 = bf16[1,32]{1,0:T(2,128)(2,1)S(1)} all-reduce(bf16[1,32]{1,0:T(2,128)(2,1)S(1)} %fusion.42), channel_id=1, replica_groups=mesh['grp'=8,'seq'=16] {'seq'}, use_global_device_ids=true, to_apply=%region_3.4 | all-reduce | flops 32 | bytes 128 | tf_op jit(solution)/shard_map/psum | solution.py:27
  377.2 10.5 %all-gather.2 = bf16[8,1,32]{2,1,0:T(2,128)(2,1)S(1)} all-gather(bf16[1,1,32]{2,1,0:T(2,128)(2,1)S(1)} %bitcast.126), channel_id=1, replica_groups=mesh['grp'=8,'seq'=16] {'grp'}, dimensions={0}, use_global_device_ids=true | all-gather | bytes 576 | tf_op jit(solution)/shard_map/all_gather | solution.py:33
  387.6 21.5 %while.31 = (s32[]{:T(128)}, bf16[32,128,128]{2,1,0:T(8,128)(2,1)}, s32[]{:T(128)}, bf16[8,32]{1,0:T(8,128)(2,1)S(1)}, bf16[8,32,128,128]{3,2,1,0:T(8,128)(2,1)}, /*index=5*/s32[]{:T(128)}, s32[]{:T(128)}) while((s32[]{:T(128)}, bf16[32,128,128]{2,1,0:T(8,128)(2,1)}, s32[]{:T(128)}, bf16[8,32]{1,0:T(8,128)(2,1)S(1)}, ...), condition=%wide.region_6.7_spmd.clone, body=%wide.region_5.6_spmd.clone.sunk | while | flops 2097156 | bytes 3146025 | solution.py:50
  387.6 2.4 fusion.54
  390.1 2.7 fusion.54
  392.8 2.7 fusion.54
  395.5 2.7 fusion.54
  398.2 2.7 fusion.54
  400.9 2.7 fusion.54
  403.7 2.7 fusion.54
  406.4 2.7 fusion.54
  409.1 4.2 multiply_reduce_fusion.1
  413.3 1.9 copy.94
  415.3 2.6 fusion.9
  418.7 32.4 %all_to_all.10 = bf16[16,16,4096]{2,1,0:T(8,128)(2,1)} all-to-all(bf16[16,16,4096]{2,1,0:T(8,128)(2,1)S(1)} %bitcast.118), channel_id=1, replica_groups=mesh['grp'=8,'seq'=16] {'seq'}, dimensions={0} | all-to-all | bytes 4194304 | tf_op jit(solution)/shard_map/all_to_all | solution.py:142
  451.4 80.7 %all-gather.9.cloned.1.call-done = bf16[2048,4096]{1,0:T(8,128)(2,1)} async-done(((bf16[256,4096]{1,0:T(8,128)(2,1)}), bf16[2048,4096]{1,0:T(8,128)(2,1)}) %all-gather.9.cloned.1.call-update) | async-done | bytes 16777232 | tf_op jit(solution)/shard_map/all_gather | solution.py:147
  532.1 26.9 %fusion.2 = f32[2048,2,576]{0,2,1:T(8,128)} fusion(bf16[2048,4096]{1,0:T(8,128)(2,1)} %all-gather.9.cloned.1.call-done, bf16[1,4096,2,576]{1,3,2,0:T(8,128)(2,1)} %param.26), kind=kOutput, calls=%fused_computation.9 | convolution fusion | flops 19327352832 | bytes 35651584 | tf_op jit(solution)/shard_map/dot_general | solution.py:148
  559.0 20.6 %convolution_convert_fusion = bf16[2048,4096]{1,0:T(8,128)(2,1)} fusion(bf16[1,576,4096]{2,1,0:T(8,128)(2,1)} %param.27, f32[2048,2,576]{0,2,1:T(8,128)} %fusion.2), kind=kOutput, calls=%fused_computation.11 | convolution fusion | flops 9679142912 | bytes 30932992 | tf_op jit(solution)/shard_map/dot_general | solution.py:154
  579.6 92.5 %reduce-scatter.2.cloned.1.call-done = bf16[256,4096]{1,0:T(8,128)(2,1)} async-done(((bf16[2048,4096]{1,0:T(8,128)(2,1)}), bf16[256,4096]{1,0:T(8,128)(2,1)}) %reduce-scatter.2.cloned.1.call-update) | async-done | bytes 2097168 | tf_op jit(solution)/shard_map/reduce_scatter | solution.py:153
  672.1 7.1 all-to-all-start.1
  679.6 28.9 %all-to-all-done.1 = bf16[16,16,4096]{2,1,0:T(8,128)(2,1)S(1)} async-done(((bf16[16,16,4096]{2,1,0:T(8,128)(2,1)}), bf16[16,16,4096]{2,1,0:T(8,128)(2,1)S(1)}, u32[]{:S(2)}, u32[]{:S(2)}) %all-to-all-start.1) | async-done | bytes 2097184 | tf_op jit(solution)/shard_map/all_to_all | solution.py:159
  708.5 3.2 gather_fusion
  711.7 5.4 reshape.137
  717.1 8.8 %multiply_reduce_fusion = f32[128,4096]{1,0:T(8,128)S(1)} fusion(f32[128,2,4096]{2,1,0:T(2,128)} %reshape.137, f32[128,2]{1,0:T(8,128)S(1)} %copy.95), kind=kLoop, calls=%fused_computation.17 | loop fusion | flops 1572864 | bytes 6292480 | tf_op jit(solution)/shard_map/reduce_sum | solution.py:168
  725.9 1.2 fusion.12
  (84 shorter events, 4.9 us)
Async XLA Ops:
  6.5 328.3 %copy-start = (bf16[128,4096]{1,0:T(8,128)(2,1)S(1)}, bf16[128,4096]{1,0:T(8,128)(2,1)}, u32[]{:S(2)}) copy-start(bf16[128,4096]{1,0:T(8,128)(2,1)} %param.16) | copy-start | bytes 3145732
  6.5 2.9 copy-start.3
  6.5 204.5 %all-gather.11.cloned.1.call-start = ((), (), s32[]{:S(2)}) async-start(), calls=%async_computation.7 | async-start | bytes 35651584 | tf_op jit(solution)/shard_map/all_gather | solution.py:9
  9.4 1.8 copy-start.2
  11.2 321.8 %all-reduce.2.cloned.1.call-start = ((), (), s32[]{:S(2)}) async-start(), calls=%async_computation.3 | async-start | bytes 2097152 | tf_op jit(solution)/shard_map/psum | solution.py:27
  246.1 87.0 %copy-start.6 = (s32[128,2]{0,1:T(2,128)S(1)}, s32[128,2]{0,1:T(2,128)}, u32[]{:S(2)}) copy-start(s32[128,2]{0,1:T(2,128)} %param.24) | copy-start | bytes 3076
  246.1 141.5 %all-gather.7.cloned.1.call-start = ((), (), s32[]{:S(2)}) async-start(), calls=%async_computation.4 | async-start | bytes 9437184 | tf_op jit(solution)/shard_map/all_gather | solution.py:33
  333.1 199.0 %all-gather.9.cloned.1.call-start = ((), (), s32[]{:S(2)}) async-start(), calls=%async_computation.5 | async-start | bytes 18874368 | tf_op jit(solution)/shard_map/all_gather | solution.py:147
  413.3 2.0 copy-start.4
  415.3 2.6 copy-start.5
  451.1 221.0 %reduce-scatter.2.cloned.1.call-start = ((), (), s32[]{:S(2)}) async-start(), calls=%async_computation.6 | async-start | bytes 18874368 | tf_op jit(solution)/shard_map/reduce_scatter | solution.py:153
  672.1 7.4 %copy-start.7 = (f32[128,2]{0,1:T(2,128)S(1)}, f32[128,2]{0,1:T(2,128)}, u32[]{:S(2)}) copy-start(f32[128,2]{0,1:T(2,128)} %param.25) | copy-start | bytes 3076
  672.1 36.4 %all-to-all-start.1 = ((bf16[16,16,4096]{2,1,0:T(8,128)(2,1)}), bf16[16,16,4096]{2,1,0:T(8,128)(2,1)S(1)}, u32[]{:S(2)}, u32[]{:S(2)}) async-start(bf16[16,16,4096]{2,1,0:T(8,128)(2,1)} %bitcast.122), calls=%async_computation.2 | async-start | bytes 4194304 | tf_op jit(solution)/shard_map/all_to_all | solution.py:159
  717.1 10.1 %copy-start.1 = (bf16[128,4096]{1,0:T(8,128)(2,1)S(1)}, bf16[128,4096]{1,0:T(8,128)(2,1)}, u32[]{:S(2)}) copy-start(bf16[128,4096]{1,0:T(8,128)(2,1)} %param.16) | copy-start | bytes 3145732
Sparse Core Ops, SparseCore 0:
  11.3 199.6 all-gather.10
  246.2 86.7 all-reduce.1
  334.8 48.7 all-gather.6
  451.3 80.7 all-gather.8
  579.7 92.3 reduce-scatter.1
where the time goes:
time: 735 us; the launch traced here: 734 us
  waiting for transfers between devices  467 us (64%)
  blocking collectives  103 us (14%)
  other arithmetic  69.7 us (9%)
  matrix products  58.3 us (8%)
  local copies, waits for them, and re-layouts  14.6 us (2%)
  between operations  13.4 us (2%)
  starting transfers between devices  7.44 us (1%)
    all_gather x1, waiting for transfers between devices, prefix(): pieces = jax.tree.map(lambda part: lax.all_gather(part, axis), value)  178 us
    reduce_scatter x1, waiting for transfers between devices, body(): lax.psum_scatter(jnp.dot(block_rows, down_local, preferred_element_type=j...  92.5 us
    psum x1, waiting for transfers between devices, from_root(): return lax.psum(block, axis)  86.9 us
    all_gather x1, waiting for transfers between devices, body(): block_rows = lax.all_gather(arrived, 'grp', axis=0, tiled=True)  80.7 us
    psum x1, blocking collectives, from_root(): return lax.psum(block, axis)  38.1 us
    all_to_all x1, blocking collectives, body(): lax.all_to_all(binned, 'seq', split_axis=0, concat_axis=0, tiled=True)  32.4 us
    select_n x30, other arithmetic, prefix_lap(): jnp.where(position < mine, new, old)  31.7 us
    all_to_all x1, waiting for transfers between devices, body(): lax.all_to_all(summed.reshape(expert_count, slot_count, model_width), 'se...  28.9 us
  transfers between devices with their start and end apart: 6, of which 5 were waited for; matrix products, arithmetic and copies ran while one was open for 1% of the time, Pallas kernels for 0%

commit v1 on v0

v1 whole, which is shorter than its diff:
```python
import functools

import jax
import jax.numpy as jnp
from jax import lax
from jax.experimental import pallas as pl
from jax.experimental.pallas import tpu as pltpu
from jax.sharding import PartitionSpec as P

F32, BF16 = (jnp.float32, jnp.bfloat16)
HEAD = 128
PIECE = 32
EXTRA = 16
MIB = 1 << 20
NT = (((1,), (1,)), ((), ()))
TN = (((0,), (0,)), ((), ()))


def vmem(count):
    return [pl.BlockSpec(memory_space=pltpu.VMEM)] * count


def whole_call(kernel, outs, args, flops, limit, scratch=()):
    moved = sum(a.size * a.dtype.itemsize for a in (*args, *outs))
    return pl.pallas_call(
        kernel,
        out_shape=outs,
        in_specs=vmem(len(args)),
        out_specs=vmem(len(outs)),
        scratch_shapes=list(scratch),
        cost_estimate=pl.CostEstimate(flops=flops, bytes_accessed=moved, transcendentals=0),
        compiler_params=pltpu.CompilerParams(vmem_limit_bytes=limit * MIB),
    )(*args)


def lane_block(h):
    return slice(h * HEAD, (h + 1) * HEAD)


def state_kernel(rates_ref, key_ref, value_ref, sent_ref, by_head_ref, by_token_ref):
    heads, tokens = rates_ref.shape
    at = lambda dim: lax.broadcasted_iota(jnp.int32, (tokens, tokens), dim)
    upto = (at(0) <= at(1)).astype(F32)
    by_head = jnp.dot(
        rates_ref[...], upto, precision=lax.Precision.HIGHEST, preferred_element_type=F32
    )
    by_token = by_head.T
    by_head_ref[...] = by_head
    by_token_ref[...] = by_token
    fade = jnp.exp(by_token - by_token[tokens - 1 :, :])
    keep = jnp.broadcast_to(jnp.exp(-by_head[:, tokens - 1 :]), (heads, HEAD))
    high = keep.astype(BF16).astype(F32)
    middle = (keep - high).astype(BF16).astype(F32)
    low = keep - high - middle
    row = lax.broadcasted_iota(jnp.int32, (EXTRA, HEAD), 0)
    parts = HEAD // PIECE
    for h in range(heads):
        faded = (key_ref[:, lane_block(h)].astype(F32) * fade[:, h : h + 1]).astype(BF16)
        state = lax.dot_general(faded, value_ref[:, lane_block(h)], TN, preferred_element_type=F32)
        tail = jnp.where(row == 0, high[h : h + 1], 0.0)
        tail = jnp.where(row == 1, middle[h : h + 1], tail)
        tail = jnp.where(row == 2, low[h : h + 1], tail).astype(BF16)
        for part in range(parts):
            sent_ref[h * parts + part, :PIECE, :] = state[
                part * PIECE : (part + 1) * PIECE
            ].astype(BF16)
            sent_ref[h * parts + part, PIECE:, :] = tail


def scan_kernel(arrived_ref, carried_ref):
    def step(block, carry):
        carried_ref[block] = carry.astype(BF16)
        tail = arrived_ref[block, PIECE:, :].astype(F32)
        keep = tail[0:1] + tail[1:2] + tail[2:3]
        return keep * carry + arrived_ref[block, :PIECE, :].astype(F32)

    lax.fori_loop(
        0, carried_ref.shape[0], step, jnp.zeros((PIECE, HEAD), F32), unroll=8
    )


def local_kernel(query_ref, key_ref, value_ref, by_head_ref, by_token_ref, out_ref):
    heads, tokens = by_head_ref.shape
    at = lambda dim: lax.broadcasted_iota(jnp.int32, (tokens, tokens), dim)
    causal = at(0) >= at(1)
    for h in range(heads):
        scores = lax.dot_general(
            query_ref[:, lane_block(h)], key_ref[:, lane_block(h)], NT, preferred_element_type=F32
        )
        spacing = by_head_ref[h : h + 1, :] - by_token_ref[:, h : h + 1]
        fading = jnp.exp(jnp.minimum(spacing, 0.0))
        weights = jnp.where(causal, scores * fading, 0.0).astype(BF16)
        out_ref[:, lane_block(h)] = jnp.dot(
            weights, value_ref[:, lane_block(h)], preferred_element_type=F32
        )


def places(index_ref, experts):
    tokens = index_ref.shape[1]
    expert = lax.broadcasted_iota(jnp.int32, (experts, tokens), 0)
    first, second = (index_ref[0:1, :] == expert, index_ref[1:2, :] == expert)
    named = (first | second).astype(F32)
    at = lambda dim: lax.broadcasted_iota(jnp.int32, (tokens, tokens), dim)
    earlier = (at(0) < at(1)).astype(BF16)
    slot = jnp.dot(named.astype(BF16), earlier, preferred_element_type=F32)
    return first, second, jnp.where(named > 0.0, slot, -1.0)


def chunk_rows(slot, chunk, rows):
    experts, tokens = slot.shape
    wanted = lax.broadcasted_iota(jnp.int32, (rows, tokens), 0).astype(F32) + float(chunk * rows)
    return [slot[e : e + 1, :] == wanted for e in range(experts)]


def stream_kernel(
    query_ref,
    carried_ref,
    by_token_ref,
    local_ref,
    gate_ref,
    residual_ref,
    attention_gain_ref,
    expert_gain_ref,
    index_ref,
    stream_ref,
    *rest,
):
    *bin_refs, attention_ref = rest
    tokens, width = query_ref.shape
    heads = width // HEAD
    since = jnp.exp(-by_token_ref[...])
    total = jnp.zeros((tokens, HEAD), F32)
    for h in range(heads):
        carried_out = jnp.dot(
            query_ref[:, lane_block(h)], carried_ref[h], preferred_element_type=F32
        )
        attention = local_ref[:, lane_block(h)] + since[:, h : h + 1] * carried_out
        attention_ref[:, lane_block(h)] = attention
        total = total + attention * attention
    inverse = lax.rsqrt(jnp.sum(total, axis=1, keepdims=True) / width + 1e-05)
    total = jnp.zeros((tokens, HEAD), F32)
    for h in range(heads):
        gate = gate_ref[:, lane_block(h)].astype(F32)
        sigmoid = 1.0 / (1.0 + jnp.exp(-gate))
        gained = attention_ref[:, lane_block(h)] * inverse * attention_gain_ref[:, lane_block(h)]
        stream = (residual_ref[:, lane_block(h)].astype(F32) + gained * sigmoid).astype(BF16)
        stream_ref[:, lane_block(h)] = stream
        wide = stream.astype(F32)
        total = total + wide * wide
    inverse = lax.rsqrt(jnp.sum(total, axis=1, keepdims=True) / width + 1e-05)
    experts = bin_refs[0].shape[0]
    rows = bin_refs[0].shape[1]
    slot = places(index_ref, experts)[2]
    selectors = [
        jnp.concatenate([m.astype(F32) for m in chunk_rows(slot, c, rows)], axis=0).astype(BF16)
        for c in range(len(bin_refs))
    ]
    for h in range(heads):
        wide = stream_ref[:, lane_block(h)].astype(F32)
        entry = (wide * inverse * expert_gain_ref[:, lane_block(h)]).astype(BF16)
        for selector, bin_ref in zip(selectors, bin_refs):
            picked = jnp.dot(selector, entry, preferred_element_type=F32)
            bin_ref[:, :, lane_block(h)] = picked.astype(BF16).reshape(experts, rows, HEAD)


def mix_kernel(stream_ref, index_ref, router_ref, *rest):
    *returned_refs, out_ref = rest
    experts, rows, width = returned_refs[0].shape
    first, second, slot = places(index_ref, experts)
    scale = jnp.where(first, router_ref[0:1, :], 0.0) + jnp.where(second, router_ref[1:2, :], 0.0)
    weights = []
    for c in range(len(returned_refs)):
        masks = chunk_rows(slot, c, rows)
        chosen = jnp.concatenate(
            [jnp.where(m, scale[e : e + 1, :], 0.0) for e, m in enumerate(masks)], axis=0
        ).T
        high = chosen.astype(BF16)
        weights.append((high, (chosen - high.astype(F32)).astype(BF16)))
    for h in range(width // HEAD // 4):
        columns = slice(h * 4 * HEAD, (h + 1) * 4 * HEAD)
        total = stream_ref[:, columns].astype(F32)
        for (high, low), returned_ref in zip(weights, returned_refs):
            returned = returned_ref[:, :, columns].reshape(experts * rows, 4 * HEAD)
            total = total + jnp.dot(high, returned, preferred_element_type=F32)
            total = total + jnp.dot(low, returned, preferred_element_type=F32)
        out_ref[:, columns] = total.astype(BF16)


def expert_kernel(
    steps_in,
    steps_out,
    own_ref,
    left_ref,
    right_ref,
    far_a_ref,
    far_b_ref,
    up_own_ref,
    up_other_ref,
    down_own_ref,
    down_other_ref,
    out_own_ref,
    out_left_ref,
    out_right_ref,
    out_far_ref,
    rows_ref,
    turned_ref,
    hidden_own_ref,
    hidden_other_ref,
):
    step = pl.program_id(0)
    half = steps_in // 2
    count = own_ref.shape[0]

    @pl.when(step == 0)
    def _():
        rows_ref[0:count] = own_ref[...]
        rows_ref[count : 2 * count] = left_ref[...]
        rows_ref[2 * count : 3 * count] = right_ref[...]
        rows_ref[3 * count : 3 * count + count // 2] = far_a_ref[...]
        rows_ref[3 * count + count // 2 :] = far_b_ref[...]

    def enter(weight_ref):
        tile = weight_ref.shape[1]
        gate = lax.dot_general(weight_ref[0], rows_ref[...], NT, preferred_element_type=F32)
        up = lax.dot_general(weight_ref[1], rows_ref[...], NT, preferred_element_type=F32)
        hidden = gate / (1.0 + jnp.exp(-gate)) * up
        turned_ref[pl.ds(pl.multiple_of(step * tile, tile), tile), :] = hidden.astype(BF16)

    @pl.when(step < half)
    def _():
        enter(up_own_ref)

    @pl.when((step >= half) & (step < steps_in))
    def _():
        enter(up_other_ref)

    @pl.when(step == steps_in)
    def _():
        units = hidden_own_ref.shape[1]
        hidden_own_ref[...] = turned_ref[:units, :].T
        hidden_other_ref[...] = turned_ref[units:, :].T

    @pl.when(step >= steps_in)
    def _():
        out = jnp.dot(hidden_own_ref[...], down_own_ref[...], preferred_element_type=F32)
        out = out + jnp.dot(hidden_other_ref[...], down_other_ref[...], preferred_element_type=F32)
        out = out.astype(BF16)
        for place, ref in enumerate((out_own_ref, out_left_ref, out_right_ref, out_far_ref)):
            ref[...] = out[place * count : (place + 1) * count]


def expert_rows(blocks, up_own, up_other, down_own, down_other):
    count, width = blocks[0].shape
    units = down_own.shape[0]
    steps_in, steps_out = (4, 4)
    tile, columns = (2 * units // steps_in, width // steps_out)
    half = steps_in // 2
    once = pl.Buffered(1)
    fixed = lambda a: pl.BlockSpec(a.shape, lambda i: (0, 0), pipeline_mode=once)
    clip = lambda i, low, high: jnp.minimum(jnp.maximum(i, low), high)
    up_spec = lambda start: pl.BlockSpec(
        (2, tile, width), lambda i: (0, clip(i - start, 0, half - 1), 0)
    )
    down_spec = pl.BlockSpec((units, columns), lambda i: (0, clip(i - steps_in, 0, steps_out - 1)))
    out_spec = pl.BlockSpec((count, columns), lambda i: (0, clip(i - steps_in, 0, steps_out - 1)))
    return pl.pallas_call(
        functools.partial(expert_kernel, steps_in, steps_out),
        grid=(steps_in + steps_out,),
        in_specs=[fixed(b) for b in blocks]
        + [up_spec(0), up_spec(half), down_spec, down_spec],
        out_specs=[out_spec] * 4,
        out_shape=[jax.ShapeDtypeStruct((count, width), BF16)] * 4,
        scratch_shapes=[
            pltpu.VMEM((4 * count, width), BF16),
            pltpu.VMEM((2 * units, 4 * count), BF16),
            pltpu.VMEM((4 * count, units), BF16),
            pltpu.VMEM((4 * count, units), BF16),
        ],
        cost_estimate=pl.CostEstimate(
            flops=4 * count * 2 * units * width * 6,
            bytes_accessed=6 * units * width * 2 + 8 * count * width * 2,
            transcendentals=0,
        ),
        compiler_params=pltpu.CompilerParams(vmem_limit_bytes=44 * MIB),
    )(*blocks, up_own, up_other, down_own, down_other)


def body(
    queries,
    key_rows,
    value_rows,
    gate_logits,
    residual_in,
    decay_rate,
    attention_gain,
    expert_gain,
    expert_index,
    router_weight,
    gate_up_weight,
    down_weight,
):
    groups, experts = (lax.axis_size("grp"), lax.axis_size("seq"))
    devices = groups * experts
    tokens, width = queries.shape
    heads = decay_rate.shape[1]
    chunks = 2
    slots = tokens * expert_index.shape[1] // experts
    rows = slots // chunks
    count = experts * rows

    swap = [(g, g ^ 1) for g in range(groups)]
    ahead = [(g, (g + 2) % groups) for g in range(groups)]
    back = [(g, (g - 2) % groups) for g in range(groups)]
    go_ahead = lambda a: lax.ppermute(a, "grp", ahead)
    go_back = lambda a: lax.ppermute(a, "grp", back)
    everywhere = ("grp", "seq")
    exchange = lambda a, axis: lax.all_to_all(a, axis, split_axis=0, concat_axis=0, tiled=True)
    shape = jax.ShapeDtypeStruct

    up_own = jnp.transpose(gate_up_weight[0], (1, 2, 0))
    down_own = down_weight[0]
    up_other = lax.ppermute(up_own, "grp", swap)
    down_other = lax.ppermute(down_own, "grp", swap)

    sent, by_head, by_token = whole_call(
        state_kernel,
        [
            shape((devices, PIECE + EXTRA, HEAD), BF16),
            shape((heads, tokens), F32),
            shape((tokens, heads), F32),
        ],
        [decay_rate.T, key_rows, value_rows],
        2 * tokens * width * HEAD,
        16,
    )
    arrived = exchange(sent, everywhere)
    (local_out,) = whole_call(
        local_kernel,
        [shape((tokens, width), F32)],
        [queries, key_rows, value_rows, by_head, by_token],
        4 * tokens * width * tokens,
        16,
    )
    (carried,) = whole_call(
        scan_kernel, [shape((devices, PIECE, HEAD), BF16)], [arrived], devices * PIECE * HEAD, 16
    )
    carried_low = exchange(carried, everywhere).reshape(heads, HEAD, HEAD)
    index = expert_index.T
    stream, *bins = whole_call(
        stream_kernel,
        [shape((tokens, width), BF16)] + [shape((experts, rows, width), BF16)] * chunks,
        [
            queries,
            carried_low,
            by_token,
            local_out,
            gate_logits,
            residual_in,
            attention_gain[None, :],
            expert_gain[None, :],
            index,
        ],
        2 * tokens * width * (HEAD + chunks * count),
        32,
        [pltpu.VMEM((tokens, width), F32)],
    )

    half = count // 2
    returned = []
    for bin_rows in bins:
        own = exchange(bin_rows, "seq").reshape(count, width)
        left, right = (go_ahead(own), go_back(own))
        far_a, far_b = (go_ahead(left[:half]), go_back(right[half:]))
        out_own, out_left, out_right, out_far = expert_rows(
            (own, left, right, far_a, far_b), up_own, up_other, down_own, down_other
        )
        pass_a, pass_b = (go_ahead(out_far[:half]), go_back(out_far[half:]))
        right_low, left_high = (go_ahead(out_right[half:]), go_back(out_left[:half]))
        wide = lambda a: a.astype(F32)
        right_high = go_ahead((wide(out_right[:half]) + wide(pass_a)).astype(BF16))
        left_low = go_back((wide(out_left[half:]) + wide(pass_b)).astype(BF16))
        summed = jnp.concatenate(
            [
                wide(out_own[:half]) + wide(right_high) + wide(left_high),
                wide(out_own[half:]) + wide(right_low) + wide(left_low),
            ],
            axis=0,
        ).astype(BF16)
        returned.append(exchange(summed.reshape(experts, rows, width), "seq"))
    (out,) = whole_call(
        mix_kernel,
        [shape((tokens, width), BF16)],
        [stream, index, router_weight.T, *returned],
        4 * tokens * width * count * chunks,
        16,
    )
    return out


def solution(mesh):
    rows = P(("grp", "seq"), None)
    return jax.shard_map(
        body,
        mesh=mesh,
        in_specs=(
            rows,
            rows,
            rows,
            rows,
            rows,
            rows,
            P(),
            P(),
            rows,
            rows,
            P("seq", None, None, "grp"),
            P("seq", "grp", None),
        ),
        out_specs=rows,
        check_vma=False,
    )
```

time: 735 us -> 297 us (0.40)
  waiting for transfers between devices: 467 us -> 119 us
  blocking collectives: 103 us -> 35.7 us
  Pallas kernels: 0 us -> 65.4 us
  other arithmetic: 69.7 us -> 5.71 us
  matrix products: 58.3 us -> 0 us
  starting transfers between devices: 7.44 us -> 56.2 us
  between operations: 13.4 us -> 0.29 us
    all_gather x3 -> x0, waiting for transfers between devices: 258 us -> none  [the longest x1 178 us: prefix(): pieces = jax.tree.map(lambda part: lax.all_gather(part, axis), value)]
    reduce_scatter x1 -> x0, waiting for transfers between devices: 92.5 us -> none  [body(): lax.psum_scatter(jnp.dot(block_rows, down_local, preferred_element_type=j...]
    psum x1 -> x0, waiting for transfers between devices: 86.9 us -> none  [from_root(): return lax.psum(block, axis)]
    pallas_call x0 -> x7, Pallas kernels: none -> 65.4 us  [the longest x2 48.3 us: expert_rows(): pl.pallas_call(functools.partial(expert_kernel, steps_in, steps_out), gri...]
    ppermute x0 -> x22, waiting for transfers between devices: none -> 61.1 us  [the longest x10 43.6 us: body(): go_ahead = lambda a: lax.ppermute(a, 'grp', ahead)]
    dot_general x6 -> x0, matrix products: 58.3 us -> none  [the longest x1 26.9 us: body(): jnp.dot(block_rows, gate_up, preferred_element_type=jnp.float32)]
    select_n x39 -> x0, other arithmetic: 53.1 us -> none  [the longest x30 31.7 us: prefix_lap(): jnp.where(position < mine, new, old)]
    psum x1 -> x0, blocking collectives: 38.1 us -> none  [from_root(): return lax.psum(block, axis)]
  transfers between devices with their start and end apart: 6 -> 26, of which waited for: 5 -> 13; matrix products, arithmetic and copies ran while one was open for 1% -> 3% of each run, Pallas kernels for 0% -> 21%
where the time goes in v1:
time: 297 us; the launch traced here: 296 us
  waiting for transfers between devices  119 us (40%)
  Pallas kernels  65.4 us (22%)
  starting transfers between devices  56.2 us (19%)
  blocking collectives  35.7 us (12%)
  local copies, waits for them, and re-layouts  13.5 us (5%)
  other arithmetic  5.71 us (2%)
    all_to_all x4, waiting for transfers between devices, body(): lax.all_to_all(a, axis, split_axis=0, concat_axis=0, tiled=True)  58.2 us
    pallas_call x2, Pallas kernels, expert_rows(): pl.pallas_call(functools.partial(expert_kernel, steps_in, steps_out), gri...  48.3 us
    ppermute x10, waiting for transfers between devices, body(): go_ahead = lambda a: lax.ppermute(a, 'grp', ahead)  43.6 us
    all_to_all x2, blocking collectives, body(): lax.all_to_all(a, axis, split_axis=0, concat_axis=0, tiled=True)  35.7 us
    all_to_all x4, starting transfers between devices, body(): lax.all_to_all(a, axis, split_axis=0, concat_axis=0, tiled=True)  27.4 us
    ppermute x10, starting transfers between devices, body(): go_back = lambda a: lax.ppermute(a, 'grp', back)  22.7 us
    ppermute x10, waiting for transfers between devices, body(): go_back = lambda a: lax.ppermute(a, 'grp', back)  17.5 us
    pallas_call x5, Pallas kernels, whole_call(): pl.pallas_call(kernel, out_shape=outs, in_specs=vmem(len(args)), out_spec...  17.1 us
  transfers between devices with their start and end apart: 26, of which 13 were waited for; matrix products, arithmetic and copies ran while one was open for 3% of the time, Pallas kernels for 21%

profile of v1, /device:TPU:0, one launch (start us, length us, event | category | flops | bytes accessed | tf_op | source)
XLA Modules:
  0.0 296.1 jit_solution(16245336186218712214)
XLA Ops:
  0.0 1.2 copy-done
  1.2 1.2 copy-done.2
  3.2 3.3 %shard_map.118 = (bf16[128,48,128]{2,1,0:T(8,128)(2,1)}, f32[32,128]{1,0:T(8,128)S(1)}, f32[128,32]{1,0:T(8,128)S(1)}) custom-call(f32[32,128]{1,0:T(8,128)S(1)} %bitcast.22, bf16[128,4096]{1,0:T(8,128)(2,1)S(1)} %copy-done, bf16[128,4096]{1,0:T(8,128)(2,1)S(1)} %copy-done.2), custom_call_target="tpu_custom_call" | custom-call | flops 134217728 | bytes 3719168 | tf_op jit(solution)/shard_map/pallas_call | solution.py:25
  6.5 11.3 %all-to-all-start = ((bf16[128,48,128]{2,1,0:T(8,128)(2,1)}), bf16[128,48,128]{2,1,0:T(8,128)(2,1)S(1)}, u32[]{:S(2)}, u32[]{:S(2)}) async-start(bf16[128,48,128]{2,1,0:T(8,128)(2,1)} %get-tuple-element.19), calls=%async_computation | async-start | bytes 3145728 | tf_op jit(solution)/shard_map/all_to_all | solution.py:317
  17.9 24.4 %all-to-all-done.arrived_ref = bf16[128,48,128]{2,1,0:T(8,128)(2,1)S(1)} async-done(((bf16[128,48,128]{2,1,0:T(8,128)(2,1)}), bf16[128,48,128]{2,1,0:T(8,128)(2,1)S(1)}, u32[]{:S(2)}, u32[]{:S(2)}) %all-to-all-start) | async-done | bytes 1572896 | tf_op jit(solution)/shard_map/all_to_all | solution.py:317
  42.2 1.4 shard_map.119
  43.6 5.8 %all-to-all-start.1 = ((bf16[128,32,128]{2,1,0:T(8,128)(2,1)}), bf16[128,32,128]{2,1,0:T(8,128)(2,1)}, u32[]{:S(2)}, u32[]{:S(2)}) async-start(bf16[128,32,128]{2,1,0:T(8,128)(2,1)} %shard_map.119), calls=%async_computation.1 | async-start | bytes 2097152 | tf_op jit(solution)/shard_map/all_to_all | solution.py:317
  49.4 1.2 copy-done.3
  50.6 1.2 copy-done.4
  51.8 5.1 %shard_map.120.local_ref = f32[128,4096]{1,0:T(8,128)S(1)} custom-call(bf16[128,4096]{1,0:T(8,128)(2,1)S(1)} %copy-done.4, bf16[128,4096]{1,0:T(8,128)(2,1)S(1)} %copy-done.1, bf16[128,4096]{1,0:T(8,128)(2,1)S(1)} %copy-done.3, f32[32,128]{1,0:T(8,128)S(1)} %get-tuple-element.21.by_head_ref, f32[128,32]{1,0:T(8,128)S(1)} %get-tuple-element.20.by_token_ref), custom_call_target="tpu_custom_call" | custom-call | flops 268435456 | bytes 5275648 | tf_op jit(solution)/shard_map/pallas_call | solution.py:25
  56.9 11.1 %all-to-all-done.1 = bf16[128,32,128]{2,1,0:T(8,128)(2,1)} async-done(((bf16[128,32,128]{2,1,0:T(8,128)(2,1)}), bf16[128,32,128]{2,1,0:T(8,128)(2,1)}, u32[]{:S(2)}, u32[]{:S(2)}) %all-to-all-start.1) | async-done | bytes 1048608 | tf_op jit(solution)/shard_map/all_to_all | solution.py:317
  68.0 1.2 copy-done.5
  69.2 1.2 copy-done.6
  70.4 1.2 copy-done.7
  71.7 5.0 %shard_map.121 = (bf16[128,4096]{1,0:T(8,128)(2,1)S(1)}, bf16[16,8,4096]{2,1,0:T(8,128)(2,1)}, bf16[16,8,4096]{2,1,0:T(8,128)(2,1)S(1)}) custom-call(bf16[128,4096]{1,0:T(8,128)(2,1)S(1)} %copy-done.5, bf16[32,128,128]{2,1,0:T(8,128)(2,1)} %bitcast.1.carried_ref, f32[128,32]{1,0:T(8,128)S(1)} %get-tuple-element.20.by_token_ref, ...), custom_call_target="tpu_custom_call" | custom-call | flops 402653184 | bytes 9487360 | tf_op jit(solution)/shard_map/pallas_call | solution.py:25
  76.6 19.5 %all_to_all.30 = bf16[16,8,4096]{2,1,0:T(8,128)(2,1)S(1)} all-to-all(bf16[16,8,4096]{2,1,0:T(8,128)(2,1)S(1)} %get-tuple-element.28), channel_id=1, replica_groups=mesh['grp'=8,'seq'=16] {'seq'}, dimensions={0} | all-to-all | bytes 2097152 | tf_op jit(solution)/shard_map/all_to_all | solution.py:317
  96.1 3.8 %all-to-all-start.2 = ((bf16[16,8,4096]{2,1,0:T(8,128)(2,1)}), bf16[16,8,4096]{2,1,0:T(8,128)(2,1)S(1)}, u32[]{:S(2)}, u32[]{:S(2)}) async-start(bf16[16,8,4096]{2,1,0:T(8,128)(2,1)} %get-tuple-element.23), calls=%async_computation.2 | async-start | bytes 2097152 | tf_op jit(solution)/shard_map/all_to_all | solution.py:317
  100.8 2.5 collective-permute-start.13
  103.3 12.6 %all-to-all-done.2 = bf16[16,8,4096]{2,1,0:T(8,128)(2,1)S(1)} async-done(((bf16[16,8,4096]{2,1,0:T(8,128)(2,1)}), bf16[16,8,4096]{2,1,0:T(8,128)(2,1)S(1)}, u32[]{:S(2)}, u32[]{:S(2)}) %all-to-all-start.2) | async-done | bytes 1048608 | tf_op jit(solution)/shard_map/all_to_all | solution.py:317
  116.6 10.8 %collective-permute-done.12.left_ref = bf16[128,4096]{1,0:T(8,128)(2,1)} collective-permute-done((bf16[128,4096]{1,0:T(8,128)(2,1)S(1)}, bf16[128,4096]{1,0:T(8,128)(2,1)}, u32[]{:S(2)}, u32[]{:S(2)}) %collective-permute-start.12) | collective-permute-done | bytes 1048608 | tf_op jit(solution)/shard_map/ppermute | solution.py:314
  127.5 1.1 slice.82
  128.6 2.0 collective-permute-start.14
  130.6 1.1 slice.83
  131.7 18.1 %collective-permute-done.left_ref = bf16[128,4096]{1,0:T(8,128)(2,1)S(1)} collective-permute-done((bf16[128,4096]{1,0:T(8,128)(2,1)S(1)}, bf16[128,4096]{1,0:T(8,128)(2,1)S(1)}, u32[]{:S(2)}, u32[]{:S(2)}) %collective-permute-start) | collective-permute-done | bytes 1048608 | tf_op jit(solution)/shard_map/ppermute | solution.py:314
  150.0 2.0 collective-permute-start.2
  152.0 1.5 collective-permute-start.3
  153.6 7.5 %collective-permute-done.14.far_a_ref = bf16[64,4096]{1,0:T(8,128)(2,1)S(1)} collective-permute-done((bf16[64,4096]{1,0:T(8,128)(2,1)S(1)}, bf16[64,4096]{1,0:T(8,128)(2,1)S(1)}, u32[]{:S(2)}, u32[]{:S(2)}) %collective-permute-start.14) | collective-permute-done | bytes 524320 | tf_op jit(solution)/shard_map/ppermute | solution.py:314
  161.1 3.1 %collective-permute-done.15.far_b_ref = bf16[64,4096]{1,0:T(8,128)(2,1)S(1)} collective-permute-done((bf16[64,4096]{1,0:T(8,128)(2,1)S(1)}, bf16[64,4096]{1,0:T(8,128)(2,1)S(1)}, u32[]{:S(2)}, u32[]{:S(2)}) %collective-permute-start.15) | collective-permute-done | bytes 524320 | tf_op jit(solution)/shard_map/ppermute | solution.py:315
  164.2 24.5 %shard_map.123 = (bf16[128,4096]{1,0:T(8,128)(2,1)S(1)}, bf16[128,4096]{1,0:T(8,128)(2,1)S(1)}, bf16[128,4096]{1,0:T(8,128)(2,1)S(1)}, bf16[128,4096]{1,0:T(8,128)(2,1)S(1)}) custom-call(bf16[128,4096]{1,0:T(8,128)(2,1)S(1)} %bitcast.21, bf16[128,4096]{1,0:T(8,128)(2,1)} %collective-permute-done.12.left_ref, ...), custom_call_target="tpu_custom_call" | custom-call | flops 14495514624 | bytes 36700160 | tf_op jit(solution)/shard_map/pallas_call | solution.py:266
  188.8 1.9 collective-permute-start.20
  190.9 3.1 %collective-permute-start.18 = (bf16[64,4096]{1,0:T(8,128)(2,1)S(1)}, bf16[64,4096]{1,0:T(8,128)(2,1)S(1)}, u32[]{:S(2)}, u32[]{:S(2)}) collective-permute-start(bf16[64,4096]{1,0:T(8,128)(2,1)S(1)} %slice.75), channel_id=1, source_target_pairs={{0,96},{16,112},{32,0},{48,16},{64,32},{80,48},{96,64},{112,80},{1... | collective-permute-start | bytes 1572872 | tf_op jit(solution)/shard_map/ppermute | solution.py:315
  194.3 23.8 %shard_map.122 = (bf16[128,4096]{1,0:T(8,128)(2,1)S(1)}, bf16[128,4096]{1,0:T(8,128)(2,1)S(1)}, bf16[128,4096]{1,0:T(8,128)(2,1)S(1)}, bf16[128,4096]{1,0:T(8,128)(2,1)S(1)}) custom-call(bf16[128,4096]{1,0:T(8,128)(2,1)S(1)} %bitcast.18, bf16[128,4096]{1,0:T(8,128)(2,1)S(1)} %collective-permute-done.left_ref, ...), custom_call_target="tpu_custom_call" | custom-call | flops 14495514624 | bytes 36700160 | tf_op jit(solution)/shard_map/pallas_call | solution.py:266
  218.2 3.2 %collective-permute-start.10 = (bf16[64,4096]{1,0:T(8,128)(2,1)S(1)}, bf16[64,4096]{1,0:T(8,128)(2,1)S(1)}, u32[]{:S(2)}, u32[]{:S(2)}) collective-permute-start(bf16[64,4096]{1,0:T(8,128)(2,1)S(1)} %get-tuple-element.40), channel_id=1, source_target_pairs={{0,96},{16,112},{32,0},{48,16},{64,32},{80,48},{96,64},{112,80},{1... | collective-permute-start | bytes 1572872 | tf_op jit(solution)/shard_map/ppermute | solution.py:315
  223.3 3.3 %collective-permute-start.8 = (bf16[64,4096]{1,0:T(8,128)(2,1)}, bf16[64,4096]{1,0:T(8,128)(2,1)}, u32[]{:S(2)}, u32[]{:S(2)}) collective-permute-start(bf16[64,4096]{1,0:T(8,128)(2,1)} %slice.65), channel_id=1, source_target_pairs={{0,96},{16,112},{32,0},{48,16},{64,32},{80,48},{96,64},{112,80},{1... | collective-permute-start | bytes 1572872 | tf_op jit(solution)/shard_map/ppermute | solution.py:315
  226.7 7.1 %collective-permute-done.10 = bf16[64,4096]{1,0:T(8,128)(2,1)S(1)} collective-permute-done((bf16[64,4096]{1,0:T(8,128)(2,1)S(1)}, bf16[64,4096]{1,0:T(8,128)(2,1)S(1)}, u32[]{:S(2)}, u32[]{:S(2)}) %collective-permute-start.10) | collective-permute-done | bytes 524320 | tf_op jit(solution)/shard_map/ppermute | solution.py:315
  233.9 3.7 %collective-permute-start.21 = (bf16[64,4096]{1,0:T(8,128)(2,1)S(1)}, bf16[64,4096]{1,0:T(8,128)(2,1)S(1)}, u32[]{:S(2)}, u32[]{:S(2)}) collective-permute-start(bf16[64,4096]{1,0:T(8,128)(2,1)S(1)} %add_convert_fusion.1), channel_id=1, source_target_pairs={{0,96},{16,112},{32,0},{48,16},{64,32},{80,48},{96,64},{112,80},{1... | collective-permute-start | bytes 1572872 | tf_op jit(solution)/shard_map/ppermute | solution.py:315
  237.6 0.9 add_convert_fusion.5
  239.3 0.9 add_convert_fusion.7
  240.2 3.3 %collective-permute-start.11 = (bf16[64,4096]{1,0:T(8,128)(2,1)}, bf16[64,4096]{1,0:T(8,128)(2,1)}, u32[]{:S(2)}, u32[]{:S(2)}) collective-permute-start(bf16[64,4096]{1,0:T(8,128)(2,1)} %add_convert_fusion.5), channel_id=1, source_target_pairs={{0,96},{16,112},{32,0},{48,16},{64,32},{80,48},{96,64},{112,80},{1... | collective-permute-start | bytes 1572872 | tf_op jit(solution)/shard_map/ppermute | solution.py:315
  243.5 7.2 %collective-permute-done.21 = bf16[64,4096]{1,0:T(8,128)(2,1)S(1)} collective-permute-done((bf16[64,4096]{1,0:T(8,128)(2,1)S(1)}, bf16[64,4096]{1,0:T(8,128)(2,1)S(1)}, u32[]{:S(2)}, u32[]{:S(2)}) %collective-permute-start.21) | collective-permute-done | bytes 524320 | tf_op jit(solution)/shard_map/ppermute | solution.py:315
  250.7 3.1 %collective-permute-done.17 = bf16[64,4096]{1,0:T(8,128)(2,1)S(1)} collective-permute-done((bf16[64,4096]{1,0:T(8,128)(2,1)S(1)}, bf16[64,4096]{1,0:T(8,128)(2,1)S(1)}, u32[]{:S(2)}, u32[]{:S(2)}) %collective-permute-start.17) | collective-permute-done | bytes 524320 | tf_op jit(solution)/shard_map/ppermute | solution.py:314
  254.3 1.1 maximum_bitcast_fusion.1
  255.4 6.5 %all-to-all-start.5 = ((bf16[16,8,4096]{2,1,0:T(8,128)(2,1)}), bf16[16,8,4096]{2,1,0:T(8,128)(2,1)S(1)}, u32[]{:S(2)}, u32[]{:S(2)}) async-start(bf16[16,8,4096]{2,1,0:T(8,128)(2,1)} %maximum_bitcast_fusion.1), calls=%async_computation.5 | async-start | bytes 2097152 | tf_op jit(solution)/shard_map/all_to_all | solution.py:317
  261.9 3.2 %collective-permute-done.7 = bf16[64,4096]{1,0:T(8,128)(2,1)} collective-permute-done((bf16[64,4096]{1,0:T(8,128)(2,1)}, bf16[64,4096]{1,0:T(8,128)(2,1)}, u32[]{:S(2)}, u32[]{:S(2)}) %collective-permute-start.7) | collective-permute-done | bytes 524320 | tf_op jit(solution)/shard_map/ppermute | solution.py:314
  265.1 2.0 add_convert_fusion.6
  267.3 10.2 %all-to-all-done.5.rest_1_ = bf16[16,8,4096]{2,1,0:T(8,128)(2,1)S(1)} async-done(((bf16[16,8,4096]{2,1,0:T(8,128)(2,1)}), bf16[16,8,4096]{2,1,0:T(8,128)(2,1)S(1)}, u32[]{:S(2)}, u32[]{:S(2)}) %all-to-all-start.5) | async-done | bytes 1048608 | tf_op jit(solution)/shard_map/all_to_all | solution.py:317
  277.4 16.2 %all_to_all.31.rest_0_ = bf16[16,8,4096]{2,1,0:T(8,128)(2,1)S(1)} all-to-all(bf16[16,8,4096]{2,1,0:T(8,128)(2,1)S(1)} %maximum_bitcast_fusion), channel_id=1, replica_groups=mesh['grp'=8,'seq'=16] {'seq'}, dimensions={0} | all-to-all | bytes 2097152 | tf_op jit(solution)/shard_map/all_to_all | solution.py:317
  293.7 2.4 shard_map.124
  (57 shorter events, 6.7 us)
Async XLA Ops:
  0.0 164.2 %collective-permute-start.4 = (bf16[2,576,4096]{2,1,0:T(8,128)(2,1)}, bf16[2,576,4096]{2,1,0:T(8,128)(2,1)}, u32[]{:S(2)}, u32[]{:S(2)}) collective-permute-start(bf16[2,576,4096]{2,1,0:T(8,128)(2,1)} %bitcast.28), channel_id=1, source_target_pairs={{0,16},{16,0},{32,48},{48,32},{64,80},{80,64},{96,112},{112,96},{1... | collective-permute-start | bytes 28311560 | tf_op jit(solution)/shard_map/ppermute | solution.py:322
  0.0 1.2 copy-start
  1.2 1.2 copy-start.2
  2.5 0.7 copy-start.8
  6.5 35.7 %all-to-all-start = ((bf16[128,48,128]{2,1,0:T(8,128)(2,1)}), bf16[128,48,128]{2,1,0:T(8,128)(2,1)S(1)}, u32[]{:S(2)}, u32[]{:S(2)}) async-start(bf16[128,48,128]{2,1,0:T(8,128)(2,1)} %get-tuple-element.19), calls=%async_computation | async-start | bytes 3145728 | tf_op jit(solution)/shard_map/all_to_all | solution.py:317
  17.8 31.6 %copy-start.1 = (bf16[128,4096]{1,0:T(8,128)(2,1)S(1)}, bf16[128,4096]{1,0:T(8,128)(2,1)}, u32[]{:S(2)}) copy-start(bf16[128,4096]{1,0:T(8,128)(2,1)} %key_ref.3) | copy-start | bytes 3145732
  17.8 134.2 %collective-permute-start.5 = (bf16[576,4096]{1,0:T(8,128)(2,1)}, bf16[576,4096]{1,0:T(8,128)(2,1)}, u32[]{:S(2)}, u32[]{:S(2)}) collective-permute-start(bf16[576,4096]{1,0:T(8,128)(2,1)} %bitcast.31), channel_id=1, source_target_pairs={{0,16},{16,0},{32,48},{48,32},{64,80},{80,64},{96,112},{112,96},{1... | collective-permute-start | bytes 14155784 | tf_op jit(solution)/shard_map/ppermute | solution.py:323
  43.6 24.4 %all-to-all-start.1 = ((bf16[128,32,128]{2,1,0:T(8,128)(2,1)}), bf16[128,32,128]{2,1,0:T(8,128)(2,1)}, u32[]{:S(2)}, u32[]{:S(2)}) async-start(bf16[128,32,128]{2,1,0:T(8,128)(2,1)} %shard_map.119), calls=%async_computation.1 | async-start | bytes 2097152 | tf_op jit(solution)/shard_map/all_to_all | solution.py:317
  49.4 1.2 copy-start.3
  50.6 1.2 copy-start.4
  51.8 16.2 %copy-start.9 = (f32[4096]{0:T(1024)S(1)}, f32[4096]{0:T(1024)}, u32[]{:S(2)}) copy-start(f32[4096]{0:T(1024)} %param.18) | copy-start | bytes 49156
  51.8 16.2 %copy-start.10 = (f32[4096]{0:T(1024)S(1)}, f32[4096]{0:T(1024)}, u32[]{:S(2)}) copy-start(f32[4096]{0:T(1024)} %param.19) | copy-start | bytes 49156
  51.8 16.2 %copy-start.11 = (s32[128,2]{0,1:T(2,128)S(1)}, s32[128,2]{0,1:T(2,128)}, u32[]{:S(2)}) copy-start(s32[128,2]{0,1:T(2,128)} %param.20) | copy-start | bytes 3076
  68.0 1.2 copy-start.5
  69.2 1.2 copy-start.6
  70.4 1.2 copy-start.7
  96.1 19.8 %all-to-all-start.2 = ((bf16[16,8,4096]{2,1,0:T(8,128)(2,1)}), bf16[16,8,4096]{2,1,0:T(8,128)(2,1)S(1)}, u32[]{:S(2)}, u32[]{:S(2)}) async-start(bf16[16,8,4096]{2,1,0:T(8,128)(2,1)} %get-tuple-element.23), calls=%async_computation.2 | async-start | bytes 2097152 | tf_op jit(solution)/shard_map/all_to_all | solution.py:317
  100.0 27.5 %collective-permute-start.12 = (bf16[128,4096]{1,0:T(8,128)(2,1)S(1)}, bf16[128,4096]{1,0:T(8,128)(2,1)}, u32[]{:S(2)}, u32[]{:S(2)}) collective-permute-start(bf16[128,4096]{1,0:T(8,128)(2,1)S(1)} %bitcast.19), channel_id=1, source_target_pairs={{0,32},{16,48},{32,64},{48,80},{64,96},{80,112},{96,0},{112,16},{1... | collective-permute-start | bytes 3145736 | tf_op jit(solution)/shard_map/ppermute | solution.py:314
  100.8 27.9 %collective-permute-start.13 = (bf16[128,4096]{1,0:T(8,128)(2,1)S(1)}, bf16[128,4096]{1,0:T(8,128)(2,1)}, u32[]{:S(2)}, u32[]{:S(2)}) collective-permute-start(bf16[128,4096]{1,0:T(8,128)(2,1)S(1)} %bitcast.20), channel_id=1, source_target_pairs={{0,96},{16,112},{32,0},{48,16},{64,32},{80,48},{96,64},{112,80},{1... | collective-permute-start | bytes 3145736 | tf_op jit(solution)/shard_map/ppermute | solution.py:315
  115.9 33.9 %collective-permute-start = (bf16[128,4096]{1,0:T(8,128)(2,1)S(1)}, bf16[128,4096]{1,0:T(8,128)(2,1)S(1)}, u32[]{:S(2)}, u32[]{:S(2)}) collective-permute-start(bf16[128,4096]{1,0:T(8,128)(2,1)S(1)} %bitcast.16), channel_id=1, source_target_pairs={{0,32},{16,48},{32,64},{48,80},{64,96},{80,112},{96,0},{112,16},{1... | collective-permute-start | bytes 3145736 | tf_op jit(solution)/shard_map/ppermute | solution.py:314
  127.5 22.5 %collective-permute-start.1 = (bf16[128,4096]{1,0:T(8,128)(2,1)S(1)}, bf16[128,4096]{1,0:T(8,128)(2,1)S(1)}, u32[]{:S(2)}, u32[]{:S(2)}) collective-permute-start(bf16[128,4096]{1,0:T(8,128)(2,1)S(1)} %bitcast.17), channel_id=1, source_target_pairs={{0,96},{16,112},{32,0},{48,16},{64,32},{80,48},{96,64},{112,80},{1... | collective-permute-start | bytes 3145736 | tf_op jit(solution)/shard_map/ppermute | solution.py:315
  128.6 32.4 %collective-permute-start.14 = (bf16[64,4096]{1,0:T(8,128)(2,1)S(1)}, bf16[64,4096]{1,0:T(8,128)(2,1)S(1)}, u32[]{:S(2)}, u32[]{:S(2)}) collective-permute-start(bf16[64,4096]{1,0:T(8,128)(2,1)S(1)} %slice.82), channel_id=1, source_target_pairs={{0,32},{16,48},{32,64},{48,80},{64,96},{80,112},{96,0},{112,16},{1... | collective-permute-start | bytes 1572872 | tf_op jit(solution)/shard_map/ppermute | solution.py:314
  149.8 14.4 %collective-permute-start.15 = (bf16[64,4096]{1,0:T(8,128)(2,1)S(1)}, bf16[64,4096]{1,0:T(8,128)(2,1)S(1)}, u32[]{:S(2)}, u32[]{:S(2)}) collective-permute-start(bf16[64,4096]{1,0:T(8,128)(2,1)S(1)} %slice.83), channel_id=1, source_target_pairs={{0,96},{16,112},{32,0},{48,16},{64,32},{80,48},{96,64},{112,80},{1... | collective-permute-start | bytes 1572872 | tf_op jit(solution)/shard_map/ppermute | solution.py:315
  150.0 44.1 %collective-permute-start.2 = (bf16[64,4096]{1,0:T(8,128)(2,1)S(1)}, bf16[64,4096]{1,0:T(8,128)(2,1)S(1)}, u32[]{:S(2)}, u32[]{:S(2)}) collective-permute-start(bf16[64,4096]{1,0:T(8,128)(2,1)S(1)} %slice.80), channel_id=1, source_target_pairs={{0,32},{16,48},{32,64},{48,80},{64,96},{80,112},{96,0},{112,16},{1... | collective-permute-start | bytes 1572872 | tf_op jit(solution)/shard_map/ppermute | solution.py:314
  152.0 42.3 %collective-permute-start.3 = (bf16[64,4096]{1,0:T(8,128)(2,1)S(1)}, bf16[64,4096]{1,0:T(8,128)(2,1)S(1)}, u32[]{:S(2)}, u32[]{:S(2)}) collective-permute-start(bf16[64,4096]{1,0:T(8,128)(2,1)S(1)} %slice.81), channel_id=1, source_target_pairs={{0,96},{16,112},{32,0},{48,16},{64,32},{80,48},{96,64},{112,80},{1... | collective-permute-start | bytes 1572872 | tf_op jit(solution)/shard_map/ppermute | solution.py:315
  188.8 34.4 %collective-permute-start.20 = (bf16[64,4096]{1,0:T(8,128)(2,1)S(1)}, bf16[64,4096]{1,0:T(8,128)(2,1)S(1)}, u32[]{:S(2)}, u32[]{:S(2)}) collective-permute-start(bf16[64,4096]{1,0:T(8,128)(2,1)S(1)} %get-tuple-element.36), channel_id=1, source_target_pairs={{0,96},{16,112},{32,0},{48,16},{64,32},{80,48},{96,64},{112,80},{1... | collective-permute-start | bytes 1572872 | tf_op jit(solution)/shard_map/ppermute | solution.py:315
  190.6 32.7 %collective-permute-start.16 = (bf16[64,4096]{1,0:T(8,128)(2,1)S(1)}, bf16[64,4096]{1,0:T(8,128)(2,1)S(1)}, u32[]{:S(2)}, u32[]{:S(2)}) collective-permute-start(bf16[64,4096]{1,0:T(8,128)(2,1)S(1)} %get-tuple-element.35), channel_id=1, source_target_pairs={{0,32},{16,48},{32,64},{48,80},{64,96},{80,112},{96,0},{112,16},{1... | collective-permute-start | bytes 1572872 | tf_op jit(solution)/shard_map/ppermute | solution.py:314
  190.9 49.3 %collective-permute-start.18 = (bf16[64,4096]{1,0:T(8,128)(2,1)S(1)}, bf16[64,4096]{1,0:T(8,128)(2,1)S(1)}, u32[]{:S(2)}, u32[]{:S(2)}) collective-permute-start(bf16[64,4096]{1,0:T(8,128)(2,1)S(1)} %slice.75), channel_id=1, source_target_pairs={{0,96},{16,112},{32,0},{48,16},{64,32},{80,48},{96,64},{112,80},{1... | collective-permute-start | bytes 1572872 | tf_op jit(solution)/shard_map/ppermute | solution.py:315
  194.0 46.2 %collective-permute-start.19 = (bf16[64,4096]{1,0:T(8,128)(2,1)S(1)}, bf16[64,4096]{1,0:T(8,128)(2,1)S(1)}, u32[]{:S(2)}, u32[]{:S(2)}) collective-permute-start(bf16[64,4096]{1,0:T(8,128)(2,1)S(1)} %slice.77), channel_id=1, source_target_pairs={{0,32},{16,48},{32,64},{48,80},{64,96},{80,112},{96,0},{112,16},{1... | collective-permute-start | bytes 1572872 | tf_op jit(solution)/shard_map/ppermute | solution.py:314
  218.2 15.6 %collective-permute-start.10 = (bf16[64,4096]{1,0:T(8,128)(2,1)S(1)}, bf16[64,4096]{1,0:T(8,128)(2,1)S(1)}, u32[]{:S(2)}, u32[]{:S(2)}) collective-permute-start(bf16[64,4096]{1,0:T(8,128)(2,1)S(1)} %get-tuple-element.40), channel_id=1, source_target_pairs={{0,96},{16,112},{32,0},{48,16},{64,32},{80,48},{96,64},{112,80},{1... | collective-permute-start | bytes 1572872 | tf_op jit(solution)/shard_map/ppermute | solution.py:315
  223.2 16.1 %collective-permute-start.6 = (bf16[64,4096]{1,0:T(8,128)(2,1)S(1)}, bf16[64,4096]{1,0:T(8,128)(2,1)S(1)}, u32[]{:S(2)}, u32[]{:S(2)}) collective-permute-start(bf16[64,4096]{1,0:T(8,128)(2,1)S(1)} %get-tuple-element.39), channel_id=1, source_target_pairs={{0,32},{16,48},{32,64},{48,80},{64,96},{80,112},{96,0},{112,16},{1... | collective-permute-start | bytes 1572872 | tf_op jit(solution)/shard_map/ppermute | solution.py:314
  223.3 38.6 %collective-permute-start.8 = (bf16[64,4096]{1,0:T(8,128)(2,1)}, bf16[64,4096]{1,0:T(8,128)(2,1)}, u32[]{:S(2)}, u32[]{:S(2)}) collective-permute-start(bf16[64,4096]{1,0:T(8,128)(2,1)} %slice.65), channel_id=1, source_target_pairs={{0,96},{16,112},{32,0},{48,16},{64,32},{80,48},{96,64},{112,80},{1... | collective-permute-start | bytes 1572872 | tf_op jit(solution)/shard_map/ppermute | solution.py:315
  233.9 16.8 %collective-permute-start.21 = (bf16[64,4096]{1,0:T(8,128)(2,1)S(1)}, bf16[64,4096]{1,0:T(8,128)(2,1)S(1)}, u32[]{:S(2)}, u32[]{:S(2)}) collective-permute-start(bf16[64,4096]{1,0:T(8,128)(2,1)S(1)} %add_convert_fusion.1), channel_id=1, source_target_pairs={{0,96},{16,112},{32,0},{48,16},{64,32},{80,48},{96,64},{112,80},{1... | collective-permute-start | bytes 1572872 | tf_op jit(solution)/shard_map/ppermute | solution.py:315
  239.3 14.6 %collective-permute-start.17 = (bf16[64,4096]{1,0:T(8,128)(2,1)S(1)}, bf16[64,4096]{1,0:T(8,128)(2,1)S(1)}, u32[]{:S(2)}, u32[]{:S(2)}) collective-permute-start(bf16[64,4096]{1,0:T(8,128)(2,1)S(1)} %add_convert_fusion.3), channel_id=1, source_target_pairs={{0,32},{16,48},{32,64},{48,80},{64,96},{80,112},{96,0},{112,16},{1... | collective-permute-start | bytes 1572872 | tf_op jit(solution)/shard_map/ppermute | solution.py:314
  240.2 21.7 %collective-permute-start.9 = (bf16[64,4096]{1,0:T(8,128)(2,1)}, bf16[64,4096]{1,0:T(8,128)(2,1)}, u32[]{:S(2)}, u32[]{:S(2)}) collective-permute-start(bf16[64,4096]{1,0:T(8,128)(2,1)} %slice.67), channel_id=1, source_target_pairs={{0,32},{16,48},{32,64},{48,80},{64,96},{80,112},{96,0},{112,16},{1... | collective-permute-start | bytes 1572872 | tf_op jit(solution)/shard_map/ppermute | solution.py:314
  240.2 21.7 %collective-permute-start.11 = (bf16[64,4096]{1,0:T(8,128)(2,1)}, bf16[64,4096]{1,0:T(8,128)(2,1)}, u32[]{:S(2)}, u32[]{:S(2)}) collective-permute-start(bf16[64,4096]{1,0:T(8,128)(2,1)} %add_convert_fusion.5), channel_id=1, source_target_pairs={{0,96},{16,112},{32,0},{48,16},{64,32},{80,48},{96,64},{112,80},{1... | collective-permute-start | bytes 1572872 | tf_op jit(solution)/shard_map/ppermute | solution.py:315
  250.7 14.5 %collective-permute-start.7 = (bf16[64,4096]{1,0:T(8,128)(2,1)}, bf16[64,4096]{1,0:T(8,128)(2,1)}, u32[]{:S(2)}, u32[]{:S(2)}) collective-permute-start(bf16[64,4096]{1,0:T(8,128)(2,1)} %add_convert_fusion.7), channel_id=1, source_target_pairs={{0,32},{16,48},{32,64},{48,80},{64,96},{80,112},{96,0},{112,16},{1... | collective-permute-start | bytes 1572872 | tf_op jit(solution)/shard_map/ppermute | solution.py:314
  255.4 22.1 %all-to-all-start.5 = ((bf16[16,8,4096]{2,1,0:T(8,128)(2,1)}), bf16[16,8,4096]{2,1,0:T(8,128)(2,1)S(1)}, u32[]{:S(2)}, u32[]{:S(2)}) async-start(bf16[16,8,4096]{2,1,0:T(8,128)(2,1)} %maximum_bitcast_fusion.1), calls=%async_computation.5 | async-start | bytes 2097152 | tf_op jit(solution)/shard_map/all_to_all | solution.py:317
  267.1 26.5 %copy-start.12 = (f32[128,2]{0,1:T(2,128)S(1)}, f32[128,2]{0,1:T(2,128)}, u32[]{:S(2)}) copy-start(f32[128,2]{0,1:T(2,128)} %param.21) | copy-start | bytes 3076

commit v2 on v1

v2 whole, which is shorter than its diff:
```python
import functools

import jax
import jax.numpy as jnp
from jax import lax
from jax.experimental import pallas as pl
from jax.experimental.pallas import tpu as pltpu
from jax.sharding import Mesh
from jax.sharding import PartitionSpec as P

F32, BF16 = (jnp.float32, jnp.bfloat16)
HEAD = 128
EXTRA = 8
MIB = 1 << 20
NT = (((1,), (1,)), ((), ()))
TN = (((0,), (0,)), ((), ()))


def vmem(count):
    return [pl.BlockSpec(memory_space=pltpu.VMEM)] * count


def whole_call(kernel, outs, args, flops, limit, scratch=(), in_place=()):
    moved = sum(a.size * a.dtype.itemsize for a in (*args, *outs))
    return pl.pallas_call(
        kernel,
        out_shape=outs,
        in_specs=[
            pl.BlockSpec(memory_space=pltpu.HBM if place in in_place else pltpu.VMEM)
            for place in range(len(args))
        ],
        out_specs=vmem(len(outs)),
        scratch_shapes=list(scratch),
        cost_estimate=pl.CostEstimate(flops=flops, bytes_accessed=moved, transcendentals=0),
        compiler_params=pltpu.CompilerParams(vmem_limit_bytes=limit * MIB),
    )(*args)


def lane_block(h):
    return slice(h * HEAD, (h + 1) * HEAD)


def state_kernel(
    rates_in_ref,
    key_rows_ref,
    value_rows_ref,
    sent_ref,
    by_head_ref,
    by_token_ref,
    rates_ref,
    key_ref,
    value_ref,
    loaded,
    rates_loaded,
):
    heads, tokens = rates_ref.shape
    rates_copy = pltpu.make_async_copy(rates_in_ref, rates_ref, rates_loaded)
    rates_copy.start()
    groups = loaded.shape[1]
    columns = heads * HEAD // groups
    copies = [
        [
            pltpu.make_async_copy(
                source.at[:, pl.ds(g * columns, columns)],
                target.at[:, pl.ds(g * columns, columns)],
                loaded.at[place, g],
            )
            for place, (source, target) in enumerate(
                ((key_rows_ref, key_ref), (value_rows_ref, value_ref))
            )
        ]
        for g in range(groups)
    ]
    for pair in copies:
        for copy in pair:
            copy.start()
    rates_copy.wait()
    at = lambda dim: lax.broadcasted_iota(jnp.int32, (tokens, tokens), dim)
    upto = (at(0) <= at(1)).astype(F32)
    by_head = jnp.dot(
        rates_ref[...], upto, precision=lax.Precision.HIGHEST, preferred_element_type=F32
    )
    by_token = by_head.T
    by_head_ref[...] = by_head
    by_token_ref[...] = by_token
    fade = jnp.exp(by_token - by_token[tokens - 1 :, :])
    keep = jnp.broadcast_to(jnp.exp(-by_head[:, tokens - 1 :]), (heads, HEAD))
    high = keep.astype(BF16).astype(F32)
    middle = (keep - high).astype(BF16).astype(F32)
    low = keep - high - middle
    row = lax.broadcasted_iota(jnp.int32, (EXTRA, HEAD), 0)
    for h in range(heads):
        if h % (heads // groups) == 0:
            for copy in copies[h // (heads // groups)]:
                copy.wait()
        faded = (key_ref[:, lane_block(h)].astype(F32) * fade[:, h : h + 1]).astype(BF16)
        state = lax.dot_general(faded, value_ref[:, lane_block(h)], TN, preferred_element_type=F32)
        tail = jnp.where(row == 0, high[h : h + 1], 0.0)
        tail = jnp.where(row == 1, middle[h : h + 1], tail)
        tail = jnp.where(row == 2, low[h : h + 1], tail).astype(BF16)
        sent_ref[h, :HEAD, :] = state.astype(BF16)
        sent_ref[h, HEAD:, :] = tail


def scan_kernel(arrived_ref, within_ref, kept_ref, total_ref):
    def step(block, carry):
        state, kept = carry
        within_ref[block] = state
        kept_ref[block] = kept
        tail = arrived_ref[block, HEAD:, :].astype(F32)
        keep = tail[0:1] + tail[1:2] + tail[2:3]
        return keep * state + arrived_ref[block, :HEAD, :].astype(F32), keep * kept

    start = (jnp.zeros((HEAD, HEAD), F32), jnp.ones((EXTRA, HEAD), F32))
    state, kept = lax.fori_loop(0, within_ref.shape[0], step, start, unroll=4)
    total_ref[:HEAD, :] = state
    total_ref[HEAD:, :] = kept


def carry_kernel(within_ref, kept_ref, *rest):
    *total_refs, carried_ref = rest
    before = jnp.zeros((HEAD, HEAD), F32)
    for total_ref in reversed(total_refs):
        before = total_ref[:HEAD, :] + total_ref[HEAD : HEAD + 1, :] * before

    def step(block, _):
        carried = within_ref[block] + kept_ref[block, 0:1, :] * before
        carried_ref[block] = carried.astype(BF16)
        return 0

    lax.fori_loop(0, carried_ref.shape[0], step, 0, unroll=4)


def local_kernel(
    query_ref,
    key_ref,
    value_ref,
    by_head_ref,
    by_token_ref,
    out_ref,
):
    heads, tokens = by_head_ref.shape
    at = lambda dim: lax.broadcasted_iota(jnp.int32, (tokens, tokens), dim)
    causal = at(0) >= at(1)
    for h in range(heads):
        scores = lax.dot_general(
            query_ref[:, lane_block(h)], key_ref[:, lane_block(h)], NT, preferred_element_type=F32
        )
        spacing = by_head_ref[h : h + 1, :] - by_token_ref[:, h : h + 1]
        fading = jnp.exp(jnp.minimum(spacing, 0.0))
        weights = jnp.where(causal, scores * fading, 0.0).astype(BF16)
        out_ref[:, lane_block(h)] = jnp.dot(
            weights, value_ref[:, lane_block(h)], preferred_element_type=F32
        )


def places(index_ref, experts):
    tokens = index_ref.shape[1]
    expert = lax.broadcasted_iota(jnp.int32, (experts, tokens), 0)
    first, second = (index_ref[0:1, :] == expert, index_ref[1:2, :] == expert)
    named = (first | second).astype(F32)
    at = lambda dim: lax.broadcasted_iota(jnp.int32, (tokens, tokens), dim)
    earlier = (at(0) < at(1)).astype(BF16)
    slot = jnp.dot(named.astype(BF16), earlier, preferred_element_type=F32)
    return first, second, jnp.where(named > 0.0, slot, -1.0)


def chunk_rows(slot, chunk, rows):
    experts, tokens = slot.shape
    wanted = lax.broadcasted_iota(jnp.int32, (rows, tokens), 0).astype(F32) + float(chunk * rows)
    return [slot[e : e + 1, :] == wanted for e in range(experts)]


def stream_kernel(
    query_ref,
    local_ref,
    gate_ref,
    residual_ref,
    carried_ref,
    by_token_ref,
    attention_gain_ref,
    expert_gain_ref,
    index_ref,
    stream_ref,
    *rest,
):
    *bin_refs, attention_ref = rest
    tokens, width = query_ref.shape
    heads = width // HEAD
    since = jnp.exp(-by_token_ref[...])
    total = jnp.zeros((tokens, HEAD), F32)
    for h in range(heads):
        carried_out = jnp.dot(
            query_ref[:, lane_block(h)], carried_ref[h], preferred_element_type=F32
        )
        attention = local_ref[:, lane_block(h)] + since[:, h : h + 1] * carried_out
        attention_ref[:, lane_block(h)] = attention
        total = total + attention * attention
    inverse = lax.rsqrt(jnp.sum(total, axis=1, keepdims=True) / width + 1e-05)
    total = jnp.zeros((tokens, HEAD), F32)
    for h in range(heads):
        gate = gate_ref[:, lane_block(h)].astype(F32)
        gain = attention_gain_ref[:, lane_block(h)] / (1.0 + jnp.exp(-gate))
        gated = attention_ref[:, lane_block(h)] * inverse * gain
        stream = (residual_ref[:, lane_block(h)].astype(F32) + gated).astype(BF16)
        stream_ref[:, lane_block(h)] = stream
        wide = stream.astype(F32)
        total = total + wide * wide
    inverse = lax.rsqrt(jnp.sum(total, axis=1, keepdims=True) / width + 1e-05)
    experts = bin_refs[0].shape[0]
    rows = bin_refs[0].shape[1]
    slot = places(index_ref, experts)[2]
    selectors = [
        jnp.concatenate([m.astype(F32) for m in chunk_rows(slot, c, rows)], axis=0).astype(BF16)
        for c in range(len(bin_refs))
    ]
    for h in range(heads):
        wide = stream_ref[:, lane_block(h)].astype(F32)
        entry = (wide * inverse * expert_gain_ref[:, lane_block(h)]).astype(BF16)
        for selector, bin_ref in zip(selectors, bin_refs):
            picked = jnp.dot(selector, entry, preferred_element_type=F32)
            bin_ref[:, :, lane_block(h)] = picked.astype(BF16).reshape(experts, rows, HEAD)


def mix_kernel(stream_ref, index_ref, router_ref, *rest):
    *returned_refs, out_ref = rest
    experts, rows, width = returned_refs[0].shape
    first, second, slot = places(index_ref, experts)
    scale = jnp.where(first, router_ref[0:1, :], 0.0) + jnp.where(second, router_ref[1:2, :], 0.0)
    weights = []
    for c in range(len(returned_refs)):
        masks = chunk_rows(slot, c, rows)
        chosen = jnp.concatenate(
            [jnp.where(m, scale[e : e + 1, :], 0.0) for e, m in enumerate(masks)], axis=0
        ).T
        high = chosen.astype(BF16)
        weights.append((high, (chosen - high.astype(F32)).astype(BF16)))
    for h in range(width // HEAD // 4):
        columns = slice(h * 4 * HEAD, (h + 1) * 4 * HEAD)
        total = stream_ref[:, columns].astype(F32)
        for (high, low), returned_ref in zip(weights, returned_refs):
            returned = returned_ref[:, :, columns].reshape(experts * rows, 4 * HEAD)
            total = total + jnp.dot(high, returned, preferred_element_type=F32)
            total = total + jnp.dot(low, returned, preferred_element_type=F32)
        out_ref[:, columns] = total.astype(BF16)


def expert_kernel(
    own_ref,
    left_ref,
    right_ref,
    far_ref,
    up_own_ref,
    up_other_ref,
    down_own_ref,
    down_other_ref,
    out_own_ref,
    out_left_ref,
    out_right_ref,
    out_far_ref,
    rows_ref,
    up_ref,
    down_ref,
    turned_ref,
    hidden_ref,
    up_sem,
    down_sem,
):
    count = own_ref.shape[0]
    tiles, _, tile, width = up_ref.shape
    units = down_own_ref.shape[0]
    parts, _, columns = down_ref.shape
    each = tiles // 2

    def up_copies(k):
        source = (up_own_ref, up_other_ref)[k // each]
        part = source.at[:, pl.ds(k % each * tile, tile), :]
        return [pltpu.make_async_copy(part, up_ref.at[k], up_sem.at[k])]

    def down_copies(k):
        return [
            pltpu.make_async_copy(
                source.at[:, pl.ds(k * columns, columns)],
                down_ref.at[k, pl.ds(place * units, units), :],
                down_sem.at[k, place],
            )
            for place, source in enumerate((down_own_ref, down_other_ref))
        ]

    loads = [up_copies(k) for k in range(tiles)] + [down_copies(k) for k in range(parts)]
    in_flight = 2

    def start(k):
        if k < len(loads):
            for copy in loads[k]:
                copy.start()

    def arrive(k):
        for copy in loads[k]:
            copy.wait()
        start(k + in_flight)

    for k in range(in_flight):
        start(k)
    rows_ref[0:count] = own_ref[...]
    rows_ref[count : 2 * count] = left_ref[...]
    rows_ref[2 * count : 3 * count] = right_ref[...]
    rows_ref[3 * count :] = far_ref[...]
    for k in range(tiles):
        arrive(k)
        both = up_ref[k].reshape(2 * tile, width)
        pair = lax.dot_general(both, rows_ref[...], NT, preferred_element_type=F32)
        gate, up = (pair[:tile], pair[tile:])
        hidden = gate / (1.0 + jnp.exp(-gate)) * up
        turned_ref[k * tile : (k + 1) * tile, :] = hidden.astype(BF16)
    hidden_ref[...] = turned_ref[...].T
    for k in range(parts):
        arrive(tiles + k)
        out = jnp.dot(hidden_ref[...], down_ref[k], preferred_element_type=F32).astype(BF16)
        for place, ref in enumerate((out_own_ref, out_left_ref, out_right_ref, out_far_ref)):
            ref[:, k * columns : (k + 1) * columns] = out[place * count : (place + 1) * count]


def expert_rows(blocks, up_own, up_other, down_own, down_other):
    count, width = blocks[0].shape
    units = down_own.shape[0]
    tiles, parts = (4, 4)
    tile, columns = (2 * units // tiles, width // parts)
    in_place = [pl.BlockSpec(memory_space=pltpu.HBM)] * 4
    return pl.pallas_call(
        expert_kernel,
        in_specs=vmem(len(blocks)) + in_place,
        out_specs=vmem(4),
        out_shape=[jax.ShapeDtypeStruct((count, width), BF16)] * 4,
        scratch_shapes=[
            pltpu.VMEM((4 * count, width), BF16),
            pltpu.VMEM((tiles, 2, tile, width), BF16),
            pltpu.VMEM((parts, 2 * units, columns), BF16),
            pltpu.VMEM((2 * units, 4 * count), BF16),
            pltpu.VMEM((4 * count, 2 * units), BF16),
            pltpu.SemaphoreType.DMA((tiles,)),
            pltpu.SemaphoreType.DMA((parts, 2)),
        ],
        cost_estimate=pl.CostEstimate(
            flops=4 * count * 2 * units * width * 6,
            bytes_accessed=6 * units * width * 2 + 8 * count * width * 2,
            transcendentals=0,
        ),
        compiler_params=pltpu.CompilerParams(vmem_limit_bytes=46 * MIB),
    )(*blocks, up_own, up_other, down_own, down_other)


def body(
    queries,
    key_rows,
    value_rows,
    gate_logits,
    residual_in,
    decay_rate,
    attention_gain,
    expert_gain,
    expert_index,
    router_weight,
    gate_up_weight,
    down_weight,
):
    chips, experts = (lax.axis_size("x"), lax.axis_size("seq"))
    tokens, width = queries.shape
    heads = decay_rate.shape[1]
    chunks = 2
    slots = tokens * expert_index.shape[1] // experts
    rows = slots // chunks
    count = experts * rows

    swap = lambda a: lax.ppermute(a, "core", [(0, 1), (1, 0)])
    go_ahead = lambda a: lax.ppermute(a, "x", [(i, (i + 1) % chips) for i in range(chips)])
    go_back = lambda a: lax.ppermute(a, "x", [(i, (i - 1) % chips) for i in range(chips)])
    to_later = lambda a, k: lax.ppermute(a, "x", [(i, i + k) for i in range(chips - k)])
    plane = ("core", "seq")
    after = lambda value, *earlier: lax.optimization_barrier((value, earlier))[0]
    exchange = lambda a, axis: lax.all_to_all(a, axis, split_axis=0, concat_axis=0, tiled=True)
    shape = jax.ShapeDtypeStruct

    up_own = jnp.transpose(gate_up_weight[0], (1, 2, 0))
    down_own = down_weight[0]

    sent, by_head, by_token = whole_call(
        state_kernel,
        [
            shape((heads, HEAD + EXTRA, HEAD), BF16),
            shape((heads, tokens), F32),
            shape((tokens, heads), F32),
        ],
        [decay_rate.T, key_rows, value_rows],
        2 * tokens * width * HEAD,
        62,
        [
            pltpu.VMEM((heads, tokens), F32),
            pltpu.VMEM((tokens, width), BF16),
            pltpu.VMEM((tokens, width), BF16),
            pltpu.SemaphoreType.DMA((2, 4)),
            pltpu.SemaphoreType.DMA,
        ],
        (0, 1, 2),
    )
    arrived = exchange(sent, plane)
    (local_out,) = whole_call(
        local_kernel,
        [shape((tokens, width), F32)],
        [queries, key_rows, value_rows, by_head, by_token],
        4 * tokens * width * tokens,
        16,
    )
    within, kept, total = whole_call(
        scan_kernel,
        [
            shape((heads, HEAD, HEAD), F32),
            shape((heads, EXTRA, HEAD), F32),
            shape((HEAD + EXTRA, HEAD), F32),
        ],
        [after(arrived, local_out)],
        2 * heads * HEAD * HEAD,
        8,
    )
    totals = [to_later(total, k) for k in range(1, chips)]
    (carried,) = whole_call(
        carry_kernel,
        [shape((heads, HEAD, HEAD), BF16)],
        [within, kept, *totals],
        2 * heads * HEAD * HEAD,
        8,
    )
    carried_low = exchange(carried, plane)
    index = expert_index.T
    stream, *bins = whole_call(
        stream_kernel,
        [shape((tokens, width), BF16)] + [shape((experts, rows, width), BF16)] * chunks,
        [
            queries,
            local_out,
            gate_logits,
            residual_in,
            carried_low,
            by_token,
            attention_gain[None, :],
            expert_gain[None, :],
            index,
        ],
        2 * tokens * width * (HEAD + chunks * count),
        8,
        [pltpu.VMEM((tokens, width), F32)],
    )

    up_other = swap(after(up_own, stream))
    down_other = swap(after(down_own, stream))
    weights = (up_own, up_other, down_own, down_other)
    wide = lambda a: a.astype(F32)
    plus = lambda *terms: functools.reduce(jnp.add, map(wide, terms)).astype(BF16)

    own_a, own_b = (exchange(bin_rows, "seq").reshape(count, width) for bin_rows in bins)
    left_a, right_a = (go_ahead(own_a), go_back(own_a))
    far_a = go_ahead(left_a)
    right_b = go_back(after(own_b, right_a))
    left_b = go_ahead(after(own_b, far_a))
    far_b = go_back(right_b)
    out_own_a, out_left_a, out_right_a, out_far_a = expert_rows(
        (own_a, left_a, right_a, far_a), *weights
    )
    pass_a, back_a = (go_ahead(out_far_a), go_back(out_left_a))
    out_own_b, out_left_b, out_right_b, out_far_b = expert_rows(
        (own_b, left_b, right_b, far_b), *weights
    )
    pass_b = go_back(after(out_far_b, pass_a, back_a))
    ahead_a = go_ahead(plus(out_right_a, pass_a))
    ahead_b = go_ahead(after(out_right_b, ahead_a))
    to_left_b = plus(out_left_b, pass_b)
    back_b = go_back(to_left_b)
    home = lambda *terms: plus(*terms).reshape(experts, rows, width)
    returned = [
        exchange(after(home(out_own_a, ahead_a, back_a), to_left_b), "seq"),
        exchange(home(out_own_b, ahead_b, back_b), "seq"),
    ]
    (out,) = whole_call(
        mix_kernel,
        [shape((tokens, width), BF16)],
        [stream, index, router_weight.T, *returned],
        4 * tokens * width * count * chunks,
        16,
    )
    return out


def solution(mesh):
    groups, experts = (mesh.shape["grp"], mesh.shape["seq"])
    split = Mesh(mesh.devices.reshape(groups // 2, 2, experts), ("x", "core", "seq"))
    rows = P(("x", "core", "seq"), None)
    return jax.shard_map(
        body,
        mesh=split,
        in_specs=(
            rows,
            rows,
            rows,
            rows,
            rows,
            rows,
            P(),
            P(),
            rows,
            rows,
            P("seq", None, None, ("x", "core")),
            P("seq", ("x", "core"), None),
        ),
        out_specs=rows,
        check_vma=False,
    )
```

time: 297 us -> 259 us (0.87)
  waiting for transfers between devices: 119 us -> 85 us
  blocking collectives: 35.7 us -> 60 us
  starting transfers between devices: 56.2 us -> 43.4 us
  local copies, waits for them, and re-layouts: 13.5 us -> 4.68 us
  Pallas kernels: 65.4 us -> 59.4 us
    all_to_all x4 -> x3, waiting for transfers between devices: 58.2 us -> 9.37 us  [body(): lax.all_to_all(a, axis, split_axis=0, concat_axis=0, tiled=True)]
    all_to_all x2 -> x3, blocking collectives: 35.7 us -> 60 us  [body(): lax.all_to_all(a, axis, split_axis=0, concat_axis=0, tiled=True)]
    ppermute x22 -> x17, waiting for transfers between devices: 61.1 us -> 75.6 us  [the longest x6 42.3 us: body(): lax.ppermute(a, 'x', [(i, (i + 1) % chips) for i in range(chips)])]
    all_to_all x4 -> x3, starting transfers between devices: 27.4 us -> 17.2 us  [body(): lax.all_to_all(a, axis, split_axis=0, concat_axis=0, tiled=True)]
    pallas_call x7 -> x8, Pallas kernels: 65.4 us -> 59.4 us  [the longest x2 42.9 us: expert_rows(): pl.pallas_call(expert_kernel, in_specs=vmem(len(blocks)) + in_place, out_...]
    unnamed x26, local copies, waits for them, and re-layouts: 9.3 us -> 4.68 us
    reshape x0 -> x2, other arithmetic: none -> 4.43 us  [body(): home = lambda *terms: plus(*terms).reshape(experts, rows, width)]
    slice x10 -> x0, local copies, waits for them, and re-layouts: 4.16 us -> none  [the longest x4 2.22 us: body(): far_a, far_b = (go_ahead(left[:half]), go_back(right[half:]))]
  transfers between devices with their start and end apart: 26 -> 20, of which waited for: 13 -> 8; matrix products, arithmetic and copies ran while one was open for 3% -> 2% of each run, Pallas kernels for 21% -> 19%
where the time goes in v2:
time: 259 us
  waiting for transfers between devices  85 us (33%)
  blocking collectives  60 us (23%)
  Pallas kernels  59.4 us (23%)
  starting transfers between devices  43.4 us (17%)
  other arithmetic  5.9 us (2%)
  local copies, waits for them, and re-layouts  4.68 us (2%)
    all_to_all x3, blocking collectives, body(): lax.all_to_all(a, axis, split_axis=0, concat_axis=0, tiled=True)  60 us
    pallas_call x2, Pallas kernels, expert_rows(): pl.pallas_call(expert_kernel, in_specs=vmem(len(blocks)) + in_place, out_...  42.9 us
    ppermute x6, waiting for transfers between devices, body(): lax.ppermute(a, 'x', [(i, (i + 1) % chips) for i in range(chips)])  42.3 us
    ppermute x6, waiting for transfers between devices, body(): lax.ppermute(a, 'x', [(i, (i - 1) % chips) for i in range(chips)])  31.4 us
    all_to_all x3, starting transfers between devices, body(): lax.all_to_all(a, axis, split_axis=0, concat_axis=0, tiled=True)  17.2 us
    pallas_call x6, Pallas kernels, whole_call(): pl.pallas_call(kernel, out_shape=outs, in_specs=[pl.BlockSpec(memory_spac...  16.6 us
    ppermute x6, starting transfers between devices, body(): lax.ppermute(a, 'x', [(i, (i - 1) % chips) for i in range(chips)])  13.6 us
    all_to_all x3, waiting for transfers between devices, body(): lax.all_to_all(a, axis, split_axis=0, concat_axis=0, tiled=True)  9.37 us
  transfers between devices with their start and end apart: 20, of which 8 were waited for; matrix products, arithmetic and copies ran while one was open for 2% of the time, Pallas kernels for 19%

profile of v2, /device:TPU:0, one launch (start us, length us, event | category | flops | bytes accessed | tf_op | source)
XLA Modules:
  0.0 258.6 jit_solution(4649024677171329369)
XLA Ops:
  0.0 4.9 %shard_map.118 = (bf16[32,136,128]{2,1,0:T(8,128)(2,1)}, f32[32,128]{1,0:T(8,128)}, f32[128,32]{1,0:T(8,128)}) custom-call(f32[32,128]{1,0:T(8,128)} %bitcast.26, bf16[128,4096]{1,0:T(8,128)(2,1)} %key_ref.1, bf16[128,4096]{1,0:T(8,128)(2,1)} %value_ref.1), custom_call_target="tpu_custom_call" | custom-call | flops 134217728 | bytes 3260416 | tf_op jit(solution)/shard_map/pallas_call | solution.py:25
  4.9 0.0 copy-start.6
  4.9 8.6 %all-to-all-start = ((bf16[32,136,128]{2,1,0:T(8,128)(2,1)}), bf16[32,136,128]{2,1,0:T(8,128)(2,1)S(1)}, u32[]{:S(2)}, u32[]{:S(2)}) async-start(bf16[32,136,128]{2,1,0:T(8,128)(2,1)} %get-tuple-element.32), calls=%async_computation | async-start | bytes 2228224 | tf_op jit(solution)/shard_map/all_to_all | solution.py:381
  13.5 0.0 copy-start
  13.5 1.2 copy-done
  14.7 1.2 copy-done.1
  16.0 1.2 copy-done.2
  17.2 5.1 %shard_map.119.local_ref = f32[128,4096]{1,0:T(8,128)S(1)} custom-call(bf16[128,4096]{1,0:T(8,128)(2,1)S(1)} %copy-done.2, bf16[128,4096]{1,0:T(8,128)(2,1)S(1)} %copy-done, bf16[128,4096]{1,0:T(8,128)(2,1)S(1)} %copy-done.1, f32[32,128]{1,0:T(8,128)S(1)} %copy-done.9, f32[128,32]{1,0:T(8,128)S(1)} %copy-done.6), custom_call_target="tpu_custom_call" | custom-call | flops 268435456 | bytes 5275648 | tf_op jit(solution)/shard_map/pallas_call | solution.py:25
  22.3 9.4 %all-to-all-done.arrived_ref = bf16[32,136,128]{2,1,0:T(8,128)(2,1)S(1)} async-done(((bf16[32,136,128]{2,1,0:T(8,128)(2,1)}), bf16[32,136,128]{2,1,0:T(8,128)(2,1)S(1)}, u32[]{:S(2)}, u32[]{:S(2)}) %all-to-all-start) | async-done | bytes 1114144 | tf_op jit(solution)/shard_map/all_to_all | solution.py:381
  31.6 0.3 shard_map.120
  31.9 3.4 %collective-permute-start = (f32[136,128]{1,0:T(8,128)S(1)}, f32[136,128]{1,0:T(8,128)S(1)}, u32[]{:S(2)}, u32[]{:S(2)}) collective-permute-start(f32[136,128]{1,0:T(8,128)S(1)} %get-tuple-element.36), channel_id=1, source_target_pairs={{0,32},{32,64},{64,96},{1,33},{33,65},{65,97},{2,34},{34,66},{66,9... | collective-permute-start | bytes 208904 | tf_op jit(solution)/shard_map/ppermute | solution.py:378
  35.3 4.6 %collective-permute-start.1 = (f32[136,128]{1,0:T(8,128)S(1)}, f32[136,128]{1,0:T(8,128)S(1)}, u32[]{:S(2)}, u32[]{:S(2)}) collective-permute-start(f32[136,128]{1,0:T(8,128)S(1)} %get-tuple-element.36), channel_id=1, source_target_pairs={{0,64},{32,96},{1,65},{33,97},{2,66},{34,98},{3,67},{35,99},{4,68}... | collective-permute-start | bytes 208904 | tf_op jit(solution)/shard_map/ppermute | solution.py:378
  40.0 1.3 collective-permute-start.2
  41.3 0.6 collective-permute-done.1.rest_1_
  41.9 1.3 collective-permute-done.2.rest_2_
  43.2 0.0 copy-start.10
  43.2 0.2 shard_map.121
  43.5 20.9 %all_to_all.30.carried_ref = bf16[32,128,128]{2,1,0:T(8,128)(2,1)S(1)} all-to-all(bf16[32,128,128]{2,1,0:T(8,128)(2,1)S(1)} %shard_map.121), channel_id=1, replica_groups=mesh['x'=4,'core'=2,'seq'=16] {'core','seq'}, dimensions={0} | all-to-all | bytes 2097152 | tf_op jit(solution)/shard_map/all_to_all | solution.py:381
  64.4 3.7 %shard_map.122 = (bf16[128,4096]{1,0:T(8,128)(2,1)S(1)}, bf16[16,8,4096]{2,1,0:T(8,128)(2,1)S(1)}, bf16[16,8,4096]{2,1,0:T(8,128)(2,1)}) custom-call(bf16[128,4096]{1,0:T(8,128)(2,1)S(1)} %copy-done.3, f32[128,4096]{1,0:T(8,128)S(1)} %shard_map.119.local_ref, bf16[128,4096]{1,0:T(8,128)(2,1)S(1)} %copy-done.4, bf16[128,4096]{1,0:T(8,128)(2,1)S(1)} %copy-done.5, ...), custom_call_target="tpu_custom_call" | custom-call | flops 402653184 | bytes 9487360 | tf_op jit(solution)/shard_map/pallas_call | solution.py:25
  68.1 0.0 collective-permute-start.6
  68.1 0.5 collective-permute-start.7
  68.6 20.4 %all_to_all.31 = bf16[16,8,4096]{2,1,0:T(8,128)(2,1)S(1)} all-to-all(bf16[16,8,4096]{2,1,0:T(8,128)(2,1)S(1)} %get-tuple-element.38), channel_id=1, replica_groups=mesh['x'=4,'core'=2,'seq'=16] {'seq'}, dimensions={0} | all-to-all | bytes 2097152 | tf_op jit(solution)/shard_map/all_to_all | solution.py:381
  89.0 3.6 %collective-permute-start.4 = (bf16[128,4096]{1,0:T(8,128)(2,1)S(1)}, bf16[128,4096]{1,0:T(8,128)(2,1)}, u32[]{:S(2)}, u32[]{:S(2)}) collective-permute-start(bf16[128,4096]{1,0:T(8,128)(2,1)S(1)} %bitcast.19), channel_id=1, source_target_pairs={{0,96},{32,0},{64,32},{96,64},{1,97},{33,1},{65,33},{97,65},{2,98}... | collective-permute-start | bytes 3145736 | tf_op jit(solution)/shard_map/ppermute | solution.py:377
  92.5 3.7 %all-to-all-start.3 = ((bf16[16,8,4096]{2,1,0:T(8,128)(2,1)}), bf16[16,8,4096]{2,1,0:T(8,128)(2,1)S(1)}, u32[]{:S(2)}, u32[]{:S(2)}) async-start(bf16[16,8,4096]{2,1,0:T(8,128)(2,1)} %get-tuple-element.45), calls=%async_computation.3 | async-start | bytes 2097152 | tf_op jit(solution)/shard_map/all_to_all | solution.py:381
  96.2 18.2 %collective-permute-done.3.left_ref = bf16[128,4096]{1,0:T(8,128)(2,1)} collective-permute-done((bf16[128,4096]{1,0:T(8,128)(2,1)S(1)}, bf16[128,4096]{1,0:T(8,128)(2,1)}, u32[]{:S(2)}, u32[]{:S(2)}) %collective-permute-start.3) | collective-permute-done | bytes 1048608 | tf_op jit(solution)/shard_map/ppermute | solution.py:376
  114.4 0.0 collective-permute-done.4.right_ref
  114.4 3.2 %collective-permute-start.12 = (bf16[128,4096]{1,0:T(8,128)(2,1)S(1)}, bf16[128,4096]{1,0:T(8,128)(2,1)S(1)}, u32[]{:S(2)}, u32[]{:S(2)}) collective-permute-start(bf16[128,4096]{1,0:T(8,128)(2,1)S(1)} %bitcast.15), channel_id=1, source_target_pairs={{0,96},{32,0},{64,32},{96,64},{1,97},{33,1},{65,33},{97,65},{2,98}... | collective-permute-start | bytes 3145736 | tf_op jit(solution)/shard_map/ppermute | solution.py:377
  117.6 21.1 %collective-permute-done.5.far_ref = bf16[128,4096]{1,0:T(8,128)(2,1)} collective-permute-done((bf16[128,4096]{1,0:T(8,128)(2,1)}, bf16[128,4096]{1,0:T(8,128)(2,1)}, u32[]{:S(2)}, u32[]{:S(2)}) %collective-permute-start.5) | collective-permute-done | bytes 1048608 | tf_op jit(solution)/shard_map/ppermute | solution.py:376
  138.7 3.2 %collective-permute-start.13 = (bf16[128,4096]{1,0:T(8,128)(2,1)S(1)}, bf16[128,4096]{1,0:T(8,128)(2,1)S(1)}, u32[]{:S(2)}, u32[]{:S(2)}) collective-permute-start(bf16[128,4096]{1,0:T(8,128)(2,1)S(1)} %collective-permute-done.12.right_ref), channel_id=1, source_target_pairs={{0,96},{32,0},{64,32},{96,64},{1,97},{33,1},{65,33},{97,65},{2,98}... | collective-permute-start | bytes 3145736 | tf_op jit(solution)/shard_map/ppermute | solution.py:377
  142.0 21.2 %shard_map.123 = (bf16[128,4096]{1,0:T(8,128)(2,1)S(1)}, bf16[128,4096]{1,0:T(8,128)(2,1)S(1)}, bf16[128,4096]{1,0:T(8,128)(2,1)S(1)}, bf16[128,4096]{1,0:T(8,128)(2,1)S(1)}) custom-call(bf16[128,4096]{1,0:T(8,128)(2,1)S(1)} %bitcast.20, bf16[128,4096]{1,0:T(8,128)(2,1)} %collective-permute-done.3.left_ref, ...), custom_call_target="tpu_custom_call" | custom-call | flops 14495514624 | bytes 36700160 | tf_op jit(solution)/shard_map/pallas_call | solution.py:330
  163.2 0.1 collective-permute-start.10
  163.3 2.0 collective-permute-start.8
  165.3 1.0 copy-done.12
  166.3 21.7 %shard_map.124 = (bf16[128,4096]{1,0:T(8,128)(2,1)S(1)}, bf16[128,4096]{1,0:T(8,128)(2,1)S(1)}, bf16[128,4096]{1,0:T(8,128)(2,1)}, bf16[128,4096]{1,0:T(8,128)(2,1)S(1)}) custom-call(bf16[128,4096]{1,0:T(8,128)(2,1)S(1)} %bitcast.17, bf16[128,4096]{1,0:T(8,128)(2,1)S(1)} %collective-permute-done.11.left_ref, ...), custom_call_target="tpu_custom_call" | custom-call | flops 14495514624 | bytes 36700160 | tf_op jit(solution)/shard_map/pallas_call | solution.py:330
  188.0 1.6 collective-permute-start.14
  189.6 0.2 add_convert_fusion.3
  189.8 0.6 collective-permute-start.9
  190.4 19.5 %collective-permute-done.14 = bf16[128,4096]{1,0:T(8,128)(2,1)S(1)} collective-permute-done((bf16[128,4096]{1,0:T(8,128)(2,1)S(1)}, bf16[128,4096]{1,0:T(8,128)(2,1)S(1)}, u32[]{:S(2)}, u32[]{:S(2)}) %collective-permute-start.14) | collective-permute-done | bytes 1048608 | tf_op jit(solution)/shard_map/ppermute | solution.py:377
  209.9 1.2 add_convert_fusion.1
  211.2 1.9 collective-permute-start.16
  213.1 0.1 collective-permute-start.15
  213.2 1.4 fusion
  214.6 5.0 %all-to-all-start.4 = ((bf16[16,8,4096]{2,1,0:T(8,128)(2,1)}), bf16[16,8,4096]{2,1,0:T(8,128)(2,1)S(1)}, u32[]{:S(2)}, u32[]{:S(2)}) async-start(bf16[16,8,4096]{2,1,0:T(8,128)(2,1)} %fusion), calls=%async_computation.4 | async-start | bytes 2097152 | tf_op jit(solution)/shard_map/all_to_all | solution.py:381
  219.6 11.8 %collective-permute-done.16 = bf16[128,4096]{1,0:T(8,128)(2,1)} collective-permute-done((bf16[128,4096]{1,0:T(8,128)(2,1)}, bf16[128,4096]{1,0:T(8,128)(2,1)}, u32[]{:S(2)}, u32[]{:S(2)}) %collective-permute-start.16) | collective-permute-done | bytes 1048608 | tf_op jit(solution)/shard_map/ppermute | solution.py:377
  231.4 3.0 %collective-permute-done.15 = bf16[128,4096]{1,0:T(8,128)(2,1)} collective-permute-done((bf16[128,4096]{1,0:T(8,128)(2,1)}, bf16[128,4096]{1,0:T(8,128)(2,1)}, u32[]{:S(2)}, u32[]{:S(2)}) %collective-permute-start.15) | collective-permute-done | bytes 1048608 | tf_op jit(solution)/shard_map/ppermute | solution.py:376
  234.4 3.0 %fusion.1 = bf16[16,8,4096]{2,1,0:T(8,128)(2,1)} fusion(bf16[128,4096]{1,0:T(8,128)(2,1)} %collective-permute-done.16, bf16[128,4096]{1,0:T(8,128)(2,1)} %collective-permute-done.15, bf16[128,4096]{1,0:T(8,128)(2,1)S(1)} %get-tuple-element.52), kind=kLoop, calls=%fused_computation.5 | loop fusion | flops 3145728 | bytes 4194304 | tf_op jit(solution)/shard_map/reshape | solution.py:478
  237.4 18.7 %all_to_all.32.rest_1_ = bf16[16,8,4096]{2,1,0:T(8,128)(2,1)S(1)} all-to-all(bf16[16,8,4096]{2,1,0:T(8,128)(2,1)} %fusion.1), channel_id=1, replica_groups=mesh['x'=4,'core'=2,'seq'=16] {'seq'}, dimensions={0} | all-to-all | bytes 2097152 | tf_op jit(solution)/shard_map/all_to_all | solution.py:381
  256.1 2.4 shard_map.125
  (33 shorter events, 0.1 us)
Async XLA Ops:
  4.9 8.6 %copy-start.6 = (f32[128,32]{1,0:T(8,128)S(1)}, f32[128,32]{1,0:T(8,128)}, u32[]{:S(2)}) copy-start(f32[128,32]{1,0:T(8,128)} %get-tuple-element.31.by_token_ref) | copy-start | bytes 49156
  4.9 8.6 %copy-start.9 = (f32[32,128]{1,0:T(8,128)S(1)}, f32[32,128]{1,0:T(8,128)}, u32[]{:S(2)}) copy-start(f32[32,128]{1,0:T(8,128)} %get-tuple-element.30.by_head_ref) | copy-start | bytes 49156
  4.9 26.7 %all-to-all-start = ((bf16[32,136,128]{2,1,0:T(8,128)(2,1)}), bf16[32,136,128]{2,1,0:T(8,128)(2,1)S(1)}, u32[]{:S(2)}, u32[]{:S(2)}) async-start(bf16[32,136,128]{2,1,0:T(8,128)(2,1)} %get-tuple-element.32), calls=%async_computation | async-start | bytes 2228224 | tf_op jit(solution)/shard_map/all_to_all | solution.py:381
  13.5 1.2 copy-start
  14.7 1.2 copy-start.1
  16.0 1.2 copy-start.2
  31.9 9.4 %collective-permute-start = (f32[136,128]{1,0:T(8,128)S(1)}, f32[136,128]{1,0:T(8,128)S(1)}, u32[]{:S(2)}, u32[]{:S(2)}) collective-permute-start(f32[136,128]{1,0:T(8,128)S(1)} %get-tuple-element.36), channel_id=1, source_target_pairs={{0,32},{32,64},{64,96},{1,33},{33,65},{65,97},{2,34},{34,66},{66,9... | collective-permute-start | bytes 208904 | tf_op jit(solution)/shard_map/ppermute | solution.py:378
  35.3 6.6 %collective-permute-start.1 = (f32[136,128]{1,0:T(8,128)S(1)}, f32[136,128]{1,0:T(8,128)S(1)}, u32[]{:S(2)}, u32[]{:S(2)}) collective-permute-start(f32[136,128]{1,0:T(8,128)S(1)} %get-tuple-element.36), channel_id=1, source_target_pairs={{0,64},{32,96},{1,65},{33,97},{2,66},{34,98},{3,67},{35,99},{4,68}... | collective-permute-start | bytes 208904 | tf_op jit(solution)/shard_map/ppermute | solution.py:378
  40.0 3.2 %collective-permute-start.2 = (f32[136,128]{1,0:T(8,128)S(1)}, f32[136,128]{1,0:T(8,128)S(1)}, u32[]{:S(2)}, u32[]{:S(2)}) collective-permute-start(f32[136,128]{1,0:T(8,128)S(1)} %get-tuple-element.36), channel_id=1, source_target_pairs={{0,96},{1,97},{2,98},{3,99},{4,100},{5,101},{6,102},{7,103},{8,104... | collective-permute-start | bytes 208904 | tf_op jit(solution)/shard_map/ppermute | solution.py:378
  43.2 21.1 %copy-start.3 = (bf16[128,4096]{1,0:T(8,128)(2,1)S(1)}, bf16[128,4096]{1,0:T(8,128)(2,1)}, u32[]{:S(2)}) copy-start(bf16[128,4096]{1,0:T(8,128)(2,1)} %query_ref.3) | copy-start | bytes 3145732
  43.2 21.1 %copy-start.4 = (bf16[128,4096]{1,0:T(8,128)(2,1)S(1)}, bf16[128,4096]{1,0:T(8,128)(2,1)}, u32[]{:S(2)}) copy-start(bf16[128,4096]{1,0:T(8,128)(2,1)} %gate_ref.1) | copy-start | bytes 3145732
  43.2 21.1 %copy-start.5 = (bf16[128,4096]{1,0:T(8,128)(2,1)S(1)}, bf16[128,4096]{1,0:T(8,128)(2,1)}, u32[]{:S(2)}) copy-start(bf16[128,4096]{1,0:T(8,128)(2,1)} %residual_ref.1) | copy-start | bytes 3145732
  43.2 21.2 %copy-start.7 = (f32[4096]{0:T(1024)S(1)}, f32[4096]{0:T(1024)}, u32[]{:S(2)}) copy-start(f32[4096]{0:T(1024)} %param.18) | copy-start | bytes 49156
  43.2 21.2 %copy-start.8 = (f32[4096]{0:T(1024)S(1)}, f32[4096]{0:T(1024)}, u32[]{:S(2)}) copy-start(f32[4096]{0:T(1024)} %param.19) | copy-start | bytes 49156
  43.2 21.2 %copy-start.10 = (s32[128,2]{0,1:T(2,128)S(1)}, s32[128,2]{0,1:T(2,128)}, u32[]{:S(2)}) copy-start(s32[128,2]{0,1:T(2,128)} %param.20) | copy-start | bytes 3076
  68.1 73.9 %collective-permute-start.6 = (bf16[2,576,4096]{2,1,0:T(8,128)(2,1)}, bf16[2,576,4096]{2,1,0:T(8,128)(2,1)}, u32[]{:S(2)}, u32[]{:S(2)}) collective-permute-start(bf16[2,576,4096]{2,1,0:T(8,128)(2,1)} %bitcast.27), channel_id=1, source_target_pairs={{0,16},{16,0},{1,17},{17,1},{2,18},{18,2},{3,19},{19,3},{4,20},{20... | collective-permute-start | bytes 28311560 | tf_op jit(solution)/shard_map/ppermute | solution.py:375
  68.1 73.9 %collective-permute-start.7 = (bf16[576,4096]{1,0:T(8,128)(2,1)}, bf16[576,4096]{1,0:T(8,128)(2,1)}, u32[]{:S(2)}, u32[]{:S(2)}) collective-permute-start(bf16[576,4096]{1,0:T(8,128)(2,1)} %bitcast.30), channel_id=1, source_target_pairs={{0,16},{16,0},{1,17},{17,1},{2,18},{18,2},{3,19},{19,3},{4,20},{20... | collective-permute-start | bytes 14155784 | tf_op jit(solution)/shard_map/ppermute | solution.py:375
  89.0 25.4 %collective-permute-start.3 = (bf16[128,4096]{1,0:T(8,128)(2,1)S(1)}, bf16[128,4096]{1,0:T(8,128)(2,1)}, u32[]{:S(2)}, u32[]{:S(2)}) collective-permute-start(bf16[128,4096]{1,0:T(8,128)(2,1)S(1)} %bitcast.18), channel_id=1, source_target_pairs={{0,32},{32,64},{64,96},{96,0},{1,33},{33,65},{65,97},{97,1},{2,34}... | collective-permute-start | bytes 3145736 | tf_op jit(solution)/shard_map/ppermute | solution.py:376
  89.0 25.4 %collective-permute-start.4 = (bf16[128,4096]{1,0:T(8,128)(2,1)S(1)}, bf16[128,4096]{1,0:T(8,128)(2,1)}, u32[]{:S(2)}, u32[]{:S(2)}) collective-permute-start(bf16[128,4096]{1,0:T(8,128)(2,1)S(1)} %bitcast.19), channel_id=1, source_target_pairs={{0,96},{32,0},{64,32},{96,64},{1,97},{33,1},{65,33},{97,65},{2,98}... | collective-permute-start | bytes 3145736 | tf_op jit(solution)/shard_map/ppermute | solution.py:377
  92.5 21.8 %all-to-all-start.3 = ((bf16[16,8,4096]{2,1,0:T(8,128)(2,1)}), bf16[16,8,4096]{2,1,0:T(8,128)(2,1)S(1)}, u32[]{:S(2)}, u32[]{:S(2)}) async-start(bf16[16,8,4096]{2,1,0:T(8,128)(2,1)} %get-tuple-element.45), calls=%async_computation.3 | async-start | bytes 2097152 | tf_op jit(solution)/shard_map/all_to_all | solution.py:381
  114.4 24.4 %collective-permute-start.5 = (bf16[128,4096]{1,0:T(8,128)(2,1)}, bf16[128,4096]{1,0:T(8,128)(2,1)}, u32[]{:S(2)}, u32[]{:S(2)}) collective-permute-start(bf16[128,4096]{1,0:T(8,128)(2,1)} %collective-permute-done.3.left_ref), channel_id=1, source_target_pairs={{0,32},{32,64},{64,96},{96,0},{1,33},{33,65},{65,97},{97,1},{2,34}... | collective-permute-start | bytes 3145736 | tf_op jit(solution)/shard_map/ppermute | solution.py:376
  114.4 24.4 %collective-permute-start.12 = (bf16[128,4096]{1,0:T(8,128)(2,1)S(1)}, bf16[128,4096]{1,0:T(8,128)(2,1)S(1)}, u32[]{:S(2)}, u32[]{:S(2)}) collective-permute-start(bf16[128,4096]{1,0:T(8,128)(2,1)S(1)} %bitcast.15), channel_id=1, source_target_pairs={{0,96},{32,0},{64,32},{96,64},{1,97},{33,1},{65,33},{97,65},{2,98}... | collective-permute-start | bytes 3145736 | tf_op jit(solution)/shard_map/ppermute | solution.py:377
  138.7 26.6 %collective-permute-start.11 = (bf16[128,4096]{1,0:T(8,128)(2,1)S(1)}, bf16[128,4096]{1,0:T(8,128)(2,1)S(1)}, u32[]{:S(2)}, u32[]{:S(2)}) collective-permute-start(bf16[128,4096]{1,0:T(8,128)(2,1)S(1)} %bitcast.16), channel_id=1, source_target_pairs={{0,32},{32,64},{64,96},{96,0},{1,33},{33,65},{65,97},{97,1},{2,34}... | collective-permute-start | bytes 3145736 | tf_op jit(solution)/shard_map/ppermute | solution.py:376
  138.7 26.6 %collective-permute-start.13 = (bf16[128,4096]{1,0:T(8,128)(2,1)S(1)}, bf16[128,4096]{1,0:T(8,128)(2,1)S(1)}, u32[]{:S(2)}, u32[]{:S(2)}) collective-permute-start(bf16[128,4096]{1,0:T(8,128)(2,1)S(1)} %collective-permute-done.12.right_ref), channel_id=1, source_target_pairs={{0,96},{32,0},{64,32},{96,64},{1,97},{33,1},{65,33},{97,65},{2,98}... | collective-permute-start | bytes 3145736 | tf_op jit(solution)/shard_map/ppermute | solution.py:377
  163.2 24.8 %collective-permute-start.10 = (bf16[128,4096]{1,0:T(8,128)(2,1)S(1)}, bf16[128,4096]{1,0:T(8,128)(2,1)S(1)}, u32[]{:S(2)}, u32[]{:S(2)}) collective-permute-start(bf16[128,4096]{1,0:T(8,128)(2,1)S(1)} %get-tuple-element.44), channel_id=1, source_target_pairs={{0,96},{32,0},{64,32},{96,64},{1,97},{33,1},{65,33},{97,65},{2,98}... | collective-permute-start | bytes 3145736 | tf_op jit(solution)/shard_map/ppermute | solution.py:377
  163.3 24.7 %collective-permute-start.8 = (bf16[128,4096]{1,0:T(8,128)(2,1)S(1)}, bf16[128,4096]{1,0:T(8,128)(2,1)S(1)}, u32[]{:S(2)}, u32[]{:S(2)}) collective-permute-start(bf16[128,4096]{1,0:T(8,128)(2,1)S(1)} %get-tuple-element.43), channel_id=1, source_target_pairs={{0,32},{32,64},{64,96},{96,0},{1,33},{33,65},{65,97},{97,1},{2,34}... | collective-permute-start | bytes 3145736 | tf_op jit(solution)/shard_map/ppermute | solution.py:376
  165.3 1.0 copy-start.12
  188.0 22.0 %collective-permute-start.14 = (bf16[128,4096]{1,0:T(8,128)(2,1)S(1)}, bf16[128,4096]{1,0:T(8,128)(2,1)S(1)}, u32[]{:S(2)}, u32[]{:S(2)}) collective-permute-start(bf16[128,4096]{1,0:T(8,128)(2,1)S(1)} %get-tuple-element.50), channel_id=1, source_target_pairs={{0,96},{32,0},{64,32},{96,64},{1,97},{33,1},{65,33},{97,65},{2,98}... | collective-permute-start | bytes 3145736 | tf_op jit(solution)/shard_map/ppermute | solution.py:377
  189.8 23.3 %collective-permute-start.9 = (bf16[128,4096]{1,0:T(8,128)(2,1)S(1)}, bf16[128,4096]{1,0:T(8,128)(2,1)S(1)}, u32[]{:S(2)}, u32[]{:S(2)}) collective-permute-start(bf16[128,4096]{1,0:T(8,128)(2,1)S(1)} %add_convert_fusion.3), channel_id=1, source_target_pairs={{0,32},{32,64},{64,96},{96,0},{1,33},{33,65},{65,97},{97,1},{2,34}... | collective-permute-start | bytes 3145736 | tf_op jit(solution)/shard_map/ppermute | solution.py:376
  211.2 20.3 %collective-permute-start.16 = (bf16[128,4096]{1,0:T(8,128)(2,1)}, bf16[128,4096]{1,0:T(8,128)(2,1)}, u32[]{:S(2)}, u32[]{:S(2)}) collective-permute-start(bf16[128,4096]{1,0:T(8,128)(2,1)} %add_convert_fusion.1), channel_id=1, source_target_pairs={{0,96},{32,0},{64,32},{96,64},{1,97},{33,1},{65,33},{97,65},{2,98}... | collective-permute-start | bytes 3145736 | tf_op jit(solution)/shard_map/ppermute | solution.py:377
  213.1 21.4 %collective-permute-start.15 = (bf16[128,4096]{1,0:T(8,128)(2,1)}, bf16[128,4096]{1,0:T(8,128)(2,1)}, u32[]{:S(2)}, u32[]{:S(2)}) collective-permute-start(bf16[128,4096]{1,0:T(8,128)(2,1)} %get-tuple-element.54), channel_id=1, source_target_pairs={{0,32},{32,64},{64,96},{96,0},{1,33},{33,65},{65,97},{97,1},{2,34}... | collective-permute-start | bytes 3145736 | tf_op jit(solution)/shard_map/ppermute | solution.py:376
  214.6 22.8 %all-to-all-start.4 = ((bf16[16,8,4096]{2,1,0:T(8,128)(2,1)}), bf16[16,8,4096]{2,1,0:T(8,128)(2,1)S(1)}, u32[]{:S(2)}, u32[]{:S(2)}) async-start(bf16[16,8,4096]{2,1,0:T(8,128)(2,1)} %fusion), calls=%async_computation.4 | async-start | bytes 2097152 | tf_op jit(solution)/shard_map/all_to_all | solution.py:381
  237.4 18.7 %copy-start.11 = (f32[128,2]{0,1:T(2,128)S(1)}, f32[128,2]{0,1:T(2,128)}, u32[]{:S(2)}) copy-start(f32[128,2]{0,1:T(2,128)} %param.21) | copy-start | bytes 3076

commit v3 on v2

--- a/solution.py
+++ b/solution.py
@@ -422,7 +422,7 @@
         2 * heads * HEAD * HEAD,
         8,
     )
-    totals = [to_later(total, k) for k in range(1, chips)]
+    totals = [to_later(total, k) for k in range(chips - 1, 0, -1)][::-1]
     (carried,) = whole_call(
         carry_kernel,
         [shape((heads, HEAD, HEAD), BF16)],
@@ -476,14 +476,12 @@
     to_left_b = plus(out_left_b, pass_b)
     back_b = go_back(to_left_b)
     home = lambda *terms: plus(*terms).reshape(experts, rows, width)
-    returned = [
-        exchange(after(home(out_own_a, ahead_a, back_a), to_left_b), "seq"),
-        exchange(home(out_own_b, ahead_b, back_b), "seq"),
-    ]
+    returned_a = exchange(after(home(out_own_a, ahead_a, back_a), to_left_b), "seq")
+    returned_b = exchange(home(after(out_own_b, returned_a), ahead_b, back_b), "seq")
     (out,) = whole_call(
         mix_kernel,
         [shape((tokens, width), BF16)],
-        [stream, index, router_weight.T, *returned],
+        [stream, index, router_weight.T, returned_a, returned_b],
         4 * tokens * width * count * chunks,
         16,
     )

time: 259 us -> 255 us (0.985)
  blocking collectives: 60 us -> 76.4 us
  waiting for transfers between devices: 85 us -> 74.5 us
  starting transfers between devices: 43.4 us -> 38.4 us
  other arithmetic: 5.9 us -> 1.43 us
    all_to_all x3 -> x4, blocking collectives: 60 us -> 76.4 us  [body(): lax.all_to_all(a, axis, split_axis=0, concat_axis=0, tiled=True)]
    ppermute x6, waiting for transfers between devices: 31.4 us -> 20.8 us  [body(): lax.ppermute(a, 'x', [(i, (i - 1) % chips) for i in range(chips)])]
    all_to_all x3 -> x2, starting transfers between devices: 17.2 us -> 12.2 us  [body(): lax.all_to_all(a, axis, split_axis=0, concat_axis=0, tiled=True)]
    reshape x2, other arithmetic: 4.43 us -> 0.94 us  [body(): home = lambda *terms: plus(*terms).reshape(experts, rows, width)]
    all_to_all x3 -> x2, waiting for transfers between devices: 9.37 us -> 9.37 us  [body(): lax.all_to_all(a, axis, split_axis=0, concat_axis=0, tiled=True)]
  transfers between devices with their start and end apart: 20 -> 19, of which waited for: 8 -> 8; matrix products, arithmetic and copies ran while one was open for 2% -> 0% of each run, Pallas kernels for 19% -> 18%
where the time goes in v3:
time: 255 us; the launch traced here: 254 us
  blocking collectives  76.4 us (30%)
  waiting for transfers between devices  74.5 us (29%)
  Pallas kernels  58.5 us (23%)
  starting transfers between devices  38.4 us (15%)
  local copies, waits for them, and re-layouts  4.68 us (2%)
    all_to_all x4, blocking collectives, body(): lax.all_to_all(a, axis, split_axis=0, concat_axis=0, tiled=True)  76.4 us
    ppermute x6, waiting for transfers between devices, body(): lax.ppermute(a, 'x', [(i, (i + 1) % chips) for i in range(chips)])  42.4 us
    pallas_call x2, Pallas kernels, expert_rows(): pl.pallas_call(expert_kernel, in_specs=vmem(len(blocks)) + in_place, out_...  41.9 us
    ppermute x6, waiting for transfers between devices, body(): lax.ppermute(a, 'x', [(i, (i - 1) % chips) for i in range(chips)])  20.8 us
    pallas_call x6, Pallas kernels, whole_call(): pl.pallas_call(kernel, out_shape=outs, in_specs=[pl.BlockSpec(memory_spac...  16.6 us
    ppermute x6, starting transfers between devices, body(): lax.ppermute(a, 'x', [(i, (i - 1) % chips) for i in range(chips)])  13.3 us
    all_to_all x2, starting transfers between devices, body(): lax.all_to_all(a, axis, split_axis=0, concat_axis=0, tiled=True)  12.2 us
    all_to_all x2, waiting for transfers between devices, body(): lax.all_to_all(a, axis, split_axis=0, concat_axis=0, tiled=True)  9.37 us
  transfers between devices with their start and end apart: 19, of which 8 were waited for; matrix products, arithmetic and copies ran while one was open for 0% of the time, Pallas kernels for 18%

profile of v3, /device:TPU:0, one launch (start us, length us, event | category | flops | bytes accessed | tf_op | source)
XLA Modules:
  0.0 254.2 jit_solution(7207211767604906224)
XLA Ops:
  0.0 4.9 %shard_map.118 = (bf16[32,136,128]{2,1,0:T(8,128)(2,1)}, f32[32,128]{1,0:T(8,128)}, f32[128,32]{1,0:T(8,128)}) custom-call(f32[32,128]{1,0:T(8,128)} %bitcast.26, bf16[128,4096]{1,0:T(8,128)(2,1)} %key_ref.1, bf16[128,4096]{1,0:T(8,128)(2,1)} %value_ref.1), custom_call_target="tpu_custom_call" | custom-call | flops 134217728 | bytes 3260416 | tf_op jit(solution)/shard_map/pallas_call | solution.py:25
  4.9 0.0 copy-start.6
  4.9 8.6 %all-to-all-start = ((bf16[32,136,128]{2,1,0:T(8,128)(2,1)}), bf16[32,136,128]{2,1,0:T(8,128)(2,1)S(1)}, u32[]{:S(2)}, u32[]{:S(2)}) async-start(bf16[32,136,128]{2,1,0:T(8,128)(2,1)} %get-tuple-element.33), calls=%async_computation | async-start | bytes 2228224 | tf_op jit(solution)/shard_map/all_to_all | solution.py:381
  13.5 0.0 copy-start
  13.5 1.2 copy-done
  14.7 1.2 copy-done.1
  16.0 1.2 copy-done.2
  17.2 5.1 %shard_map.119.local_ref = f32[128,4096]{1,0:T(8,128)S(1)} custom-call(bf16[128,4096]{1,0:T(8,128)(2,1)S(1)} %copy-done.2, bf16[128,4096]{1,0:T(8,128)(2,1)S(1)} %copy-done, bf16[128,4096]{1,0:T(8,128)(2,1)S(1)} %copy-done.1, f32[32,128]{1,0:T(8,128)S(1)} %copy-done.9, f32[128,32]{1,0:T(8,128)S(1)} %copy-done.6), custom_call_target="tpu_custom_call" | custom-call | flops 268435456 | bytes 5275648 | tf_op jit(solution)/shard_map/pallas_call | solution.py:25
  22.3 9.4 %all-to-all-done.arrived_ref = bf16[32,136,128]{2,1,0:T(8,128)(2,1)S(1)} async-done(((bf16[32,136,128]{2,1,0:T(8,128)(2,1)}), bf16[32,136,128]{2,1,0:T(8,128)(2,1)S(1)}, u32[]{:S(2)}, u32[]{:S(2)}) %all-to-all-start) | async-done | bytes 1114144 | tf_op jit(solution)/shard_map/all_to_all | solution.py:381
  31.6 0.3 shard_map.120
  31.9 3.4 %collective-permute-start = (f32[136,128]{1,0:T(8,128)S(1)}, f32[136,128]{1,0:T(8,128)S(1)}, u32[]{:S(2)}, u32[]{:S(2)}) collective-permute-start(f32[136,128]{1,0:T(8,128)S(1)} %get-tuple-element.37), channel_id=1, source_target_pairs={{0,32},{32,64},{64,96},{1,33},{33,65},{65,97},{2,34},{34,66},{66,9... | collective-permute-start | bytes 208904 | tf_op jit(solution)/shard_map/ppermute | solution.py:378
  35.3 4.6 %collective-permute-start.1 = (f32[136,128]{1,0:T(8,128)S(1)}, f32[136,128]{1,0:T(8,128)S(1)}, u32[]{:S(2)}, u32[]{:S(2)}) collective-permute-start(f32[136,128]{1,0:T(8,128)S(1)} %get-tuple-element.37), channel_id=1, source_target_pairs={{0,64},{32,96},{1,65},{33,97},{2,66},{34,98},{3,67},{35,99},{4,68}... | collective-permute-start | bytes 208904 | tf_op jit(solution)/shard_map/ppermute | solution.py:378
  40.0 1.3 collective-permute-start.2
  41.3 0.6 collective-permute-done.1.rest_1_
  41.9 1.3 collective-permute-done.2.rest_2_
  43.2 0.0 copy-start.10
  43.2 0.2 shard_map.121
  43.5 20.9 %all_to_all.30.carried_ref = bf16[32,128,128]{2,1,0:T(8,128)(2,1)S(1)} all-to-all(bf16[32,128,128]{2,1,0:T(8,128)(2,1)S(1)} %shard_map.121), channel_id=1, replica_groups=mesh['x'=4,'core'=2,'seq'=16] {'core','seq'}, dimensions={0} | all-to-all | bytes 2097152 | tf_op jit(solution)/shard_map/all_to_all | solution.py:381
  64.4 3.7 %shard_map.122 = (bf16[128,4096]{1,0:T(8,128)(2,1)S(1)}, bf16[16,8,4096]{2,1,0:T(8,128)(2,1)S(1)}, bf16[16,8,4096]{2,1,0:T(8,128)(2,1)}) custom-call(bf16[128,4096]{1,0:T(8,128)(2,1)S(1)} %copy-done.3, f32[128,4096]{1,0:T(8,128)S(1)} %shard_map.119.local_ref, bf16[128,4096]{1,0:T(8,128)(2,1)S(1)} %copy-done.4, bf16[128,4096]{1,0:T(8,128)(2,1)S(1)} %copy-done.5, ...), custom_call_target="tpu_custom_call" | custom-call | flops 402653184 | bytes 9487360 | tf_op jit(solution)/shard_map/pallas_call | solution.py:25
  68.1 0.5 collective-permute-start.7
  68.6 20.4 %all_to_all.31 = bf16[16,8,4096]{2,1,0:T(8,128)(2,1)S(1)} all-to-all(bf16[16,8,4096]{2,1,0:T(8,128)(2,1)S(1)} %get-tuple-element.39), channel_id=1, replica_groups=mesh['x'=4,'core'=2,'seq'=16] {'seq'}, dimensions={0} | all-to-all | bytes 2097152 | tf_op jit(solution)/shard_map/all_to_all | solution.py:381
  89.0 3.6 %collective-permute-start.4 = (bf16[128,4096]{1,0:T(8,128)(2,1)S(1)}, bf16[128,4096]{1,0:T(8,128)(2,1)}, u32[]{:S(2)}, u32[]{:S(2)}) collective-permute-start(bf16[128,4096]{1,0:T(8,128)(2,1)S(1)} %bitcast.19), channel_id=1, source_target_pairs={{0,96},{32,0},{64,32},{96,64},{1,97},{33,1},{65,33},{97,65},{2,98}... | collective-permute-start | bytes 3145736 | tf_op jit(solution)/shard_map/ppermute | solution.py:377
  92.6 3.7 %all-to-all-start.3 = ((bf16[16,8,4096]{2,1,0:T(8,128)(2,1)}), bf16[16,8,4096]{2,1,0:T(8,128)(2,1)S(1)}, u32[]{:S(2)}, u32[]{:S(2)}) async-start(bf16[16,8,4096]{2,1,0:T(8,128)(2,1)} %get-tuple-element.46), calls=%async_computation.3 | async-start | bytes 2097152 | tf_op jit(solution)/shard_map/all_to_all | solution.py:381
  96.2 18.2 %collective-permute-done.3.left_ref = bf16[128,4096]{1,0:T(8,128)(2,1)} collective-permute-done((bf16[128,4096]{1,0:T(8,128)(2,1)S(1)}, bf16[128,4096]{1,0:T(8,128)(2,1)}, u32[]{:S(2)}, u32[]{:S(2)}) %collective-permute-start.3) | collective-permute-done | bytes 1048608 | tf_op jit(solution)/shard_map/ppermute | solution.py:376
  114.4 3.2 %collective-permute-start.12 = (bf16[128,4096]{1,0:T(8,128)(2,1)S(1)}, bf16[128,4096]{1,0:T(8,128)(2,1)S(1)}, u32[]{:S(2)}, u32[]{:S(2)}) collective-permute-start(bf16[128,4096]{1,0:T(8,128)(2,1)S(1)} %bitcast.15), channel_id=1, source_target_pairs={{0,96},{32,0},{64,32},{96,64},{1,97},{33,1},{65,33},{97,65},{2,98}... | collective-permute-start | bytes 3145736 | tf_op jit(solution)/shard_map/ppermute | solution.py:377
  117.6 21.1 %collective-permute-done.5.far_ref = bf16[128,4096]{1,0:T(8,128)(2,1)} collective-permute-done((bf16[128,4096]{1,0:T(8,128)(2,1)}, bf16[128,4096]{1,0:T(8,128)(2,1)}, u32[]{:S(2)}, u32[]{:S(2)}) %collective-permute-start.5) | collective-permute-done | bytes 1048608 | tf_op jit(solution)/shard_map/ppermute | solution.py:376
  138.8 3.2 %collective-permute-start.13 = (bf16[128,4096]{1,0:T(8,128)(2,1)S(1)}, bf16[128,4096]{1,0:T(8,128)(2,1)S(1)}, u32[]{:S(2)}, u32[]{:S(2)}) collective-permute-start(bf16[128,4096]{1,0:T(8,128)(2,1)S(1)} %collective-permute-done.12.right_ref), channel_id=1, source_target_pairs={{0,96},{32,0},{64,32},{96,64},{1,97},{33,1},{65,33},{97,65},{2,98}... | collective-permute-start | bytes 3145736 | tf_op jit(solution)/shard_map/ppermute | solution.py:377
  142.0 21.2 %shard_map.123 = (bf16[128,4096]{1,0:T(8,128)(2,1)S(1)}, bf16[128,4096]{1,0:T(8,128)(2,1)S(1)}, bf16[128,4096]{1,0:T(8,128)(2,1)S(1)}, bf16[128,4096]{1,0:T(8,128)(2,1)S(1)}) custom-call(bf16[128,4096]{1,0:T(8,128)(2,1)S(1)} %bitcast.20, bf16[128,4096]{1,0:T(8,128)(2,1)} %collective-permute-done.3.left_ref, ...), custom_call_target="tpu_custom_call" | custom-call | flops 14495514624 | bytes 36700160 | tf_op jit(solution)/shard_map/pallas_call | solution.py:330
  163.2 0.1 collective-permute-start.10
  163.3 2.0 collective-permute-start.8
  165.3 1.0 copy-done.12
  166.3 20.7 %shard_map.124 = (bf16[128,4096]{1,0:T(8,128)(2,1)S(1)}, bf16[128,4096]{1,0:T(8,128)(2,1)S(1)}, bf16[128,4096]{1,0:T(8,128)(2,1)S(1)}, bf16[128,4096]{1,0:T(8,128)(2,1)S(1)}) custom-call(bf16[128,4096]{1,0:T(8,128)(2,1)S(1)} %bitcast.17, bf16[128,4096]{1,0:T(8,128)(2,1)S(1)} %collective-permute-done.11.left_ref, ...), custom_call_target="tpu_custom_call" | custom-call | flops 14495514624 | bytes 36700160 | tf_op jit(solution)/shard_map/pallas_call | solution.py:330
  187.0 1.6 collective-permute-start.14
  188.6 0.2 add_convert_fusion.3
  188.9 0.6 collective-permute-start.9
  189.4 20.7 %collective-permute-done.14 = bf16[128,4096]{1,0:T(8,128)(2,1)S(1)} collective-permute-done((bf16[128,4096]{1,0:T(8,128)(2,1)S(1)}, bf16[128,4096]{1,0:T(8,128)(2,1)S(1)}, u32[]{:S(2)}, u32[]{:S(2)}) %collective-permute-start.14) | collective-permute-done | bytes 1048608 | tf_op jit(solution)/shard_map/ppermute | solution.py:377
  210.1 0.2 add_convert_fusion.1
  210.3 1.6 collective-permute-start.16
  211.9 0.0 collective-permute-done.9
  212.0 0.5 collective-permute-start.15
  212.4 0.5 fusion
  212.9 17.3 %all_to_all.32.rest_0_ = bf16[16,8,4096]{2,1,0:T(8,128)(2,1)S(1)} all-to-all(bf16[16,8,4096]{2,1,0:T(8,128)(2,1)S(1)} %fusion), channel_id=1, replica_groups=mesh['x'=4,'core'=2,'seq'=16] {'seq'}, dimensions={0} | all-to-all | bytes 2097152 | tf_op jit(solution)/shard_map/all_to_all | solution.py:381
  230.2 0.1 collective-permute-done.16
  230.3 3.0 %collective-permute-done.15 = bf16[128,4096]{1,0:T(8,128)(2,1)S(1)} collective-permute-done((bf16[128,4096]{1,0:T(8,128)(2,1)S(1)}, bf16[128,4096]{1,0:T(8,128)(2,1)S(1)}, u32[]{:S(2)}, u32[]{:S(2)}) %collective-permute-start.15) | collective-permute-done | bytes 1048608 | tf_op jit(solution)/shard_map/ppermute | solution.py:376
  233.4 0.5 fusion.1
  233.9 0.0 copy-start.11
  233.9 17.9 %all_to_all.33.rest_1_ = bf16[16,8,4096]{2,1,0:T(8,128)(2,1)S(1)} all-to-all(bf16[16,8,4096]{2,1,0:T(8,128)(2,1)S(1)} %fusion.1), channel_id=1, replica_groups=mesh['x'=4,'core'=2,'seq'=16] {'seq'}, dimensions={0} | all-to-all | bytes 2097152 | tf_op jit(solution)/shard_map/all_to_all | solution.py:381
  251.8 2.4 shard_map.125
  (32 shorter events, 0.1 us)
Async XLA Ops:
  4.9 8.6 %copy-start.6 = (f32[128,32]{1,0:T(8,128)S(1)}, f32[128,32]{1,0:T(8,128)}, u32[]{:S(2)}) copy-start(f32[128,32]{1,0:T(8,128)} %get-tuple-element.32.by_token_ref) | copy-start | bytes 49156
  4.9 8.6 %copy-start.9 = (f32[32,128]{1,0:T(8,128)S(1)}, f32[32,128]{1,0:T(8,128)}, u32[]{:S(2)}) copy-start(f32[32,128]{1,0:T(8,128)} %get-tuple-element.31.by_head_ref) | copy-start | bytes 49156
  4.9 26.7 %all-to-all-start = ((bf16[32,136,128]{2,1,0:T(8,128)(2,1)}), bf16[32,136,128]{2,1,0:T(8,128)(2,1)S(1)}, u32[]{:S(2)}, u32[]{:S(2)}) async-start(bf16[32,136,128]{2,1,0:T(8,128)(2,1)} %get-tuple-element.33), calls=%async_computation | async-start | bytes 2228224 | tf_op jit(solution)/shard_map/all_to_all | solution.py:381
  13.5 1.2 copy-start
  14.7 1.2 copy-start.1
  16.0 1.2 copy-start.2
  31.9 9.4 %collective-permute-start = (f32[136,128]{1,0:T(8,128)S(1)}, f32[136,128]{1,0:T(8,128)S(1)}, u32[]{:S(2)}, u32[]{:S(2)}) collective-permute-start(f32[136,128]{1,0:T(8,128)S(1)} %get-tuple-element.37), channel_id=1, source_target_pairs={{0,32},{32,64},{64,96},{1,33},{33,65},{65,97},{2,34},{34,66},{66,9... | collective-permute-start | bytes 208904 | tf_op jit(solution)/shard_map/ppermute | solution.py:378
  35.3 6.6 %collective-permute-start.1 = (f32[136,128]{1,0:T(8,128)S(1)}, f32[136,128]{1,0:T(8,128)S(1)}, u32[]{:S(2)}, u32[]{:S(2)}) collective-permute-start(f32[136,128]{1,0:T(8,128)S(1)} %get-tuple-element.37), channel_id=1, source_target_pairs={{0,64},{32,96},{1,65},{33,97},{2,66},{34,98},{3,67},{35,99},{4,68}... | collective-permute-start | bytes 208904 | tf_op jit(solution)/shard_map/ppermute | solution.py:378
  40.0 3.2 %collective-permute-start.2 = (f32[136,128]{1,0:T(8,128)S(1)}, f32[136,128]{1,0:T(8,128)S(1)}, u32[]{:S(2)}, u32[]{:S(2)}) collective-permute-start(f32[136,128]{1,0:T(8,128)S(1)} %get-tuple-element.37), channel_id=1, source_target_pairs={{0,96},{1,97},{2,98},{3,99},{4,100},{5,101},{6,102},{7,103},{8,104... | collective-permute-start | bytes 208904 | tf_op jit(solution)/shard_map/ppermute | solution.py:378
  43.2 21.1 %copy-start.3 = (bf16[128,4096]{1,0:T(8,128)(2,1)S(1)}, bf16[128,4096]{1,0:T(8,128)(2,1)}, u32[]{:S(2)}) copy-start(bf16[128,4096]{1,0:T(8,128)(2,1)} %query_ref.3) | copy-start | bytes 3145732
  43.2 21.1 %copy-start.4 = (bf16[128,4096]{1,0:T(8,128)(2,1)S(1)}, bf16[128,4096]{1,0:T(8,128)(2,1)}, u32[]{:S(2)}) copy-start(bf16[128,4096]{1,0:T(8,128)(2,1)} %gate_ref.1) | copy-start | bytes 3145732
  43.2 21.1 %copy-start.5 = (bf16[128,4096]{1,0:T(8,128)(2,1)S(1)}, bf16[128,4096]{1,0:T(8,128)(2,1)}, u32[]{:S(2)}) copy-start(bf16[128,4096]{1,0:T(8,128)(2,1)} %residual_ref.1) | copy-start | bytes 3145732
  43.2 21.2 %copy-start.7 = (f32[4096]{0:T(1024)S(1)}, f32[4096]{0:T(1024)}, u32[]{:S(2)}) copy-start(f32[4096]{0:T(1024)} %param.18) | copy-start | bytes 49156
  43.2 21.2 %copy-start.8 = (f32[4096]{0:T(1024)S(1)}, f32[4096]{0:T(1024)}, u32[]{:S(2)}) copy-start(f32[4096]{0:T(1024)} %param.19) | copy-start | bytes 49156
  43.2 21.2 %copy-start.10 = (s32[128,2]{0,1:T(2,128)S(1)}, s32[128,2]{0,1:T(2,128)}, u32[]{:S(2)}) copy-start(s32[128,2]{0,1:T(2,128)} %param.20) | copy-start | bytes 3076
  68.1 73.9 %collective-permute-start.6 = (bf16[2,576,4096]{2,1,0:T(8,128)(2,1)}, bf16[2,576,4096]{2,1,0:T(8,128)(2,1)}, u32[]{:S(2)}, u32[]{:S(2)}) collective-permute-start(bf16[2,576,4096]{2,1,0:T(8,128)(2,1)} %bitcast.27), channel_id=1, source_target_pairs={{0,16},{16,0},{1,17},{17,1},{2,18},{18,2},{3,19},{19,3},{4,20},{20... | collective-permute-start | bytes 28311560 | tf_op jit(solution)/shard_map/ppermute | solution.py:375
  68.1 73.9 %collective-permute-start.7 = (bf16[576,4096]{1,0:T(8,128)(2,1)}, bf16[576,4096]{1,0:T(8,128)(2,1)}, u32[]{:S(2)}, u32[]{:S(2)}) collective-permute-start(bf16[576,4096]{1,0:T(8,128)(2,1)} %bitcast.30), channel_id=1, source_target_pairs={{0,16},{16,0},{1,17},{17,1},{2,18},{18,2},{3,19},{19,3},{4,20},{20... | collective-permute-start | bytes 14155784 | tf_op jit(solution)/shard_map/ppermute | solution.py:375
  89.0 25.4 %collective-permute-start.3 = (bf16[128,4096]{1,0:T(8,128)(2,1)S(1)}, bf16[128,4096]{1,0:T(8,128)(2,1)}, u32[]{:S(2)}, u32[]{:S(2)}) collective-permute-start(bf16[128,4096]{1,0:T(8,128)(2,1)S(1)} %bitcast.18), channel_id=1, source_target_pairs={{0,32},{32,64},{64,96},{96,0},{1,33},{33,65},{65,97},{97,1},{2,34}... | collective-permute-start | bytes 3145736 | tf_op jit(solution)/shard_map/ppermute | solution.py:376
  89.0 25.4 %collective-permute-start.4 = (bf16[128,4096]{1,0:T(8,128)(2,1)S(1)}, bf16[128,4096]{1,0:T(8,128)(2,1)}, u32[]{:S(2)}, u32[]{:S(2)}) collective-permute-start(bf16[128,4096]{1,0:T(8,128)(2,1)S(1)} %bitcast.19), channel_id=1, source_target_pairs={{0,96},{32,0},{64,32},{96,64},{1,97},{33,1},{65,33},{97,65},{2,98}... | collective-permute-start | bytes 3145736 | tf_op jit(solution)/shard_map/ppermute | solution.py:377
  92.6 21.8 %all-to-all-start.3 = ((bf16[16,8,4096]{2,1,0:T(8,128)(2,1)}), bf16[16,8,4096]{2,1,0:T(8,128)(2,1)S(1)}, u32[]{:S(2)}, u32[]{:S(2)}) async-start(bf16[16,8,4096]{2,1,0:T(8,128)(2,1)} %get-tuple-element.46), calls=%async_computation.3 | async-start | bytes 2097152 | tf_op jit(solution)/shard_map/all_to_all | solution.py:381
  114.4 24.4 %collective-permute-start.5 = (bf16[128,4096]{1,0:T(8,128)(2,1)}, bf16[128,4096]{1,0:T(8,128)(2,1)}, u32[]{:S(2)}, u32[]{:S(2)}) collective-permute-start(bf16[128,4096]{1,0:T(8,128)(2,1)} %collective-permute-done.3.left_ref), channel_id=1, source_target_pairs={{0,32},{32,64},{64,96},{96,0},{1,33},{33,65},{65,97},{97,1},{2,34}... | collective-permute-start | bytes 3145736 | tf_op jit(solution)/shard_map/ppermute | solution.py:376
  114.4 24.4 %collective-permute-start.12 = (bf16[128,4096]{1,0:T(8,128)(2,1)S(1)}, bf16[128,4096]{1,0:T(8,128)(2,1)S(1)}, u32[]{:S(2)}, u32[]{:S(2)}) collective-permute-start(bf16[128,4096]{1,0:T(8,128)(2,1)S(1)} %bitcast.15), channel_id=1, source_target_pairs={{0,96},{32,0},{64,32},{96,64},{1,97},{33,1},{65,33},{97,65},{2,98}... | collective-permute-start | bytes 3145736 | tf_op jit(solution)/shard_map/ppermute | solution.py:377
  138.7 26.6 %collective-permute-start.11 = (bf16[128,4096]{1,0:T(8,128)(2,1)S(1)}, bf16[128,4096]{1,0:T(8,128)(2,1)S(1)}, u32[]{:S(2)}, u32[]{:S(2)}) collective-permute-start(bf16[128,4096]{1,0:T(8,128)(2,1)S(1)} %bitcast.16), channel_id=1, source_target_pairs={{0,32},{32,64},{64,96},{96,0},{1,33},{33,65},{65,97},{97,1},{2,34}... | collective-permute-start | bytes 3145736 | tf_op jit(solution)/shard_map/ppermute | solution.py:376
  138.8 26.6 %collective-permute-start.13 = (bf16[128,4096]{1,0:T(8,128)(2,1)S(1)}, bf16[128,4096]{1,0:T(8,128)(2,1)S(1)}, u32[]{:S(2)}, u32[]{:S(2)}) collective-permute-start(bf16[128,4096]{1,0:T(8,128)(2,1)S(1)} %collective-permute-done.12.right_ref), channel_id=1, source_target_pairs={{0,96},{32,0},{64,32},{96,64},{1,97},{33,1},{65,33},{97,65},{2,98}... | collective-permute-start | bytes 3145736 | tf_op jit(solution)/shard_map/ppermute | solution.py:377
  163.2 23.8 %collective-permute-start.10 = (bf16[128,4096]{1,0:T(8,128)(2,1)S(1)}, bf16[128,4096]{1,0:T(8,128)(2,1)S(1)}, u32[]{:S(2)}, u32[]{:S(2)}) collective-permute-start(bf16[128,4096]{1,0:T(8,128)(2,1)S(1)} %get-tuple-element.45), channel_id=1, source_target_pairs={{0,96},{32,0},{64,32},{96,64},{1,97},{33,1},{65,33},{97,65},{2,98}... | collective-permute-start | bytes 3145736 | tf_op jit(solution)/shard_map/ppermute | solution.py:377
  163.3 23.7 %collective-permute-start.8 = (bf16[128,4096]{1,0:T(8,128)(2,1)S(1)}, bf16[128,4096]{1,0:T(8,128)(2,1)S(1)}, u32[]{:S(2)}, u32[]{:S(2)}) collective-permute-start(bf16[128,4096]{1,0:T(8,128)(2,1)S(1)} %get-tuple-element.44), channel_id=1, source_target_pairs={{0,32},{32,64},{64,96},{96,0},{1,33},{33,65},{65,97},{97,1},{2,34}... | collective-permute-start | bytes 3145736 | tf_op jit(solution)/shard_map/ppermute | solution.py:376
  165.3 1.0 copy-start.12
  187.0 23.1 %collective-permute-start.14 = (bf16[128,4096]{1,0:T(8,128)(2,1)S(1)}, bf16[128,4096]{1,0:T(8,128)(2,1)S(1)}, u32[]{:S(2)}, u32[]{:S(2)}) collective-permute-start(bf16[128,4096]{1,0:T(8,128)(2,1)S(1)} %get-tuple-element.51), channel_id=1, source_target_pairs={{0,96},{32,0},{64,32},{96,64},{1,97},{33,1},{65,33},{97,65},{2,98}... | collective-permute-start | bytes 3145736 | tf_op jit(solution)/shard_map/ppermute | solution.py:377
  188.9 23.1 %collective-permute-start.9 = (bf16[128,4096]{1,0:T(8,128)(2,1)S(1)}, bf16[128,4096]{1,0:T(8,128)(2,1)S(1)}, u32[]{:S(2)}, u32[]{:S(2)}) collective-permute-start(bf16[128,4096]{1,0:T(8,128)(2,1)S(1)} %add_convert_fusion.3), channel_id=1, source_target_pairs={{0,32},{32,64},{64,96},{96,0},{1,33},{33,65},{65,97},{97,1},{2,34}... | collective-permute-start | bytes 3145736 | tf_op jit(solution)/shard_map/ppermute | solution.py:376
  210.3 20.0 %collective-permute-start.16 = (bf16[128,4096]{1,0:T(8,128)(2,1)S(1)}, bf16[128,4096]{1,0:T(8,128)(2,1)S(1)}, u32[]{:S(2)}, u32[]{:S(2)}) collective-permute-start(bf16[128,4096]{1,0:T(8,128)(2,1)S(1)} %add_convert_fusion.1), channel_id=1, source_target_pairs={{0,96},{32,0},{64,32},{96,64},{1,97},{33,1},{65,33},{97,65},{2,98}... | collective-permute-start | bytes 3145736 | tf_op jit(solution)/shard_map/ppermute | solution.py:377
  212.0 21.4 %collective-permute-start.15 = (bf16[128,4096]{1,0:T(8,128)(2,1)S(1)}, bf16[128,4096]{1,0:T(8,128)(2,1)S(1)}, u32[]{:S(2)}, u32[]{:S(2)}) collective-permute-start(bf16[128,4096]{1,0:T(8,128)(2,1)S(1)} %get-tuple-element.56), channel_id=1, source_target_pairs={{0,32},{32,64},{64,96},{96,0},{1,33},{33,65},{65,97},{97,1},{2,34}... | collective-permute-start | bytes 3145736 | tf_op jit(solution)/shard_map/ppermute | solution.py:376
  233.9 17.9 %copy-start.11 = (f32[128,2]{0,1:T(2,128)S(1)}, f32[128,2]{0,1:T(2,128)}, u32[]{:S(2)}) copy-start(f32[128,2]{0,1:T(2,128)} %param.21) | copy-start | bytes 3076

commit v4 on v3

--- a/solution.py
+++ b/solution.py
@@ -117,11 +117,12 @@
     total_ref[HEAD:, :] = kept
 
 
-def carry_kernel(within_ref, kept_ref, *rest):
+def carry_kernel(within_ref, kept_ref, earlier_ref, *rest):
     *total_refs, carried_ref = rest
     before = jnp.zeros((HEAD, HEAD), F32)
-    for total_ref in reversed(total_refs):
-        before = total_ref[:HEAD, :] + total_ref[HEAD : HEAD + 1, :] * before
+    for place, total_ref in reversed(list(enumerate(total_refs))):
+        longer = total_ref[:HEAD, :] + total_ref[HEAD : HEAD + 1, :] * before
+        before = jnp.where(earlier_ref[place : place + 1, :] > 0.0, longer, before)
 
     def step(block, _):
         carried = within_ref[block] + kept_ref[block, 0:1, :] * before
@@ -375,7 +376,7 @@
     swap = lambda a: lax.ppermute(a, "core", [(0, 1), (1, 0)])
     go_ahead = lambda a: lax.ppermute(a, "x", [(i, (i + 1) % chips) for i in range(chips)])
     go_back = lambda a: lax.ppermute(a, "x", [(i, (i - 1) % chips) for i in range(chips)])
-    to_later = lambda a, k: lax.ppermute(a, "x", [(i, i + k) for i in range(chips - k)])
+    to_later = lambda a, k: lax.ppermute(a, "x", [(i, (i + k) % chips) for i in range(chips)])
     plane = ("core", "seq")
     after = lambda value, *earlier: lax.optimization_barrier((value, earlier))[0]
     exchange = lambda a, axis: lax.all_to_all(a, axis, split_axis=0, concat_axis=0, tiled=True)
@@ -422,11 +423,13 @@
         2 * heads * HEAD * HEAD,
         8,
     )
-    totals = [to_later(total, k) for k in range(chips - 1, 0, -1)][::-1]
+    distance = lax.broadcasted_iota(jnp.int32, (chips - 1, HEAD), 0) + 1
+    earlier = (distance <= lax.axis_index("x")).astype(F32)
+    totals = [to_later(total, k) for k in range(1, chips)]
     (carried,) = whole_call(
         carry_kernel,
         [shape((heads, HEAD, HEAD), BF16)],
-        [within, kept, *totals],
+        [within, kept, earlier, *totals],
         2 * heads * HEAD * HEAD,
         8,
     )
@@ -459,8 +462,8 @@
 
     own_a, own_b = (exchange(bin_rows, "seq").reshape(count, width) for bin_rows in bins)
     left_a, right_a = (go_ahead(own_a), go_back(own_a))
-    far_a = go_ahead(left_a)
-    right_b = go_back(after(own_b, right_a))
+    far_a = go_ahead(after(left_a, own_b))
+    right_b = go_back(after(own_b, right_a, down_other))
     left_b = go_ahead(after(own_b, far_a))
     far_b = go_back(right_b)
     out_own_a, out_left_a, out_right_a, out_far_a = expert_rows(

time: 255 us -> 250 us (0.980)
  blocking collectives: 76.4 us -> 95.9 us
  waiting for transfers between devices: 74.5 us -> 59.2 us
  starting transfers between devices: 38.4 us -> 30.9 us
    all_to_all x4 -> x5, blocking collectives: 76.4 us -> 95.9 us  [body(): lax.all_to_all(a, axis, split_axis=0, concat_axis=0, tiled=True)]
    ppermute x6, waiting for transfers between devices: 42.4 us -> 26.3 us  [body(): lax.ppermute(a, 'x', [(i, (i + 1) % chips) for i in range(chips)])]
    all_to_all x2 -> x1, starting transfers between devices: 12.2 us -> 8.56 us  [body(): lax.all_to_all(a, axis, split_axis=0, concat_axis=0, tiled=True)]
    ppermute x3, starting transfers between devices: 9.33 us -> 5.72 us  [body(): lax.ppermute(a, 'x', [(i, (i + k) % chips) for i in range(chips)])]
    all_to_all x2 -> x1, waiting for transfers between devices: 9.37 us -> 9.37 us  [body(): lax.all_to_all(a, axis, split_axis=0, concat_axis=0, tiled=True)]
  transfers between devices with their start and end apart: 19 -> 18, of which waited for: 8 -> 8; matrix products, arithmetic and copies ran while one was open for 0% -> 0% of each run, Pallas kernels for 18% -> 19%
where the time goes in v4:
time: 250 us; the launch traced here: 249 us
  blocking collectives  95.9 us (38%)
  waiting for transfers between devices  59.2 us (24%)
  Pallas kernels  57.1 us (23%)
  starting transfers between devices  30.9 us (12%)
  local copies, waits for them, and re-layouts  4.75 us (2%)
    all_to_all x5, blocking collectives, body(): lax.all_to_all(a, axis, split_axis=0, concat_axis=0, tiled=True)  95.9 us
    pallas_call x2, Pallas kernels, expert_rows(): pl.pallas_call(expert_kernel, in_specs=vmem(len(blocks)) + in_place, out_...  41.4 us
    ppermute x6, waiting for transfers between devices, body(): lax.ppermute(a, 'x', [(i, (i + 1) % chips) for i in range(chips)])  26.3 us
    ppermute x6, waiting for transfers between devices, body(): lax.ppermute(a, 'x', [(i, (i - 1) % chips) for i in range(chips)])  20.6 us
    pallas_call x6, Pallas kernels, whole_call(): pl.pallas_call(kernel, out_shape=outs, in_specs=[pl.BlockSpec(memory_spac...  15.7 us
    ppermute x6, starting transfers between devices, body(): lax.ppermute(a, 'x', [(i, (i - 1) % chips) for i in range(chips)])  12.3 us
    all_to_all x1, waiting for transfers between devices, body(): lax.all_to_all(a, axis, split_axis=0, concat_axis=0, tiled=True)  9.37 us
    all_to_all x1, starting transfers between devices, body(): lax.all_to_all(a, axis, split_axis=0, concat_axis=0, tiled=True)  8.56 us
  transfers between devices with their start and end apart: 18, of which 8 were waited for; matrix products, arithmetic and copies ran while one was open for 0% of the time, Pallas kernels for 19%

profile of v4, /device:TPU:0, one launch (start us, length us, event | category | flops | bytes accessed | tf_op | source)
XLA Modules:
  0.0 249.4 jit_solution(6583387777997778256)
XLA Ops:
  0.0 4.9 %shard_map.118 = (bf16[32,136,128]{2,1,0:T(8,128)(2,1)}, f32[32,128]{1,0:T(8,128)}, f32[128,32]{1,0:T(8,128)}) custom-call(f32[32,128]{1,0:T(8,128)} %bitcast.26, bf16[128,4096]{1,0:T(8,128)(2,1)} %key_ref.1, bf16[128,4096]{1,0:T(8,128)(2,1)} %value_ref.1), custom_call_target="tpu_custom_call" | custom-call | flops 134217728 | bytes 3260416 | tf_op jit(solution)/shard_map/pallas_call | solution.py:25
  4.9 8.6 %all-to-all-start = ((bf16[32,136,128]{2,1,0:T(8,128)(2,1)}), bf16[32,136,128]{2,1,0:T(8,128)(2,1)S(1)}, u32[]{:S(2)}, u32[]{:S(2)}) async-start(bf16[32,136,128]{2,1,0:T(8,128)(2,1)} %get-tuple-element.34), calls=%async_computation | async-start | bytes 2228224 | tf_op jit(solution)/shard_map/all_to_all | solution.py:382
  13.5 0.0 copy-start
  13.5 1.2 copy-done
  14.7 1.2 copy-done.1
  16.0 1.2 copy-done.2
  17.2 5.1 %shard_map.119.local_ref = f32[128,4096]{1,0:T(8,128)S(1)} custom-call(bf16[128,4096]{1,0:T(8,128)(2,1)S(1)} %copy-done.2, bf16[128,4096]{1,0:T(8,128)(2,1)S(1)} %copy-done, bf16[128,4096]{1,0:T(8,128)(2,1)S(1)} %copy-done.1, f32[32,128]{1,0:T(8,128)S(1)} %copy-done.9, f32[128,32]{1,0:T(8,128)S(1)} %copy-done.6), custom_call_target="tpu_custom_call" | custom-call | flops 268435456 | bytes 5275648 | tf_op jit(solution)/shard_map/pallas_call | solution.py:25
  22.3 9.4 %all-to-all-done.arrived_ref = bf16[32,136,128]{2,1,0:T(8,128)(2,1)S(1)} async-done(((bf16[32,136,128]{2,1,0:T(8,128)(2,1)}), bf16[32,136,128]{2,1,0:T(8,128)(2,1)S(1)}, u32[]{:S(2)}, u32[]{:S(2)}) %all-to-all-start) | async-done | bytes 1114144 | tf_op jit(solution)/shard_map/all_to_all | solution.py:382
  31.6 0.3 shard_map.120
  31.9 1.6 collective-permute-start
  33.5 2.7 %collective-permute-start.1 = (f32[136,128]{1,0:T(8,128)S(1)}, f32[136,128]{1,0:T(8,128)S(1)}, u32[]{:S(2)}, u32[]{:S(2)}) collective-permute-start(f32[136,128]{1,0:T(8,128)S(1)} %get-tuple-element.38), channel_id=1, source_target_pairs={{0,64},{32,96},{64,0},{96,32},{1,65},{33,97},{65,1},{97,33},{2,66}... | collective-permute-start | bytes 208904 | tf_op jit(solution)/shard_map/ppermute | solution.py:379
  36.2 1.4 collective-permute-start.2
  37.6 0.6 collective-permute-done.rest_0_
  38.3 1.0 collective-permute-done.1.rest_1_
  39.3 1.2 collective-permute-done.2.rest_2_
  40.5 0.1 iota.7.earlier_ref
  40.6 0.2 shard_map.121
  40.9 20.9 %all_to_all.30.carried_ref = bf16[32,128,128]{2,1,0:T(8,128)(2,1)S(1)} all-to-all(bf16[32,128,128]{2,1,0:T(8,128)(2,1)S(1)} %shard_map.121), channel_id=1, replica_groups=mesh['x'=4,'core'=2,'seq'=16] {'core','seq'}, dimensions={0} | all-to-all | bytes 2097152 | tf_op jit(solution)/shard_map/all_to_all | solution.py:382
  61.8 2.8 %shard_map.122 = (bf16[128,4096]{1,0:T(8,128)(2,1)S(1)}, bf16[16,8,4096]{2,1,0:T(8,128)(2,1)S(1)}, bf16[16,8,4096]{2,1,0:T(8,128)(2,1)S(1)}) custom-call(bf16[128,4096]{1,0:T(8,128)(2,1)S(1)} %copy-done.3, f32[128,4096]{1,0:T(8,128)S(1)} %shard_map.119.local_ref, bf16[128,4096]{1,0:T(8,128)(2,1)S(1)} %copy-done.4, bf16[128,4096]{1,0:T(8,128)(2,1)S(1)} %copy-done.5, ...), custom_call_target="tpu_custom_call" | custom-call | flops 402653184 | bytes 9487360 | tf_op jit(solution)/shard_map/pallas_call | solution.py:25
  64.6 0.1 collective-permute-start.6
  64.7 0.5 collective-permute-start.7
  65.2 20.4 %all_to_all.31 = bf16[16,8,4096]{2,1,0:T(8,128)(2,1)S(1)} all-to-all(bf16[16,8,4096]{2,1,0:T(8,128)(2,1)S(1)} %get-tuple-element.40), channel_id=1, replica_groups=mesh['x'=4,'core'=2,'seq'=16] {'seq'}, dimensions={0} | all-to-all | bytes 2097152 | tf_op jit(solution)/shard_map/all_to_all | solution.py:382
  85.6 0.7 collective-permute-start.3
  86.2 2.5 %collective-permute-start.4 = (bf16[128,4096]{1,0:T(8,128)(2,1)S(1)}, bf16[128,4096]{1,0:T(8,128)(2,1)S(1)}, u32[]{:S(2)}, u32[]{:S(2)}) collective-permute-start(bf16[128,4096]{1,0:T(8,128)(2,1)S(1)} %bitcast.19), channel_id=1, source_target_pairs={{0,96},{32,0},{64,32},{96,64},{1,97},{33,1},{65,33},{97,65},{2,98}... | collective-permute-start | bytes 3145736 | tf_op jit(solution)/shard_map/ppermute | solution.py:378
  88.8 18.9 %all_to_all.32 = bf16[16,8,4096]{2,1,0:T(8,128)(2,1)S(1)} all-to-all(bf16[16,8,4096]{2,1,0:T(8,128)(2,1)S(1)} %get-tuple-element.41), channel_id=1, replica_groups=mesh['x'=4,'core'=2,'seq'=16] {'seq'}, dimensions={0} | all-to-all | bytes 2097152 | tf_op jit(solution)/shard_map/all_to_all | solution.py:382
  107.7 2.5 %collective-permute-done.3.left_ref = bf16[128,4096]{1,0:T(8,128)(2,1)S(1)} collective-permute-done((bf16[128,4096]{1,0:T(8,128)(2,1)S(1)}, bf16[128,4096]{1,0:T(8,128)(2,1)S(1)}, u32[]{:S(2)}, u32[]{:S(2)}) %collective-permute-start.3) | collective-permute-done | bytes 1048608 | tf_op jit(solution)/shard_map/ppermute | solution.py:377
  110.3 3.2 %collective-permute-start.12 = (bf16[128,4096]{1,0:T(8,128)(2,1)S(1)}, bf16[128,4096]{1,0:T(8,128)(2,1)S(1)}, u32[]{:S(2)}, u32[]{:S(2)}) collective-permute-start(bf16[128,4096]{1,0:T(8,128)(2,1)S(1)} %bitcast.15), channel_id=1, source_target_pairs={{0,96},{32,0},{64,32},{96,64},{1,97},{33,1},{65,33},{97,65},{2,98}... | collective-permute-start | bytes 3145736 | tf_op jit(solution)/shard_map/ppermute | solution.py:378
  113.5 20.5 %collective-permute-done.5.far_ref = bf16[128,4096]{1,0:T(8,128)(2,1)S(1)} collective-permute-done((bf16[128,4096]{1,0:T(8,128)(2,1)S(1)}, bf16[128,4096]{1,0:T(8,128)(2,1)S(1)}, u32[]{:S(2)}, u32[]{:S(2)}) %collective-permute-start.5) | collective-permute-done | bytes 1048608 | tf_op jit(solution)/shard_map/ppermute | solution.py:377
  134.0 3.2 %collective-permute-start.13 = (bf16[128,4096]{1,0:T(8,128)(2,1)S(1)}, bf16[128,4096]{1,0:T(8,128)(2,1)S(1)}, u32[]{:S(2)}, u32[]{:S(2)}) collective-permute-start(bf16[128,4096]{1,0:T(8,128)(2,1)S(1)} %collective-permute-done.12.right_ref), channel_id=1, source_target_pairs={{0,96},{32,0},{64,32},{96,64},{1,97},{33,1},{65,33},{97,65},{2,98}... | collective-permute-start | bytes 3145736 | tf_op jit(solution)/shard_map/ppermute | solution.py:378
  137.3 20.7 %shard_map.123 = (bf16[128,4096]{1,0:T(8,128)(2,1)S(1)}, bf16[128,4096]{1,0:T(8,128)(2,1)S(1)}, bf16[128,4096]{1,0:T(8,128)(2,1)S(1)}, bf16[128,4096]{1,0:T(8,128)(2,1)S(1)}) custom-call(bf16[128,4096]{1,0:T(8,128)(2,1)S(1)} %bitcast.20, bf16[128,4096]{1,0:T(8,128)(2,1)S(1)} %collective-permute-done.3.left_ref, ...), custom_call_target="tpu_custom_call" | custom-call | flops 14495514624 | bytes 36700160 | tf_op jit(solution)/shard_map/pallas_call | solution.py:331
  158.0 0.1 collective-permute-start.10
  158.1 2.0 collective-permute-start.8
  160.1 1.0 copy-done.12
  161.1 20.7 %shard_map.124 = (bf16[128,4096]{1,0:T(8,128)(2,1)S(1)}, bf16[128,4096]{1,0:T(8,128)(2,1)S(1)}, bf16[128,4096]{1,0:T(8,128)(2,1)S(1)}, bf16[128,4096]{1,0:T(8,128)(2,1)S(1)}) custom-call(bf16[128,4096]{1,0:T(8,128)(2,1)S(1)} %bitcast.17, bf16[128,4096]{1,0:T(8,128)(2,1)S(1)} %collective-permute-done.11.left_ref, ...), custom_call_target="tpu_custom_call" | custom-call | flops 14495514624 | bytes 36700160 | tf_op jit(solution)/shard_map/pallas_call | solution.py:331
  181.8 1.6 collective-permute-start.14
  183.4 0.2 add_convert_fusion.3
  183.6 0.6 collective-permute-start.9
  184.2 20.6 %collective-permute-done.14 = bf16[128,4096]{1,0:T(8,128)(2,1)S(1)} collective-permute-done((bf16[128,4096]{1,0:T(8,128)(2,1)S(1)}, bf16[128,4096]{1,0:T(8,128)(2,1)S(1)}, u32[]{:S(2)}, u32[]{:S(2)}) %collective-permute-start.14) | collective-permute-done | bytes 1048608 | tf_op jit(solution)/shard_map/ppermute | solution.py:378
  204.8 0.2 add_convert_fusion.1
  205.1 1.6 collective-permute-start.16
  206.7 0.0 collective-permute-done.9
  206.7 0.4 collective-permute-start.15
  207.2 0.5 fusion
  207.6 17.2 %all_to_all.33.rest_0_ = bf16[16,8,4096]{2,1,0:T(8,128)(2,1)S(1)} all-to-all(bf16[16,8,4096]{2,1,0:T(8,128)(2,1)S(1)} %fusion), channel_id=1, replica_groups=mesh['x'=4,'core'=2,'seq'=16] {'seq'}, dimensions={0} | all-to-all | bytes 2097152 | tf_op jit(solution)/shard_map/all_to_all | solution.py:382
  224.9 3.2 %collective-permute-done.15 = bf16[128,4096]{1,0:T(8,128)(2,1)S(1)} collective-permute-done((bf16[128,4096]{1,0:T(8,128)(2,1)S(1)}, bf16[128,4096]{1,0:T(8,128)(2,1)S(1)}, u32[]{:S(2)}, u32[]{:S(2)}) %collective-permute-start.15) | collective-permute-done | bytes 1048608 | tf_op jit(solution)/shard_map/ppermute | solution.py:377
  228.1 0.5 fusion.1
  228.6 18.4 %all_to_all.34.rest_1_ = bf16[16,8,4096]{2,1,0:T(8,128)(2,1)S(1)} all-to-all(bf16[16,8,4096]{2,1,0:T(8,128)(2,1)S(1)} %fusion.1), channel_id=1, replica_groups=mesh['x'=4,'core'=2,'seq'=16] {'seq'}, dimensions={0} | all-to-all | bytes 2097152 | tf_op jit(solution)/shard_map/all_to_all | solution.py:382
  247.0 2.4 shard_map.125
  (35 shorter events, 0.1 us)
Async XLA Ops:
  4.9 8.6 %copy-start.6 = (f32[128,32]{1,0:T(8,128)S(1)}, f32[128,32]{1,0:T(8,128)}, u32[]{:S(2)}) copy-start(f32[128,32]{1,0:T(8,128)} %get-tuple-element.33.by_token_ref) | copy-start | bytes 49156
  4.9 8.6 %copy-start.9 = (f32[32,128]{1,0:T(8,128)S(1)}, f32[32,128]{1,0:T(8,128)}, u32[]{:S(2)}) copy-start(f32[32,128]{1,0:T(8,128)} %get-tuple-element.32.by_head_ref) | copy-start | bytes 49156
  4.9 26.7 %all-to-all-start = ((bf16[32,136,128]{2,1,0:T(8,128)(2,1)}), bf16[32,136,128]{2,1,0:T(8,128)(2,1)S(1)}, u32[]{:S(2)}, u32[]{:S(2)}) async-start(bf16[32,136,128]{2,1,0:T(8,128)(2,1)} %get-tuple-element.34), calls=%async_computation | async-start | bytes 2228224 | tf_op jit(solution)/shard_map/all_to_all | solution.py:382
  13.5 1.2 copy-start
  14.7 1.2 copy-start.1
  16.0 1.2 copy-start.2
  31.9 6.3 %collective-permute-start = (f32[136,128]{1,0:T(8,128)S(1)}, f32[136,128]{1,0:T(8,128)S(1)}, u32[]{:S(2)}, u32[]{:S(2)}) collective-permute-start(f32[136,128]{1,0:T(8,128)S(1)} %get-tuple-element.38), channel_id=1, source_target_pairs={{0,32},{32,64},{64,96},{96,0},{1,33},{33,65},{65,97},{97,1},{2,34}... | collective-permute-start | bytes 208904 | tf_op jit(solution)/shard_map/ppermute | solution.py:379
  33.5 5.8 %collective-permute-start.1 = (f32[136,128]{1,0:T(8,128)S(1)}, f32[136,128]{1,0:T(8,128)S(1)}, u32[]{:S(2)}, u32[]{:S(2)}) collective-permute-start(f32[136,128]{1,0:T(8,128)S(1)} %get-tuple-element.38), channel_id=1, source_target_pairs={{0,64},{32,96},{64,0},{96,32},{1,65},{33,97},{65,1},{97,33},{2,66}... | collective-permute-start | bytes 208904 | tf_op jit(solution)/shard_map/ppermute | solution.py:379
  36.2 4.3 %collective-permute-start.2 = (f32[136,128]{1,0:T(8,128)S(1)}, f32[136,128]{1,0:T(8,128)S(1)}, u32[]{:S(2)}, u32[]{:S(2)}) collective-permute-start(f32[136,128]{1,0:T(8,128)S(1)} %get-tuple-element.38), channel_id=1, source_target_pairs={{0,96},{32,0},{64,32},{96,64},{1,97},{33,1},{65,33},{97,65},{2,98}... | collective-permute-start | bytes 208904 | tf_op jit(solution)/shard_map/ppermute | solution.py:379
  40.6 21.2 %copy-start.3 = (bf16[128,4096]{1,0:T(8,128)(2,1)S(1)}, bf16[128,4096]{1,0:T(8,128)(2,1)}, u32[]{:S(2)}) copy-start(bf16[128,4096]{1,0:T(8,128)(2,1)} %query_ref.3) | copy-start | bytes 3145732
  40.6 21.2 %copy-start.4 = (bf16[128,4096]{1,0:T(8,128)(2,1)S(1)}, bf16[128,4096]{1,0:T(8,128)(2,1)}, u32[]{:S(2)}) copy-start(bf16[128,4096]{1,0:T(8,128)(2,1)} %gate_ref.1) | copy-start | bytes 3145732
  40.6 21.2 %copy-start.5 = (bf16[128,4096]{1,0:T(8,128)(2,1)S(1)}, bf16[128,4096]{1,0:T(8,128)(2,1)}, u32[]{:S(2)}) copy-start(bf16[128,4096]{1,0:T(8,128)(2,1)} %residual_ref.1) | copy-start | bytes 3145732
  40.6 21.2 %copy-start.7 = (f32[4096]{0:T(1024)S(1)}, f32[4096]{0:T(1024)}, u32[]{:S(2)}) copy-start(f32[4096]{0:T(1024)} %param.18) | copy-start | bytes 49156
  40.6 21.2 %copy-start.8 = (f32[4096]{0:T(1024)S(1)}, f32[4096]{0:T(1024)}, u32[]{:S(2)}) copy-start(f32[4096]{0:T(1024)} %param.19) | copy-start | bytes 49156
  40.6 21.2 %copy-start.10 = (s32[128,2]{0,1:T(2,128)S(1)}, s32[128,2]{0,1:T(2,128)}, u32[]{:S(2)}) copy-start(s32[128,2]{0,1:T(2,128)} %param.20) | copy-start | bytes 3076
  64.6 72.7 %collective-permute-start.6 = (bf16[2,576,4096]{2,1,0:T(8,128)(2,1)}, bf16[2,576,4096]{2,1,0:T(8,128)(2,1)}, u32[]{:S(2)}, u32[]{:S(2)}) collective-permute-start(bf16[2,576,4096]{2,1,0:T(8,128)(2,1)} %bitcast.27), channel_id=1, source_target_pairs={{0,16},{16,0},{1,17},{17,1},{2,18},{18,2},{3,19},{19,3},{4,20},{20... | collective-permute-start | bytes 28311560 | tf_op jit(solution)/shard_map/ppermute | solution.py:376
  64.7 45.6 %collective-permute-start.7 = (bf16[576,4096]{1,0:T(8,128)(2,1)}, bf16[576,4096]{1,0:T(8,128)(2,1)}, u32[]{:S(2)}, u32[]{:S(2)}) collective-permute-start(bf16[576,4096]{1,0:T(8,128)(2,1)} %bitcast.30), channel_id=1, source_target_pairs={{0,16},{16,0},{1,17},{17,1},{2,18},{18,2},{3,19},{19,3},{4,20},{20... | collective-permute-start | bytes 14155784 | tf_op jit(solution)/shard_map/ppermute | solution.py:376
  85.6 24.7 %collective-permute-start.3 = (bf16[128,4096]{1,0:T(8,128)(2,1)S(1)}, bf16[128,4096]{1,0:T(8,128)(2,1)S(1)}, u32[]{:S(2)}, u32[]{:S(2)}) collective-permute-start(bf16[128,4096]{1,0:T(8,128)(2,1)S(1)} %bitcast.18), channel_id=1, source_target_pairs={{0,32},{32,64},{64,96},{96,0},{1,33},{33,65},{65,97},{97,1},{2,34}... | collective-permute-start | bytes 3145736 | tf_op jit(solution)/shard_map/ppermute | solution.py:377
  86.2 24.0 %collective-permute-start.4 = (bf16[128,4096]{1,0:T(8,128)(2,1)S(1)}, bf16[128,4096]{1,0:T(8,128)(2,1)S(1)}, u32[]{:S(2)}, u32[]{:S(2)}) collective-permute-start(bf16[128,4096]{1,0:T(8,128)(2,1)S(1)} %bitcast.19), channel_id=1, source_target_pairs={{0,96},{32,0},{64,32},{96,64},{1,97},{33,1},{65,33},{97,65},{2,98}... | collective-permute-start | bytes 3145736 | tf_op jit(solution)/shard_map/ppermute | solution.py:378
  110.2 23.8 %collective-permute-start.5 = (bf16[128,4096]{1,0:T(8,128)(2,1)S(1)}, bf16[128,4096]{1,0:T(8,128)(2,1)S(1)}, u32[]{:S(2)}, u32[]{:S(2)}) collective-permute-start(bf16[128,4096]{1,0:T(8,128)(2,1)S(1)} %collective-permute-done.3.left_ref), channel_id=1, source_target_pairs={{0,32},{32,64},{64,96},{96,0},{1,33},{33,65},{65,97},{97,1},{2,34}... | collective-permute-start | bytes 3145736 | tf_op jit(solution)/shard_map/ppermute | solution.py:377
  110.3 23.8 %collective-permute-start.12 = (bf16[128,4096]{1,0:T(8,128)(2,1)S(1)}, bf16[128,4096]{1,0:T(8,128)(2,1)S(1)}, u32[]{:S(2)}, u32[]{:S(2)}) collective-permute-start(bf16[128,4096]{1,0:T(8,128)(2,1)S(1)} %bitcast.15), channel_id=1, source_target_pairs={{0,96},{32,0},{64,32},{96,64},{1,97},{33,1},{65,33},{97,65},{2,98}... | collective-permute-start | bytes 3145736 | tf_op jit(solution)/shard_map/ppermute | solution.py:378
  134.0 3.2 %copy-start.13 = (bf16[128,4096]{1,0:T(8,128)(2,1)}, bf16[128,4096]{1,0:T(8,128)(2,1)S(1)}, u32[]{:S(2)}) copy-start(bf16[128,4096]{1,0:T(8,128)(2,1)S(1)} %collective-permute-done.5.far_ref) | copy-start | bytes 3145732
  134.0 26.1 %collective-permute-start.11 = (bf16[128,4096]{1,0:T(8,128)(2,1)S(1)}, bf16[128,4096]{1,0:T(8,128)(2,1)S(1)}, u32[]{:S(2)}, u32[]{:S(2)}) collective-permute-start(bf16[128,4096]{1,0:T(8,128)(2,1)S(1)} %bitcast.16), channel_id=1, source_target_pairs={{0,32},{32,64},{64,96},{96,0},{1,33},{33,65},{65,97},{97,1},{2,34}... | collective-permute-start | bytes 3145736 | tf_op jit(solution)/shard_map/ppermute | solution.py:377
  134.0 26.1 %collective-permute-start.13 = (bf16[128,4096]{1,0:T(8,128)(2,1)S(1)}, bf16[128,4096]{1,0:T(8,128)(2,1)S(1)}, u32[]{:S(2)}, u32[]{:S(2)}) collective-permute-start(bf16[128,4096]{1,0:T(8,128)(2,1)S(1)} %collective-permute-done.12.right_ref), channel_id=1, source_target_pairs={{0,96},{32,0},{64,32},{96,64},{1,97},{33,1},{65,33},{97,65},{2,98}... | collective-permute-start | bytes 3145736 | tf_op jit(solution)/shard_map/ppermute | solution.py:378
  158.0 23.8 %collective-permute-start.10 = (bf16[128,4096]{1,0:T(8,128)(2,1)S(1)}, bf16[128,4096]{1,0:T(8,128)(2,1)S(1)}, u32[]{:S(2)}, u32[]{:S(2)}) collective-permute-start(bf16[128,4096]{1,0:T(8,128)(2,1)S(1)} %get-tuple-element.48), channel_id=1, source_target_pairs={{0,96},{32,0},{64,32},{96,64},{1,97},{33,1},{65,33},{97,65},{2,98}... | collective-permute-start | bytes 3145736 | tf_op jit(solution)/shard_map/ppermute | solution.py:378
  158.1 23.7 %collective-permute-start.8 = (bf16[128,4096]{1,0:T(8,128)(2,1)S(1)}, bf16[128,4096]{1,0:T(8,128)(2,1)S(1)}, u32[]{:S(2)}, u32[]{:S(2)}) collective-permute-start(bf16[128,4096]{1,0:T(8,128)(2,1)S(1)} %get-tuple-element.47), channel_id=1, source_target_pairs={{0,32},{32,64},{64,96},{96,0},{1,33},{33,65},{65,97},{97,1},{2,34}... | collective-permute-start | bytes 3145736 | tf_op jit(solution)/shard_map/ppermute | solution.py:377
  160.1 1.0 copy-start.12
  181.8 23.0 %collective-permute-start.14 = (bf16[128,4096]{1,0:T(8,128)(2,1)S(1)}, bf16[128,4096]{1,0:T(8,128)(2,1)S(1)}, u32[]{:S(2)}, u32[]{:S(2)}) collective-permute-start(bf16[128,4096]{1,0:T(8,128)(2,1)S(1)} %get-tuple-element.53), channel_id=1, source_target_pairs={{0,96},{32,0},{64,32},{96,64},{1,97},{33,1},{65,33},{97,65},{2,98}... | collective-permute-start | bytes 3145736 | tf_op jit(solution)/shard_map/ppermute | solution.py:378
  183.6 23.1 %collective-permute-start.9 = (bf16[128,4096]{1,0:T(8,128)(2,1)S(1)}, bf16[128,4096]{1,0:T(8,128)(2,1)S(1)}, u32[]{:S(2)}, u32[]{:S(2)}) collective-permute-start(bf16[128,4096]{1,0:T(8,128)(2,1)S(1)} %add_convert_fusion.3), channel_id=1, source_target_pairs={{0,32},{32,64},{64,96},{96,0},{1,33},{33,65},{65,97},{97,1},{2,34}... | collective-permute-start | bytes 3145736 | tf_op jit(solution)/shard_map/ppermute | solution.py:377
  205.1 19.8 %collective-permute-start.16 = (bf16[128,4096]{1,0:T(8,128)(2,1)S(1)}, bf16[128,4096]{1,0:T(8,128)(2,1)S(1)}, u32[]{:S(2)}, u32[]{:S(2)}) collective-permute-start(bf16[128,4096]{1,0:T(8,128)(2,1)S(1)} %add_convert_fusion.1), channel_id=1, source_target_pairs={{0,96},{32,0},{64,32},{96,64},{1,97},{33,1},{65,33},{97,65},{2,98}... | collective-permute-start | bytes 3145736 | tf_op jit(solution)/shard_map/ppermute | solution.py:378
  206.7 21.4 %collective-permute-start.15 = (bf16[128,4096]{1,0:T(8,128)(2,1)S(1)}, bf16[128,4096]{1,0:T(8,128)(2,1)S(1)}, u32[]{:S(2)}, u32[]{:S(2)}) collective-permute-start(bf16[128,4096]{1,0:T(8,128)(2,1)S(1)} %get-tuple-element.58), channel_id=1, source_target_pairs={{0,32},{32,64},{64,96},{96,0},{1,33},{33,65},{65,97},{97,1},{2,34}... | collective-permute-start | bytes 3145736 | tf_op jit(solution)/shard_map/ppermute | solution.py:377
  228.6 18.4 %copy-start.11 = (f32[128,2]{0,1:T(2,128)S(1)}, f32[128,2]{0,1:T(2,128)}, u32[]{:S(2)}) copy-start(f32[128,2]{0,1:T(2,128)} %param.21) | copy-start | bytes 3076

commit v5 on v4

--- a/solution.py
+++ b/solution.py
@@ -46,7 +46,6 @@
     value_rows_ref,
     sent_ref,
     by_head_ref,
-    by_token_ref,
     rates_ref,
     key_ref,
     value_ref,
@@ -80,10 +79,8 @@
     by_head = jnp.dot(
         rates_ref[...], upto, precision=lax.Precision.HIGHEST, preferred_element_type=F32
     )
-    by_token = by_head.T
     by_head_ref[...] = by_head
-    by_token_ref[...] = by_token
-    fade = jnp.exp(by_token - by_token[tokens - 1 :, :])
+    fade = jnp.exp(by_head - by_head[:, tokens - 1 :])
     keep = jnp.broadcast_to(jnp.exp(-by_head[:, tokens - 1 :]), (heads, HEAD))
     high = keep.astype(BF16).astype(F32)
     middle = (keep - high).astype(BF16).astype(F32)
@@ -93,8 +90,9 @@
         if h % (heads // groups) == 0:
             for copy in copies[h // (heads // groups)]:
                 copy.wait()
-        faded = (key_ref[:, lane_block(h)].astype(F32) * fade[:, h : h + 1]).astype(BF16)
-        state = lax.dot_general(faded, value_ref[:, lane_block(h)], TN, preferred_element_type=F32)
+        turned = key_ref[:, lane_block(h)].T
+        faded = (turned.astype(F32) * fade[h : h + 1, :]).astype(BF16)
+        state = jnp.dot(faded, value_ref[:, lane_block(h)], preferred_element_type=F32)
         tail = jnp.where(row == 0, high[h : h + 1], 0.0)
         tail = jnp.where(row == 1, middle[h : h + 1], tail)
         tail = jnp.where(row == 2, low[h : h + 1], tail).astype(BF16)
@@ -137,17 +135,17 @@
     key_ref,
     value_ref,
     by_head_ref,
-    by_token_ref,
     out_ref,
 ):
     heads, tokens = by_head_ref.shape
+    by_token = by_head_ref[...].T
     at = lambda dim: lax.broadcasted_iota(jnp.int32, (tokens, tokens), dim)
     causal = at(0) >= at(1)
     for h in range(heads):
         scores = lax.dot_general(
             query_ref[:, lane_block(h)], key_ref[:, lane_block(h)], NT, preferred_element_type=F32
         )
-        spacing = by_head_ref[h : h + 1, :] - by_token_ref[:, h : h + 1]
+        spacing = by_head_ref[h : h + 1, :] - by_token[:, h : h + 1]
         fading = jnp.exp(jnp.minimum(spacing, 0.0))
         weights = jnp.where(causal, scores * fading, 0.0).astype(BF16)
         out_ref[:, lane_block(h)] = jnp.dot(
@@ -178,7 +176,7 @@
     gate_ref,
     residual_ref,
     carried_ref,
-    by_token_ref,
+    by_head_ref,
     attention_gain_ref,
     expert_gain_ref,
     index_ref,
@@ -188,7 +186,7 @@
     *bin_refs, attention_ref = rest
     tokens, width = query_ref.shape
     heads = width // HEAD
-    since = jnp.exp(-by_token_ref[...])
+    since = jnp.exp(-by_head_ref[...]).T
     total = jnp.zeros((tokens, HEAD), F32)
     for h in range(heads):
         carried_out = jnp.dot(
@@ -385,12 +383,11 @@
     up_own = jnp.transpose(gate_up_weight[0], (1, 2, 0))
     down_own = down_weight[0]
 
-    sent, by_head, by_token = whole_call(
+    sent, by_head = whole_call(
         state_kernel,
         [
             shape((heads, HEAD + EXTRA, HEAD), BF16),
             shape((heads, tokens), F32),
-            shape((tokens, heads), F32),
         ],
         [decay_rate.T, key_rows, value_rows],
         2 * tokens * width * HEAD,
@@ -408,7 +405,7 @@
     (local_out,) = whole_call(
         local_kernel,
         [shape((tokens, width), F32)],
-        [queries, key_rows, value_rows, by_head, by_token],
+        [queries, key_rows, value_rows, by_head],
         4 * tokens * width * tokens,
         16,
     )
@@ -444,7 +441,7 @@
             gate_logits,
             residual_in,
             carried_low,
-            by_token,
+            by_head,
             attention_gain[None, :],
             expert_gain[None, :],
             index,

time: 250 us -> 249 us (level)
  no operation moved by 1% of the time
where the time goes in v5:
time: 249 us
  blocking collectives  98.3 us (39%)
  waiting for transfers between devices  56.8 us (23%)
  Pallas kernels  56.1 us (23%)
  starting transfers between devices  32.1 us (13%)
  local copies, waits for them, and re-layouts  3.78 us (2%)
    all_to_all x5, blocking collectives, body(): lax.all_to_all(a, axis, split_axis=0, concat_axis=0, tiled=True)  98.3 us
    pallas_call x2, Pallas kernels, expert_rows(): pl.pallas_call(expert_kernel, in_specs=vmem(len(blocks)) + in_place, out_...  41.4 us
    ppermute x6, waiting for transfers between devices, body(): lax.ppermute(a, 'x', [(i, (i + 1) % chips) for i in range(chips)])  25.5 us
    ppermute x6, waiting for transfers between devices, body(): lax.ppermute(a, 'x', [(i, (i - 1) % chips) for i in range(chips)])  19.1 us
    pallas_call x6, Pallas kernels, whole_call(): pl.pallas_call(kernel, out_shape=outs, in_specs=[pl.BlockSpec(memory_spac...  14.7 us
    ppermute x6, starting transfers between devices, body(): lax.ppermute(a, 'x', [(i, (i - 1) % chips) for i in range(chips)])  14 us
    all_to_all x1, waiting for transfers between devices, body(): lax.all_to_all(a, axis, split_axis=0, concat_axis=0, tiled=True)  9.35 us
    all_to_all x1, starting transfers between devices, body(): lax.all_to_all(a, axis, split_axis=0, concat_axis=0, tiled=True)  8.43 us
  transfers between devices with their start and end apart: 18, of which 8 were waited for; matrix products, arithmetic and copies ran while one was open for 0% of the time, Pallas kernels for 19%

profile of v5, /device:TPU:0, one launch (start us, length us, event | category | flops | bytes accessed | tf_op | source)
XLA Modules:
  0.0 248.7 jit_solution(2394667823931322766)
XLA Ops:
  0.0 3.8 %shard_map.118 = (bf16[32,136,128]{2,1,0:T(8,128)(2,1)}, f32[32,128]{1,0:T(8,128)}) custom-call(f32[32,128]{1,0:T(8,128)} %bitcast.26, bf16[128,4096]{1,0:T(8,128)(2,1)} %key_ref.1, bf16[128,4096]{1,0:T(8,128)(2,1)} %value_ref.1), custom_call_target="tpu_custom_call" | custom-call | flops 134217728 | bytes 3244032 | tf_op jit(solution)/shard_map/pallas_call | solution.py:25
  3.8 0.0 copy-start.6
  3.8 8.4 %all-to-all-start = ((bf16[32,136,128]{2,1,0:T(8,128)(2,1)}), bf16[32,136,128]{2,1,0:T(8,128)(2,1)S(1)}, u32[]{:S(2)}, u32[]{:S(2)}) async-start(bf16[32,136,128]{2,1,0:T(8,128)(2,1)} %get-tuple-element.32), calls=%async_computation | async-start | bytes 2228224 | tf_op jit(solution)/shard_map/all_to_all | solution.py:380
  12.2 0.0 copy-start
  12.3 1.2 copy-done
  13.5 1.2 copy-done.1
  14.7 1.2 copy-done.2
  15.9 5.1 %shard_map.119.local_ref = f32[128,4096]{1,0:T(8,128)S(1)} custom-call(bf16[128,4096]{1,0:T(8,128)(2,1)S(1)} %copy-done.2, bf16[128,4096]{1,0:T(8,128)(2,1)S(1)} %copy-done, bf16[128,4096]{1,0:T(8,128)(2,1)S(1)} %copy-done.1, f32[32,128]{1,0:T(8,128)S(1)} %copy-done.6), custom_call_target="tpu_custom_call" | custom-call | flops 268435456 | bytes 5259264 | tf_op jit(solution)/shard_map/pallas_call | solution.py:25
  21.0 9.4 %all-to-all-done.arrived_ref = bf16[32,136,128]{2,1,0:T(8,128)(2,1)S(1)} async-done(((bf16[32,136,128]{2,1,0:T(8,128)(2,1)}), bf16[32,136,128]{2,1,0:T(8,128)(2,1)S(1)}, u32[]{:S(2)}, u32[]{:S(2)}) %all-to-all-start) | async-done | bytes 1114144 | tf_op jit(solution)/shard_map/all_to_all | solution.py:380
  30.4 0.3 shard_map.120
  30.7 1.6 collective-permute-start
  32.2 2.7 %collective-permute-start.1 = (f32[136,128]{1,0:T(8,128)S(1)}, f32[136,128]{1,0:T(8,128)S(1)}, u32[]{:S(2)}, u32[]{:S(2)}) collective-permute-start(f32[136,128]{1,0:T(8,128)S(1)} %get-tuple-element.36), channel_id=1, source_target_pairs={{0,64},{32,96},{64,0},{96,32},{1,65},{33,97},{65,1},{97,33},{2,66}... | collective-permute-start | bytes 208904 | tf_op jit(solution)/shard_map/ppermute | solution.py:377
  35.0 1.4 collective-permute-start.2
  36.4 0.6 collective-permute-done.rest_0_
  37.0 1.0 collective-permute-done.1.rest_1_
  38.0 1.2 collective-permute-done.2.rest_2_
  39.3 0.1 iota.7.earlier_ref
  39.4 0.0 copy-start.9
  39.4 0.2 shard_map.121
  39.6 20.9 %all_to_all.30.carried_ref = bf16[32,128,128]{2,1,0:T(8,128)(2,1)S(1)} all-to-all(bf16[32,128,128]{2,1,0:T(8,128)(2,1)S(1)} %shard_map.121), channel_id=1, replica_groups=mesh['x'=4,'core'=2,'seq'=16] {'core','seq'}, dimensions={0} | all-to-all | bytes 2097152 | tf_op jit(solution)/shard_map/all_to_all | solution.py:380
  60.5 2.9 %shard_map.122 = (bf16[128,4096]{1,0:T(8,128)(2,1)S(1)}, bf16[16,8,4096]{2,1,0:T(8,128)(2,1)S(1)}, bf16[16,8,4096]{2,1,0:T(8,128)(2,1)S(1)}) custom-call(bf16[128,4096]{1,0:T(8,128)(2,1)S(1)} %copy-done.3, f32[128,4096]{1,0:T(8,128)S(1)} %shard_map.119.local_ref, bf16[128,4096]{1,0:T(8,128)(2,1)S(1)} %copy-done.4, bf16[128,4096]{1,0:T(8,128)(2,1)S(1)} %copy-done.5, ...), custom_call_target="tpu_custom_call" | custom-call | flops 402653184 | bytes 9487360 | tf_op jit(solution)/shard_map/pallas_call | solution.py:25
  63.4 0.1 collective-permute-start.6
  63.5 0.5 collective-permute-start.7
  64.0 20.4 %all_to_all.31 = bf16[16,8,4096]{2,1,0:T(8,128)(2,1)S(1)} all-to-all(bf16[16,8,4096]{2,1,0:T(8,128)(2,1)S(1)} %get-tuple-element.38), channel_id=1, replica_groups=mesh['x'=4,'core'=2,'seq'=16] {'seq'}, dimensions={0} | all-to-all | bytes 2097152 | tf_op jit(solution)/shard_map/all_to_all | solution.py:380
  84.4 0.7 collective-permute-start.3
  85.1 2.5 %collective-permute-start.4 = (bf16[128,4096]{1,0:T(8,128)(2,1)S(1)}, bf16[128,4096]{1,0:T(8,128)(2,1)S(1)}, u32[]{:S(2)}, u32[]{:S(2)}) collective-permute-start(bf16[128,4096]{1,0:T(8,128)(2,1)S(1)} %bitcast.19), channel_id=1, source_target_pairs={{0,96},{32,0},{64,32},{96,64},{1,97},{33,1},{65,33},{97,65},{2,98}... | collective-permute-start | bytes 3145736 | tf_op jit(solution)/shard_map/ppermute | solution.py:376
  87.6 18.9 %all_to_all.32 = bf16[16,8,4096]{2,1,0:T(8,128)(2,1)S(1)} all-to-all(bf16[16,8,4096]{2,1,0:T(8,128)(2,1)S(1)} %get-tuple-element.39), channel_id=1, replica_groups=mesh['x'=4,'core'=2,'seq'=16] {'seq'}, dimensions={0} | all-to-all | bytes 2097152 | tf_op jit(solution)/shard_map/all_to_all | solution.py:380
  106.6 2.5 %collective-permute-done.3.left_ref = bf16[128,4096]{1,0:T(8,128)(2,1)S(1)} collective-permute-done((bf16[128,4096]{1,0:T(8,128)(2,1)S(1)}, bf16[128,4096]{1,0:T(8,128)(2,1)S(1)}, u32[]{:S(2)}, u32[]{:S(2)}) %collective-permute-start.3) | collective-permute-done | bytes 1048608 | tf_op jit(solution)/shard_map/ppermute | solution.py:375
  109.1 3.3 %collective-permute-start.12 = (bf16[128,4096]{1,0:T(8,128)(2,1)S(1)}, bf16[128,4096]{1,0:T(8,128)(2,1)S(1)}, u32[]{:S(2)}, u32[]{:S(2)}) collective-permute-start(bf16[128,4096]{1,0:T(8,128)(2,1)S(1)} %bitcast.15), channel_id=1, source_target_pairs={{0,96},{32,0},{64,32},{96,64},{1,97},{33,1},{65,33},{97,65},{2,98}... | collective-permute-start | bytes 3145736 | tf_op jit(solution)/shard_map/ppermute | solution.py:376
  112.4 20.4 %collective-permute-done.5.far_ref = bf16[128,4096]{1,0:T(8,128)(2,1)S(1)} collective-permute-done((bf16[128,4096]{1,0:T(8,128)(2,1)S(1)}, bf16[128,4096]{1,0:T(8,128)(2,1)S(1)}, u32[]{:S(2)}, u32[]{:S(2)}) %collective-permute-start.5) | collective-permute-done | bytes 1048608 | tf_op jit(solution)/shard_map/ppermute | solution.py:375
  132.8 3.2 %collective-permute-start.13 = (bf16[128,4096]{1,0:T(8,128)(2,1)S(1)}, bf16[128,4096]{1,0:T(8,128)(2,1)}, u32[]{:S(2)}, u32[]{:S(2)}) collective-permute-start(bf16[128,4096]{1,0:T(8,128)(2,1)S(1)} %collective-permute-done.12.right_ref), channel_id=1, source_target_pairs={{0,96},{32,0},{64,32},{96,64},{1,97},{33,1},{65,33},{97,65},{2,98}... | collective-permute-start | bytes 3145736 | tf_op jit(solution)/shard_map/ppermute | solution.py:376
  136.1 20.7 %shard_map.123 = (bf16[128,4096]{1,0:T(8,128)(2,1)S(1)}, bf16[128,4096]{1,0:T(8,128)(2,1)S(1)}, bf16[128,4096]{1,0:T(8,128)(2,1)S(1)}, bf16[128,4096]{1,0:T(8,128)(2,1)S(1)}) custom-call(bf16[128,4096]{1,0:T(8,128)(2,1)S(1)} %bitcast.20, bf16[128,4096]{1,0:T(8,128)(2,1)S(1)} %collective-permute-done.3.left_ref, ...), custom_call_target="tpu_custom_call" | custom-call | flops 14495514624 | bytes 36700160 | tf_op jit(solution)/shard_map/pallas_call | solution.py:329
  156.8 0.1 collective-permute-start.10
  156.9 2.0 collective-permute-start.8
  158.9 20.7 %shard_map.124 = (bf16[128,4096]{1,0:T(8,128)(2,1)S(1)}, bf16[128,4096]{1,0:T(8,128)(2,1)S(1)}, bf16[128,4096]{1,0:T(8,128)(2,1)S(1)}, bf16[128,4096]{1,0:T(8,128)(2,1)S(1)}) custom-call(bf16[128,4096]{1,0:T(8,128)(2,1)S(1)} %bitcast.17, bf16[128,4096]{1,0:T(8,128)(2,1)S(1)} %collective-permute-done.11.left_ref, ...), custom_call_target="tpu_custom_call" | custom-call | flops 14495514624 | bytes 36700160 | tf_op jit(solution)/shard_map/pallas_call | solution.py:329
  179.7 1.6 collective-permute-start.14
  181.3 0.2 add_convert_fusion.3
  181.5 0.6 collective-permute-start.9
  182.1 19.1 %collective-permute-done.14 = bf16[128,4096]{1,0:T(8,128)(2,1)S(1)} collective-permute-done((bf16[128,4096]{1,0:T(8,128)(2,1)S(1)}, bf16[128,4096]{1,0:T(8,128)(2,1)S(1)}, u32[]{:S(2)}, u32[]{:S(2)}) %collective-permute-start.14) | collective-permute-done | bytes 1048608 | tf_op jit(solution)/shard_map/ppermute | solution.py:376
  201.2 0.2 add_convert_fusion.1
  201.4 3.3 %collective-permute-start.16 = (bf16[128,4096]{1,0:T(8,128)(2,1)S(1)}, bf16[128,4096]{1,0:T(8,128)(2,1)S(1)}, u32[]{:S(2)}, u32[]{:S(2)}) collective-permute-start(bf16[128,4096]{1,0:T(8,128)(2,1)S(1)} %add_convert_fusion.1), channel_id=1, source_target_pairs={{0,96},{32,0},{64,32},{96,64},{1,97},{33,1},{65,33},{97,65},{2,98}... | collective-permute-start | bytes 3145736 | tf_op jit(solution)/shard_map/ppermute | solution.py:376
  204.7 0.5 fusion
  205.2 19.2 %all_to_all.33.rest_0_ = bf16[16,8,4096]{2,1,0:T(8,128)(2,1)S(1)} all-to-all(bf16[16,8,4096]{2,1,0:T(8,128)(2,1)S(1)} %fusion), channel_id=1, replica_groups=mesh['x'=4,'core'=2,'seq'=16] {'seq'}, dimensions={0} | all-to-all | bytes 2097152 | tf_op jit(solution)/shard_map/all_to_all | solution.py:380
  224.4 2.5 %collective-permute-done.15 = bf16[128,4096]{1,0:T(8,128)(2,1)S(1)} collective-permute-done((bf16[128,4096]{1,0:T(8,128)(2,1)S(1)}, bf16[128,4096]{1,0:T(8,128)(2,1)S(1)}, u32[]{:S(2)}, u32[]{:S(2)}) %collective-permute-start.15) | collective-permute-done | bytes 1048608 | tf_op jit(solution)/shard_map/ppermute | solution.py:375
  226.9 0.5 fusion.1
  227.4 0.0 copy-start.10
  227.4 18.9 %all_to_all.34.rest_1_ = bf16[16,8,4096]{2,1,0:T(8,128)(2,1)S(1)} all-to-all(bf16[16,8,4096]{2,1,0:T(8,128)(2,1)S(1)} %fusion.1), channel_id=1, replica_groups=mesh['x'=4,'core'=2,'seq'=16] {'seq'}, dimensions={0} | all-to-all | bytes 2097152 | tf_op jit(solution)/shard_map/all_to_all | solution.py:380
  246.3 2.4 shard_map.125
  (33 shorter events, 0.1 us)
Async XLA Ops:
  3.8 8.5 %copy-start.6 = (f32[32,128]{1,0:T(8,128)S(1)}, f32[32,128]{1,0:T(8,128)}, u32[]{:S(2)}) copy-start(f32[32,128]{1,0:T(8,128)} %get-tuple-element.31.by_head_ref) | copy-start | bytes 49156
  3.8 26.6 %all-to-all-start = ((bf16[32,136,128]{2,1,0:T(8,128)(2,1)}), bf16[32,136,128]{2,1,0:T(8,128)(2,1)S(1)}, u32[]{:S(2)}, u32[]{:S(2)}) async-start(bf16[32,136,128]{2,1,0:T(8,128)(2,1)} %get-tuple-element.32), calls=%async_computation | async-start | bytes 2228224 | tf_op jit(solution)/shard_map/all_to_all | solution.py:380
  12.2 1.2 copy-start
  13.5 1.2 copy-start.1
  14.7 1.2 copy-start.2
  30.7 6.3 %collective-permute-start = (f32[136,128]{1,0:T(8,128)S(1)}, f32[136,128]{1,0:T(8,128)S(1)}, u32[]{:S(2)}, u32[]{:S(2)}) collective-permute-start(f32[136,128]{1,0:T(8,128)S(1)} %get-tuple-element.36), channel_id=1, source_target_pairs={{0,32},{32,64},{64,96},{96,0},{1,33},{33,65},{65,97},{97,1},{2,34}... | collective-permute-start | bytes 208904 | tf_op jit(solution)/shard_map/ppermute | solution.py:377
  32.2 5.8 %collective-permute-start.1 = (f32[136,128]{1,0:T(8,128)S(1)}, f32[136,128]{1,0:T(8,128)S(1)}, u32[]{:S(2)}, u32[]{:S(2)}) collective-permute-start(f32[136,128]{1,0:T(8,128)S(1)} %get-tuple-element.36), channel_id=1, source_target_pairs={{0,64},{32,96},{64,0},{96,32},{1,65},{33,97},{65,1},{97,33},{2,66}... | collective-permute-start | bytes 208904 | tf_op jit(solution)/shard_map/ppermute | solution.py:377
  35.0 4.3 %collective-permute-start.2 = (f32[136,128]{1,0:T(8,128)S(1)}, f32[136,128]{1,0:T(8,128)S(1)}, u32[]{:S(2)}, u32[]{:S(2)}) collective-permute-start(f32[136,128]{1,0:T(8,128)S(1)} %get-tuple-element.36), channel_id=1, source_target_pairs={{0,96},{32,0},{64,32},{96,64},{1,97},{33,1},{65,33},{97,65},{2,98}... | collective-permute-start | bytes 208904 | tf_op jit(solution)/shard_map/ppermute | solution.py:377
  39.3 21.2 %copy-start.3 = (bf16[128,4096]{1,0:T(8,128)(2,1)S(1)}, bf16[128,4096]{1,0:T(8,128)(2,1)}, u32[]{:S(2)}) copy-start(bf16[128,4096]{1,0:T(8,128)(2,1)} %query_ref.3) | copy-start | bytes 3145732
  39.3 21.2 %copy-start.4 = (bf16[128,4096]{1,0:T(8,128)(2,1)S(1)}, bf16[128,4096]{1,0:T(8,128)(2,1)}, u32[]{:S(2)}) copy-start(bf16[128,4096]{1,0:T(8,128)(2,1)} %gate_ref.1) | copy-start | bytes 3145732
  39.3 21.2 %copy-start.5 = (bf16[128,4096]{1,0:T(8,128)(2,1)S(1)}, bf16[128,4096]{1,0:T(8,128)(2,1)}, u32[]{:S(2)}) copy-start(bf16[128,4096]{1,0:T(8,128)(2,1)} %residual_ref.1) | copy-start | bytes 3145732
  39.3 21.2 %copy-start.7 = (f32[4096]{0:T(1024)S(1)}, f32[4096]{0:T(1024)}, u32[]{:S(2)}) copy-start(f32[4096]{0:T(1024)} %param.18) | copy-start | bytes 49156
  39.3 21.2 %copy-start.8 = (f32[4096]{0:T(1024)S(1)}, f32[4096]{0:T(1024)}, u32[]{:S(2)}) copy-start(f32[4096]{0:T(1024)} %param.19) | copy-start | bytes 49156
  39.4 21.2 %copy-start.9 = (s32[128,2]{0,1:T(2,128)S(1)}, s32[128,2]{0,1:T(2,128)}, u32[]{:S(2)}) copy-start(s32[128,2]{0,1:T(2,128)} %param.20) | copy-start | bytes 3076
  63.4 72.7 %collective-permute-start.6 = (bf16[2,576,4096]{2,1,0:T(8,128)(2,1)}, bf16[2,576,4096]{2,1,0:T(8,128)(2,1)}, u32[]{:S(2)}, u32[]{:S(2)}) collective-permute-start(bf16[2,576,4096]{2,1,0:T(8,128)(2,1)} %bitcast.27), channel_id=1, source_target_pairs={{0,16},{16,0},{1,17},{17,1},{2,18},{18,2},{3,19},{19,3},{4,20},{20... | collective-permute-start | bytes 28311560 | tf_op jit(solution)/shard_map/ppermute | solution.py:374
  63.5 45.6 %collective-permute-start.7 = (bf16[576,4096]{1,0:T(8,128)(2,1)}, bf16[576,4096]{1,0:T(8,128)(2,1)S(1)}, u32[]{:S(2)}, u32[]{:S(2)}) collective-permute-start(bf16[576,4096]{1,0:T(8,128)(2,1)} %bitcast.30), channel_id=1, source_target_pairs={{0,16},{16,0},{1,17},{17,1},{2,18},{18,2},{3,19},{19,3},{4,20},{20... | collective-permute-start | bytes 14155784 | tf_op jit(solution)/shard_map/ppermute | solution.py:374
  84.4 24.7 %collective-permute-start.3 = (bf16[128,4096]{1,0:T(8,128)(2,1)S(1)}, bf16[128,4096]{1,0:T(8,128)(2,1)S(1)}, u32[]{:S(2)}, u32[]{:S(2)}) collective-permute-start(bf16[128,4096]{1,0:T(8,128)(2,1)S(1)} %bitcast.18), channel_id=1, source_target_pairs={{0,32},{32,64},{64,96},{96,0},{1,33},{33,65},{65,97},{97,1},{2,34}... | collective-permute-start | bytes 3145736 | tf_op jit(solution)/shard_map/ppermute | solution.py:375
  85.1 24.0 %collective-permute-start.4 = (bf16[128,4096]{1,0:T(8,128)(2,1)S(1)}, bf16[128,4096]{1,0:T(8,128)(2,1)S(1)}, u32[]{:S(2)}, u32[]{:S(2)}) collective-permute-start(bf16[128,4096]{1,0:T(8,128)(2,1)S(1)} %bitcast.19), channel_id=1, source_target_pairs={{0,96},{32,0},{64,32},{96,64},{1,97},{33,1},{65,33},{97,65},{2,98}... | collective-permute-start | bytes 3145736 | tf_op jit(solution)/shard_map/ppermute | solution.py:376
  109.1 23.8 %collective-permute-start.5 = (bf16[128,4096]{1,0:T(8,128)(2,1)S(1)}, bf16[128,4096]{1,0:T(8,128)(2,1)S(1)}, u32[]{:S(2)}, u32[]{:S(2)}) collective-permute-start(bf16[128,4096]{1,0:T(8,128)(2,1)S(1)} %collective-permute-done.3.left_ref), channel_id=1, source_target_pairs={{0,32},{32,64},{64,96},{96,0},{1,33},{33,65},{65,97},{97,1},{2,34}... | collective-permute-start | bytes 3145736 | tf_op jit(solution)/shard_map/ppermute | solution.py:375
  109.1 27.0 %copy-start.11 = (bf16[576,4096]{1,0:T(8,128)(2,1)}, bf16[576,4096]{1,0:T(8,128)(2,1)S(1)}, u32[]{:S(2)}) copy-start(bf16[576,4096]{1,0:T(8,128)(2,1)S(1)} %collective-permute-done.7.down_other_ref) | copy-start | bytes 14155780
  109.1 23.7 %collective-permute-start.12 = (bf16[128,4096]{1,0:T(8,128)(2,1)S(1)}, bf16[128,4096]{1,0:T(8,128)(2,1)S(1)}, u32[]{:S(2)}, u32[]{:S(2)}) collective-permute-start(bf16[128,4096]{1,0:T(8,128)(2,1)S(1)} %bitcast.15), channel_id=1, source_target_pairs={{0,96},{32,0},{64,32},{96,64},{1,97},{33,1},{65,33},{97,65},{2,98}... | collective-permute-start | bytes 3145736 | tf_op jit(solution)/shard_map/ppermute | solution.py:376
  132.8 3.3 %copy-start.12 = (bf16[128,4096]{1,0:T(8,128)(2,1)}, bf16[128,4096]{1,0:T(8,128)(2,1)S(1)}, u32[]{:S(2)}) copy-start(bf16[128,4096]{1,0:T(8,128)(2,1)S(1)} %collective-permute-done.5.far_ref) | copy-start | bytes 3145732
  132.8 26.1 %collective-permute-start.11 = (bf16[128,4096]{1,0:T(8,128)(2,1)S(1)}, bf16[128,4096]{1,0:T(8,128)(2,1)S(1)}, u32[]{:S(2)}, u32[]{:S(2)}) collective-permute-start(bf16[128,4096]{1,0:T(8,128)(2,1)S(1)} %bitcast.16), channel_id=1, source_target_pairs={{0,32},{32,64},{64,96},{96,0},{1,33},{33,65},{65,97},{97,1},{2,34}... | collective-permute-start | bytes 3145736 | tf_op jit(solution)/shard_map/ppermute | solution.py:375
  132.8 26.1 %collective-permute-start.13 = (bf16[128,4096]{1,0:T(8,128)(2,1)S(1)}, bf16[128,4096]{1,0:T(8,128)(2,1)}, u32[]{:S(2)}, u32[]{:S(2)}) collective-permute-start(bf16[128,4096]{1,0:T(8,128)(2,1)S(1)} %collective-permute-done.12.right_ref), channel_id=1, source_target_pairs={{0,96},{32,0},{64,32},{96,64},{1,97},{33,1},{65,33},{97,65},{2,98}... | collective-permute-start | bytes 3145736 | tf_op jit(solution)/shard_map/ppermute | solution.py:376
  156.8 22.8 %collective-permute-start.10 = (bf16[128,4096]{1,0:T(8,128)(2,1)S(1)}, bf16[128,4096]{1,0:T(8,128)(2,1)S(1)}, u32[]{:S(2)}, u32[]{:S(2)}) collective-permute-start(bf16[128,4096]{1,0:T(8,128)(2,1)S(1)} %get-tuple-element.46), channel_id=1, source_target_pairs={{0,96},{32,0},{64,32},{96,64},{1,97},{33,1},{65,33},{97,65},{2,98}... | collective-permute-start | bytes 3145736 | tf_op jit(solution)/shard_map/ppermute | solution.py:376
  156.9 22.8 %collective-permute-start.8 = (bf16[128,4096]{1,0:T(8,128)(2,1)S(1)}, bf16[128,4096]{1,0:T(8,128)(2,1)S(1)}, u32[]{:S(2)}, u32[]{:S(2)}) collective-permute-start(bf16[128,4096]{1,0:T(8,128)(2,1)S(1)} %get-tuple-element.45), channel_id=1, source_target_pairs={{0,32},{32,64},{64,96},{96,0},{1,33},{33,65},{65,97},{97,1},{2,34}... | collective-permute-start | bytes 3145736 | tf_op jit(solution)/shard_map/ppermute | solution.py:375
  179.7 21.5 %collective-permute-start.14 = (bf16[128,4096]{1,0:T(8,128)(2,1)S(1)}, bf16[128,4096]{1,0:T(8,128)(2,1)S(1)}, u32[]{:S(2)}, u32[]{:S(2)}) collective-permute-start(bf16[128,4096]{1,0:T(8,128)(2,1)S(1)} %get-tuple-element.51), channel_id=1, source_target_pairs={{0,96},{32,0},{64,32},{96,64},{1,97},{33,1},{65,33},{97,65},{2,98}... | collective-permute-start | bytes 3145736 | tf_op jit(solution)/shard_map/ppermute | solution.py:376
  181.5 23.2 %collective-permute-start.9 = (bf16[128,4096]{1,0:T(8,128)(2,1)S(1)}, bf16[128,4096]{1,0:T(8,128)(2,1)S(1)}, u32[]{:S(2)}, u32[]{:S(2)}) collective-permute-start(bf16[128,4096]{1,0:T(8,128)(2,1)S(1)} %add_convert_fusion.3), channel_id=1, source_target_pairs={{0,32},{32,64},{64,96},{96,0},{1,33},{33,65},{65,97},{97,1},{2,34}... | collective-permute-start | bytes 3145736 | tf_op jit(solution)/shard_map/ppermute | solution.py:375
  201.4 23.0 %collective-permute-start.16 = (bf16[128,4096]{1,0:T(8,128)(2,1)S(1)}, bf16[128,4096]{1,0:T(8,128)(2,1)S(1)}, u32[]{:S(2)}, u32[]{:S(2)}) collective-permute-start(bf16[128,4096]{1,0:T(8,128)(2,1)S(1)} %add_convert_fusion.1), channel_id=1, source_target_pairs={{0,96},{32,0},{64,32},{96,64},{1,97},{33,1},{65,33},{97,65},{2,98}... | collective-permute-start | bytes 3145736 | tf_op jit(solution)/shard_map/ppermute | solution.py:376
  204.7 22.2 %collective-permute-start.15 = (bf16[128,4096]{1,0:T(8,128)(2,1)S(1)}, bf16[128,4096]{1,0:T(8,128)(2,1)S(1)}, u32[]{:S(2)}, u32[]{:S(2)}) collective-permute-start(bf16[128,4096]{1,0:T(8,128)(2,1)S(1)} %get-tuple-element.56), channel_id=1, source_target_pairs={{0,32},{32,64},{64,96},{96,0},{1,33},{33,65},{65,97},{97,1},{2,34}... | collective-permute-start | bytes 3145736 | tf_op jit(solution)/shard_map/ppermute | solution.py:375
  227.4 18.9 %copy-start.10 = (f32[128,2]{0,1:T(2,128)S(1)}, f32[128,2]{0,1:T(2,128)}, u32[]{:S(2)}) copy-start(f32[128,2]{0,1:T(2,128)} %param.21) | copy-start | bytes 3076

commit v6 on v5

--- a/solution.py
+++ b/solution.py
@@ -20,7 +20,7 @@
     return [pl.BlockSpec(memory_space=pltpu.VMEM)] * count
 
 
-def whole_call(kernel, outs, args, flops, limit, scratch=(), in_place=()):
+def whole_call(kernel, outs, args, flops, limit, scratch=(), in_place=(), out_in_place=()):
     moved = sum(a.size * a.dtype.itemsize for a in (*args, *outs))
     return pl.pallas_call(
         kernel,
@@ -29,7 +29,10 @@
             pl.BlockSpec(memory_space=pltpu.HBM if place in in_place else pltpu.VMEM)
             for place in range(len(args))
         ],
-        out_specs=vmem(len(outs)),
+        out_specs=[
+            pl.BlockSpec(memory_space=pltpu.HBM if place in out_in_place else pltpu.VMEM)
+            for place in range(len(outs))
+        ],
         scratch_shapes=list(scratch),
         cost_estimate=pl.CostEstimate(flops=flops, bytes_accessed=moved, transcendentals=0),
         compiler_params=pltpu.CompilerParams(vmem_limit_bytes=limit * MIB),
@@ -111,15 +114,21 @@
 
     start = (jnp.zeros((HEAD, HEAD), F32), jnp.ones((EXTRA, HEAD), F32))
     state, kept = lax.fori_loop(0, within_ref.shape[0], step, start, unroll=4)
-    total_ref[:HEAD, :] = state
-    total_ref[HEAD:, :] = kept
+    total_ref[:HEAD, :] = state.astype(BF16)
+    high = kept.astype(BF16).astype(F32)
+    middle = (kept - high).astype(BF16).astype(F32)
+    row = lax.broadcasted_iota(jnp.int32, kept.shape, 0)
+    tail = jnp.where(row == 0, high, jnp.where(row == 1, middle, kept - high - middle))
+    total_ref[HEAD:, :] = tail.astype(BF16)
 
 
 def carry_kernel(within_ref, kept_ref, earlier_ref, *rest):
     *total_refs, carried_ref = rest
     before = jnp.zeros((HEAD, HEAD), F32)
     for place, total_ref in reversed(list(enumerate(total_refs))):
-        longer = total_ref[:HEAD, :] + total_ref[HEAD : HEAD + 1, :] * before
+        tail = total_ref[HEAD:, :].astype(F32)
+        keep = tail[0:1] + tail[1:2] + tail[2:3]
+        longer = total_ref[:HEAD, :].astype(F32) + keep * before
         before = jnp.where(earlier_ref[place : place + 1, :] > 0.0, longer, before)
 
     def step(block, _):
@@ -221,27 +230,49 @@
             bin_ref[:, :, lane_block(h)] = picked.astype(BF16).reshape(experts, rows, HEAD)
 
 
-def mix_kernel(stream_ref, index_ref, router_ref, *rest):
-    *returned_refs, out_ref = rest
-    experts, rows, width = returned_refs[0].shape
+def first_mix_kernel(
+    stream_ref, index_ref, router_ref, returned_ref, total_ref, later_high_ref, later_low_ref
+):
+    experts, rows, width = returned_ref.shape
     first, second, slot = places(index_ref, experts)
     scale = jnp.where(first, router_ref[0:1, :], 0.0) + jnp.where(second, router_ref[1:2, :], 0.0)
     weights = []
-    for c in range(len(returned_refs)):
+    for c in range(2):
         masks = chunk_rows(slot, c, rows)
         chosen = jnp.concatenate(
             [jnp.where(m, scale[e : e + 1, :], 0.0) for e, m in enumerate(masks)], axis=0
         ).T
         high = chosen.astype(BF16)
         weights.append((high, (chosen - high.astype(F32)).astype(BF16)))
+    later_high_ref[...], later_low_ref[...] = weights[1]
+    high, low = weights[0]
     for h in range(width // HEAD // 4):
         columns = slice(h * 4 * HEAD, (h + 1) * 4 * HEAD)
+        returned = returned_ref[:, :, columns].reshape(experts * rows, 4 * HEAD)
         total = stream_ref[:, columns].astype(F32)
-        for (high, low), returned_ref in zip(weights, returned_refs):
-            returned = returned_ref[:, :, columns].reshape(experts * rows, 4 * HEAD)
-            total = total + jnp.dot(high, returned, preferred_element_type=F32)
-            total = total + jnp.dot(low, returned, preferred_element_type=F32)
-        out_ref[:, columns] = total.astype(BF16)
+        total = total + jnp.dot(high, returned, preferred_element_type=F32)
+        total_ref[:, columns] = total + jnp.dot(low, returned, preferred_element_type=F32)
+
+
+def last_mix_kernel(total_ref, high_ref, low_ref, returned_ref, out_ref, mixed_ref, stored):
+    experts, rows, width = returned_ref.shape
+    groups = stored.shape[0]
+    size = width // groups
+    copies = []
+    for g in range(groups):
+        columns = slice(g * size, (g + 1) * size)
+        returned = returned_ref[:, :, columns].reshape(experts * rows, size)
+        total = total_ref[:, columns]
+        total = total + jnp.dot(high_ref[...], returned, preferred_element_type=F32)
+        total = total + jnp.dot(low_ref[...], returned, preferred_element_type=F32)
+        mixed_ref[:, columns] = total.astype(BF16)
+        part = pl.ds(g * size, size)
+        copies.append(
+            pltpu.make_async_copy(mixed_ref.at[:, part], out_ref.at[:, part], stored.at[g])
+        )
+        copies[-1].start()
+    for copy in copies:
+        copy.wait()
 
 
 def expert_kernel(
@@ -414,7 +445,7 @@
         [
             shape((heads, HEAD, HEAD), F32),
             shape((heads, EXTRA, HEAD), F32),
-            shape((HEAD + EXTRA, HEAD), F32),
+            shape((HEAD + EXTRA, HEAD), BF16),
         ],
         [after(arrived, local_out)],
         2 * heads * HEAD * HEAD,
@@ -477,13 +508,22 @@
     back_b = go_back(to_left_b)
     home = lambda *terms: plus(*terms).reshape(experts, rows, width)
     returned_a = exchange(after(home(out_own_a, ahead_a, back_a), to_left_b), "seq")
-    returned_b = exchange(home(after(out_own_b, returned_a), ahead_b, back_b), "seq")
+    total, high, low = whole_call(
+        first_mix_kernel,
+        [shape((tokens, width), F32)] + [shape((tokens, count), BF16)] * 2,
+        [stream, index, router_weight.T, returned_a],
+        4 * tokens * width * count,
+        8,
+    )
+    returned_b = exchange(home(after(out_own_b, total), ahead_b, back_b), "seq")
     (out,) = whole_call(
-        mix_kernel,
+        last_mix_kernel,
         [shape((tokens, width), BF16)],
-        [stream, index, router_weight.T, returned_a, returned_b],
-        4 * tokens * width * count * chunks,
-        16,
+        [total, high, low, returned_b],
+        4 * tokens * width * count,
+        8,
+        [pltpu.VMEM((tokens, width), BF16), pltpu.SemaphoreType.DMA((4,))],
+        out_in_place=(0,),
     )
     return out
 

time: 249 us -> 248 us (level)
    pallas_call x6 -> x7, Pallas kernels: 14.7 us -> 14.6 us  [whole_call(): pl.pallas_call(kernel, out_shape=outs, in_specs=[pl.BlockSpec(memory_spac...]
  transfers between devices with their start and end apart: 18 -> 18, of which waited for: 8 -> 7; matrix products, arithmetic and copies ran while one was open for 0% -> 0% of each run, Pallas kernels for 19% -> 19%
where the time goes in v6:
time: 248 us
  blocking collectives  98.2 us (40%)
  Pallas kernels  56 us (23%)
  waiting for transfers between devices  55.6 us (22%)
  starting transfers between devices  32 us (13%)
  local copies, waits for them, and re-layouts  3.78 us (2%)
    all_to_all x5, blocking collectives, body(): lax.all_to_all(a, axis, split_axis=0, concat_axis=0, tiled=True)  98.2 us
    pallas_call x2, Pallas kernels, expert_rows(): pl.pallas_call(expert_kernel, in_specs=vmem(len(blocks)) + in_place, out_...  41.4 us
    ppermute x6, waiting for transfers between devices, body(): lax.ppermute(a, 'x', [(i, (i + 1) % chips) for i in range(chips)])  24.6 us
    ppermute x6, waiting for transfers between devices, body(): lax.ppermute(a, 'x', [(i, (i - 1) % chips) for i in range(chips)])  19.1 us
    pallas_call x7, Pallas kernels, whole_call(): pl.pallas_call(kernel, out_shape=outs, in_specs=[pl.BlockSpec(memory_spac...  14.6 us
    ppermute x6, starting transfers between devices, body(): lax.ppermute(a, 'x', [(i, (i - 1) % chips) for i in range(chips)])  14.4 us
    all_to_all x1, waiting for transfers between devices, body(): lax.all_to_all(a, axis, split_axis=0, concat_axis=0, tiled=True)  9.35 us
    all_to_all x1, starting transfers between devices, body(): lax.all_to_all(a, axis, split_axis=0, concat_axis=0, tiled=True)  8.43 us
  transfers between devices with their start and end apart: 18, of which 7 were waited for; matrix products, arithmetic and copies ran while one was open for 0% of the time, Pallas kernels for 19%

profile of v6, /device:TPU:0, one launch (start us, length us, event | category | flops | bytes accessed | tf_op | source)
XLA Modules:
  0.0 247.6 jit_solution(4434757574345711867)
XLA Ops:
  0.0 3.8 %shard_map.118 = (bf16[32,136,128]{2,1,0:T(8,128)(2,1)}, f32[32,128]{1,0:T(8,128)}) custom-call(f32[32,128]{1,0:T(8,128)} %bitcast.26, bf16[128,4096]{1,0:T(8,128)(2,1)} %key_ref.1, bf16[128,4096]{1,0:T(8,128)(2,1)} %value_ref.1), custom_call_target="tpu_custom_call" | custom-call | flops 134217728 | bytes 3244032 | tf_op jit(solution)/shard_map/pallas_call | solution.py:25
  3.8 0.0 copy-start.6
  3.8 8.4 %all-to-all-start = ((bf16[32,136,128]{2,1,0:T(8,128)(2,1)}), bf16[32,136,128]{2,1,0:T(8,128)(2,1)S(1)}, u32[]{:S(2)}, u32[]{:S(2)}) async-start(bf16[32,136,128]{2,1,0:T(8,128)(2,1)} %get-tuple-element.35), calls=%async_computation | async-start | bytes 2228224 | tf_op jit(solution)/shard_map/all_to_all | solution.py:411
  12.3 0.0 copy-start
  12.3 1.2 copy-done
  13.5 1.2 copy-done.1
  14.7 1.2 copy-done.2
  15.9 5.1 %shard_map.119.local_ref = f32[128,4096]{1,0:T(8,128)S(1)} custom-call(bf16[128,4096]{1,0:T(8,128)(2,1)S(1)} %copy-done.2, bf16[128,4096]{1,0:T(8,128)(2,1)S(1)} %copy-done, bf16[128,4096]{1,0:T(8,128)(2,1)S(1)} %copy-done.1, f32[32,128]{1,0:T(8,128)S(1)} %copy-done.6), custom_call_target="tpu_custom_call" | custom-call | flops 268435456 | bytes 5259264 | tf_op jit(solution)/shard_map/pallas_call | solution.py:25
  21.0 9.4 %all-to-all-done.arrived_ref = bf16[32,136,128]{2,1,0:T(8,128)(2,1)S(1)} async-done(((bf16[32,136,128]{2,1,0:T(8,128)(2,1)}), bf16[32,136,128]{2,1,0:T(8,128)(2,1)S(1)}, u32[]{:S(2)}, u32[]{:S(2)}) %all-to-all-start) | async-done | bytes 1114144 | tf_op jit(solution)/shard_map/all_to_all | solution.py:411
  30.4 0.3 shard_map.120
  30.7 1.6 collective-permute-start
  32.2 2.7 %collective-permute-start.1 = (bf16[136,128]{1,0:T(8,128)(2,1)S(1)}, bf16[136,128]{1,0:T(8,128)(2,1)S(1)}, u32[]{:S(2)}, u32[]{:S(2)}) collective-permute-start(bf16[136,128]{1,0:T(8,128)(2,1)S(1)} %get-tuple-element.39), channel_id=1, source_target_pairs={{0,64},{32,96},{64,0},{96,32},{1,65},{33,97},{65,1},{97,33},{2,66}... | collective-permute-start | bytes 104456 | tf_op jit(solution)/shard_map/ppermute | solution.py:408
  35.0 1.4 collective-permute-start.2
  36.4 1.3 collective-permute-done.1.rest_1_
  37.7 1.2 collective-permute-done.2.rest_2_
  38.9 0.1 iota.7.earlier_ref
  39.0 0.0 copy-start.9
  39.0 0.2 shard_map.121
  39.3 20.9 %all_to_all.30.carried_ref = bf16[32,128,128]{2,1,0:T(8,128)(2,1)S(1)} all-to-all(bf16[32,128,128]{2,1,0:T(8,128)(2,1)S(1)} %shard_map.121), channel_id=1, replica_groups=mesh['x'=4,'core'=2,'seq'=16] {'core','seq'}, dimensions={0} | all-to-all | bytes 2097152 | tf_op jit(solution)/shard_map/all_to_all | solution.py:411
  60.2 2.9 %shard_map.122 = (bf16[128,4096]{1,0:T(8,128)(2,1)S(1)}, bf16[16,8,4096]{2,1,0:T(8,128)(2,1)S(1)}, bf16[16,8,4096]{2,1,0:T(8,128)(2,1)S(1)}) custom-call(bf16[128,4096]{1,0:T(8,128)(2,1)S(1)} %copy-done.3, f32[128,4096]{1,0:T(8,128)S(1)} %shard_map.119.local_ref, bf16[128,4096]{1,0:T(8,128)(2,1)S(1)} %copy-done.4, bf16[128,4096]{1,0:T(8,128)(2,1)S(1)} %copy-done.5, ...), custom_call_target="tpu_custom_call" | custom-call | flops 402653184 | bytes 9487360 | tf_op jit(solution)/shard_map/pallas_call | solution.py:25
  63.1 0.1 collective-permute-start.6
  63.2 0.5 collective-permute-start.7
  63.7 20.4 %all_to_all.31 = bf16[16,8,4096]{2,1,0:T(8,128)(2,1)S(1)} all-to-all(bf16[16,8,4096]{2,1,0:T(8,128)(2,1)S(1)} %get-tuple-element.41), channel_id=1, replica_groups=mesh['x'=4,'core'=2,'seq'=16] {'seq'}, dimensions={0} | all-to-all | bytes 2097152 | tf_op jit(solution)/shard_map/all_to_all | solution.py:411
  84.0 0.3 collective-permute-start.3
  84.3 3.0 %collective-permute-start.4 = (bf16[128,4096]{1,0:T(8,128)(2,1)S(1)}, bf16[128,4096]{1,0:T(8,128)(2,1)S(1)}, u32[]{:S(2)}, u32[]{:S(2)}) collective-permute-start(bf16[128,4096]{1,0:T(8,128)(2,1)S(1)} %bitcast.19), channel_id=1, source_target_pairs={{0,96},{32,0},{64,32},{96,64},{1,97},{33,1},{65,33},{97,65},{2,98}... | collective-permute-start | bytes 3145736 | tf_op jit(solution)/shard_map/ppermute | solution.py:407
  87.3 18.9 %all_to_all.32 = bf16[16,8,4096]{2,1,0:T(8,128)(2,1)S(1)} all-to-all(bf16[16,8,4096]{2,1,0:T(8,128)(2,1)S(1)} %get-tuple-element.42), channel_id=1, replica_groups=mesh['x'=4,'core'=2,'seq'=16] {'seq'}, dimensions={0} | all-to-all | bytes 2097152 | tf_op jit(solution)/shard_map/all_to_all | solution.py:411
  106.2 2.5 %collective-permute-done.3.left_ref = bf16[128,4096]{1,0:T(8,128)(2,1)S(1)} collective-permute-done((bf16[128,4096]{1,0:T(8,128)(2,1)S(1)}, bf16[128,4096]{1,0:T(8,128)(2,1)S(1)}, u32[]{:S(2)}, u32[]{:S(2)}) %collective-permute-start.3) | collective-permute-done | bytes 1048608 | tf_op jit(solution)/shard_map/ppermute | solution.py:406
  108.8 3.3 %collective-permute-start.12 = (bf16[128,4096]{1,0:T(8,128)(2,1)S(1)}, bf16[128,4096]{1,0:T(8,128)(2,1)S(1)}, u32[]{:S(2)}, u32[]{:S(2)}) collective-permute-start(bf16[128,4096]{1,0:T(8,128)(2,1)S(1)} %bitcast.15), channel_id=1, source_target_pairs={{0,96},{32,0},{64,32},{96,64},{1,97},{33,1},{65,33},{97,65},{2,98}... | collective-permute-start | bytes 3145736 | tf_op jit(solution)/shard_map/ppermute | solution.py:407
  112.1 20.4 %collective-permute-done.5.far_ref = bf16[128,4096]{1,0:T(8,128)(2,1)S(1)} collective-permute-done((bf16[128,4096]{1,0:T(8,128)(2,1)S(1)}, bf16[128,4096]{1,0:T(8,128)(2,1)S(1)}, u32[]{:S(2)}, u32[]{:S(2)}) %collective-permute-start.5) | collective-permute-done | bytes 1048608 | tf_op jit(solution)/shard_map/ppermute | solution.py:406
  132.5 3.2 %collective-permute-start.13 = (bf16[128,4096]{1,0:T(8,128)(2,1)S(1)}, bf16[128,4096]{1,0:T(8,128)(2,1)}, u32[]{:S(2)}, u32[]{:S(2)}) collective-permute-start(bf16[128,4096]{1,0:T(8,128)(2,1)S(1)} %collective-permute-done.12.right_ref), channel_id=1, source_target_pairs={{0,96},{32,0},{64,32},{96,64},{1,97},{33,1},{65,33},{97,65},{2,98}... | collective-permute-start | bytes 3145736 | tf_op jit(solution)/shard_map/ppermute | solution.py:407
  135.8 20.7 %shard_map.123 = (bf16[128,4096]{1,0:T(8,128)(2,1)S(1)}, bf16[128,4096]{1,0:T(8,128)(2,1)S(1)}, bf16[128,4096]{1,0:T(8,128)(2,1)S(1)}, bf16[128,4096]{1,0:T(8,128)(2,1)S(1)}) custom-call(bf16[128,4096]{1,0:T(8,128)(2,1)S(1)} %bitcast.20, bf16[128,4096]{1,0:T(8,128)(2,1)S(1)} %collective-permute-done.3.left_ref, ...), custom_call_target="tpu_custom_call" | custom-call | flops 14495514624 | bytes 36700160 | tf_op jit(solution)/shard_map/pallas_call | solution.py:360
  156.5 0.1 collective-permute-start.10
  156.6 2.0 collective-permute-start.8
  158.6 20.7 %shard_map.124 = (bf16[128,4096]{1,0:T(8,128)(2,1)S(1)}, bf16[128,4096]{1,0:T(8,128)(2,1)S(1)}, bf16[128,4096]{1,0:T(8,128)(2,1)S(1)}, bf16[128,4096]{1,0:T(8,128)(2,1)S(1)}) custom-call(bf16[128,4096]{1,0:T(8,128)(2,1)S(1)} %bitcast.17, bf16[128,4096]{1,0:T(8,128)(2,1)S(1)} %collective-permute-done.11.left_ref, ...), custom_call_target="tpu_custom_call" | custom-call | flops 14495514624 | bytes 36700160 | tf_op jit(solution)/shard_map/pallas_call | solution.py:360
  179.3 1.6 collective-permute-start.14
  180.9 0.2 add_convert_fusion.3
  181.1 0.6 collective-permute-start.9
  181.7 19.1 %collective-permute-done.14 = bf16[128,4096]{1,0:T(8,128)(2,1)S(1)} collective-permute-done((bf16[128,4096]{1,0:T(8,128)(2,1)S(1)}, bf16[128,4096]{1,0:T(8,128)(2,1)S(1)}, u32[]{:S(2)}, u32[]{:S(2)}) %collective-permute-start.14) | collective-permute-done | bytes 1048608 | tf_op jit(solution)/shard_map/ppermute | solution.py:407
  200.9 0.2 add_convert_fusion.1
  201.1 3.3 %collective-permute-start.16 = (bf16[128,4096]{1,0:T(8,128)(2,1)S(1)}, bf16[128,4096]{1,0:T(8,128)(2,1)S(1)}, u32[]{:S(2)}, u32[]{:S(2)}) collective-permute-start(bf16[128,4096]{1,0:T(8,128)(2,1)S(1)} %add_convert_fusion.1), channel_id=1, source_target_pairs={{0,96},{32,0},{64,32},{96,64},{1,97},{33,1},{65,33},{97,65},{2,98}... | collective-permute-start | bytes 3145736 | tf_op jit(solution)/shard_map/ppermute | solution.py:407
  204.4 0.5 fusion
  204.9 0.0 copy-start.10
  204.9 19.2 %all_to_all.33.returned_ref = bf16[16,8,4096]{2,1,0:T(8,128)(2,1)S(1)} all-to-all(bf16[16,8,4096]{2,1,0:T(8,128)(2,1)S(1)} %fusion), channel_id=1, replica_groups=mesh['x'=4,'core'=2,'seq'=16] {'seq'}, dimensions={0} | all-to-all | bytes 2097152 | tf_op jit(solution)/shard_map/all_to_all | solution.py:411
  224.1 0.9 shard_map.125
  225.0 1.6 collective-permute-done.15
  226.6 0.5 fusion.1
  227.1 18.9 %all_to_all.34.returned_ref = bf16[16,8,4096]{2,1,0:T(8,128)(2,1)S(1)} all-to-all(bf16[16,8,4096]{2,1,0:T(8,128)(2,1)S(1)} %fusion.1), channel_id=1, replica_groups=mesh['x'=4,'core'=2,'seq'=16] {'seq'}, dimensions={0} | all-to-all | bytes 2097152 | tf_op jit(solution)/shard_map/all_to_all | solution.py:411
  245.9 1.4 shard_map.126
  (34 shorter events, 0.1 us)
Async XLA Ops:
  3.8 8.5 %copy-start.6 = (f32[32,128]{1,0:T(8,128)S(1)}, f32[32,128]{1,0:T(8,128)}, u32[]{:S(2)}) copy-start(f32[32,128]{1,0:T(8,128)} %get-tuple-element.34.by_head_ref) | copy-start | bytes 49156
  3.8 26.6 %all-to-all-start = ((bf16[32,136,128]{2,1,0:T(8,128)(2,1)}), bf16[32,136,128]{2,1,0:T(8,128)(2,1)S(1)}, u32[]{:S(2)}, u32[]{:S(2)}) async-start(bf16[32,136,128]{2,1,0:T(8,128)(2,1)} %get-tuple-element.35), calls=%async_computation | async-start | bytes 2228224 | tf_op jit(solution)/shard_map/all_to_all | solution.py:411
  12.3 1.2 copy-start
  13.5 1.2 copy-start.1
  14.7 1.2 copy-start.2
  30.7 5.7 %collective-permute-start = (bf16[136,128]{1,0:T(8,128)(2,1)S(1)}, bf16[136,128]{1,0:T(8,128)(2,1)S(1)}, u32[]{:S(2)}, u32[]{:S(2)}) collective-permute-start(bf16[136,128]{1,0:T(8,128)(2,1)S(1)} %get-tuple-element.39), channel_id=1, source_target_pairs={{0,32},{32,64},{64,96},{96,0},{1,33},{33,65},{65,97},{97,1},{2,34}... | collective-permute-start | bytes 104456 | tf_op jit(solution)/shard_map/ppermute | solution.py:408
  32.2 5.4 %collective-permute-start.1 = (bf16[136,128]{1,0:T(8,128)(2,1)S(1)}, bf16[136,128]{1,0:T(8,128)(2,1)S(1)}, u32[]{:S(2)}, u32[]{:S(2)}) collective-permute-start(bf16[136,128]{1,0:T(8,128)(2,1)S(1)} %get-tuple-element.39), channel_id=1, source_target_pairs={{0,64},{32,96},{64,0},{96,32},{1,65},{33,97},{65,1},{97,33},{2,66}... | collective-permute-start | bytes 104456 | tf_op jit(solution)/shard_map/ppermute | solution.py:408
  35.0 3.9 %collective-permute-start.2 = (bf16[136,128]{1,0:T(8,128)(2,1)S(1)}, bf16[136,128]{1,0:T(8,128)(2,1)S(1)}, u32[]{:S(2)}, u32[]{:S(2)}) collective-permute-start(bf16[136,128]{1,0:T(8,128)(2,1)S(1)} %get-tuple-element.39), channel_id=1, source_target_pairs={{0,96},{32,0},{64,32},{96,64},{1,97},{33,1},{65,33},{97,65},{2,98}... | collective-permute-start | bytes 104456 | tf_op jit(solution)/shard_map/ppermute | solution.py:408
  39.0 21.2 %copy-start.3 = (bf16[128,4096]{1,0:T(8,128)(2,1)S(1)}, bf16[128,4096]{1,0:T(8,128)(2,1)}, u32[]{:S(2)}) copy-start(bf16[128,4096]{1,0:T(8,128)(2,1)} %query_ref.3) | copy-start | bytes 3145732
  39.0 21.2 %copy-start.4 = (bf16[128,4096]{1,0:T(8,128)(2,1)S(1)}, bf16[128,4096]{1,0:T(8,128)(2,1)}, u32[]{:S(2)}) copy-start(bf16[128,4096]{1,0:T(8,128)(2,1)} %gate_ref.1) | copy-start | bytes 3145732
  39.0 21.2 %copy-start.5 = (bf16[128,4096]{1,0:T(8,128)(2,1)S(1)}, bf16[128,4096]{1,0:T(8,128)(2,1)}, u32[]{:S(2)}) copy-start(bf16[128,4096]{1,0:T(8,128)(2,1)} %residual_ref.1) | copy-start | bytes 3145732
  39.0 21.2 %copy-start.7 = (f32[4096]{0:T(1024)S(1)}, f32[4096]{0:T(1024)}, u32[]{:S(2)}) copy-start(f32[4096]{0:T(1024)} %param.18) | copy-start | bytes 49156
  39.0 21.2 %copy-start.8 = (f32[4096]{0:T(1024)S(1)}, f32[4096]{0:T(1024)}, u32[]{:S(2)}) copy-start(f32[4096]{0:T(1024)} %param.19) | copy-start | bytes 49156
  39.0 21.2 %copy-start.9 = (s32[128,2]{0,1:T(2,128)S(1)}, s32[128,2]{0,1:T(2,128)}, u32[]{:S(2)}) copy-start(s32[128,2]{0,1:T(2,128)} %param.20) | copy-start | bytes 3076
  63.1 72.7 %collective-permute-start.6 = (bf16[2,576,4096]{2,1,0:T(8,128)(2,1)}, bf16[2,576,4096]{2,1,0:T(8,128)(2,1)}, u32[]{:S(2)}, u32[]{:S(2)}) collective-permute-start(bf16[2,576,4096]{2,1,0:T(8,128)(2,1)} %bitcast.27), channel_id=1, source_target_pairs={{0,16},{16,0},{1,17},{17,1},{2,18},{18,2},{3,19},{19,3},{4,20},{20... | collective-permute-start | bytes 28311560 | tf_op jit(solution)/shard_map/ppermute | solution.py:405
  63.2 45.6 %collective-permute-start.7 = (bf16[576,4096]{1,0:T(8,128)(2,1)}, bf16[576,4096]{1,0:T(8,128)(2,1)S(1)}, u32[]{:S(2)}, u32[]{:S(2)}) collective-permute-start(bf16[576,4096]{1,0:T(8,128)(2,1)} %bitcast.30), channel_id=1, source_target_pairs={{0,16},{16,0},{1,17},{17,1},{2,18},{18,2},{3,19},{19,3},{4,20},{20... | collective-permute-start | bytes 14155784 | tf_op jit(solution)/shard_map/ppermute | solution.py:405
  84.0 24.7 %collective-permute-start.3 = (bf16[128,4096]{1,0:T(8,128)(2,1)S(1)}, bf16[128,4096]{1,0:T(8,128)(2,1)S(1)}, u32[]{:S(2)}, u32[]{:S(2)}) collective-permute-start(bf16[128,4096]{1,0:T(8,128)(2,1)S(1)} %bitcast.18), channel_id=1, source_target_pairs={{0,32},{32,64},{64,96},{96,0},{1,33},{33,65},{65,97},{97,1},{2,34}... | collective-permute-start | bytes 3145736 | tf_op jit(solution)/shard_map/ppermute | solution.py:406
  84.3 24.4 %collective-permute-start.4 = (bf16[128,4096]{1,0:T(8,128)(2,1)S(1)}, bf16[128,4096]{1,0:T(8,128)(2,1)S(1)}, u32[]{:S(2)}, u32[]{:S(2)}) collective-permute-start(bf16[128,4096]{1,0:T(8,128)(2,1)S(1)} %bitcast.19), channel_id=1, source_target_pairs={{0,96},{32,0},{64,32},{96,64},{1,97},{33,1},{65,33},{97,65},{2,98}... | collective-permute-start | bytes 3145736 | tf_op jit(solution)/shard_map/ppermute | solution.py:407
  108.7 23.8 %collective-permute-start.5 = (bf16[128,4096]{1,0:T(8,128)(2,1)S(1)}, bf16[128,4096]{1,0:T(8,128)(2,1)S(1)}, u32[]{:S(2)}, u32[]{:S(2)}) collective-permute-start(bf16[128,4096]{1,0:T(8,128)(2,1)S(1)} %collective-permute-done.3.left_ref), channel_id=1, source_target_pairs={{0,32},{32,64},{64,96},{96,0},{1,33},{33,65},{65,97},{97,1},{2,34}... | collective-permute-start | bytes 3145736 | tf_op jit(solution)/shard_map/ppermute | solution.py:406
  108.7 27.0 %copy-start.11 = (bf16[576,4096]{1,0:T(8,128)(2,1)}, bf16[576,4096]{1,0:T(8,128)(2,1)S(1)}, u32[]{:S(2)}) copy-start(bf16[576,4096]{1,0:T(8,128)(2,1)S(1)} %collective-permute-done.7.down_other_ref) | copy-start | bytes 14155780
  108.8 23.7 %collective-permute-start.12 = (bf16[128,4096]{1,0:T(8,128)(2,1)S(1)}, bf16[128,4096]{1,0:T(8,128)(2,1)S(1)}, u32[]{:S(2)}, u32[]{:S(2)}) collective-permute-start(bf16[128,4096]{1,0:T(8,128)(2,1)S(1)} %bitcast.15), channel_id=1, source_target_pairs={{0,96},{32,0},{64,32},{96,64},{1,97},{33,1},{65,33},{97,65},{2,98}... | collective-permute-start | bytes 3145736 | tf_op jit(solution)/shard_map/ppermute | solution.py:407
  132.5 3.3 %copy-start.12 = (bf16[128,4096]{1,0:T(8,128)(2,1)}, bf16[128,4096]{1,0:T(8,128)(2,1)S(1)}, u32[]{:S(2)}) copy-start(bf16[128,4096]{1,0:T(8,128)(2,1)S(1)} %collective-permute-done.5.far_ref) | copy-start | bytes 3145732
  132.5 26.1 %collective-permute-start.11 = (bf16[128,4096]{1,0:T(8,128)(2,1)S(1)}, bf16[128,4096]{1,0:T(8,128)(2,1)S(1)}, u32[]{:S(2)}, u32[]{:S(2)}) collective-permute-start(bf16[128,4096]{1,0:T(8,128)(2,1)S(1)} %bitcast.16), channel_id=1, source_target_pairs={{0,32},{32,64},{64,96},{96,0},{1,33},{33,65},{65,97},{97,1},{2,34}... | collective-permute-start | bytes 3145736 | tf_op jit(solution)/shard_map/ppermute | solution.py:406
  132.5 26.1 %collective-permute-start.13 = (bf16[128,4096]{1,0:T(8,128)(2,1)S(1)}, bf16[128,4096]{1,0:T(8,128)(2,1)}, u32[]{:S(2)}, u32[]{:S(2)}) collective-permute-start(bf16[128,4096]{1,0:T(8,128)(2,1)S(1)} %collective-permute-done.12.right_ref), channel_id=1, source_target_pairs={{0,96},{32,0},{64,32},{96,64},{1,97},{33,1},{65,33},{97,65},{2,98}... | collective-permute-start | bytes 3145736 | tf_op jit(solution)/shard_map/ppermute | solution.py:407
  156.5 22.8 %collective-permute-start.10 = (bf16[128,4096]{1,0:T(8,128)(2,1)S(1)}, bf16[128,4096]{1,0:T(8,128)(2,1)S(1)}, u32[]{:S(2)}, u32[]{:S(2)}) collective-permute-start(bf16[128,4096]{1,0:T(8,128)(2,1)S(1)} %get-tuple-element.49), channel_id=1, source_target_pairs={{0,96},{32,0},{64,32},{96,64},{1,97},{33,1},{65,33},{97,65},{2,98}... | collective-permute-start | bytes 3145736 | tf_op jit(solution)/shard_map/ppermute | solution.py:407
  156.6 22.7 %collective-permute-start.8 = (bf16[128,4096]{1,0:T(8,128)(2,1)S(1)}, bf16[128,4096]{1,0:T(8,128)(2,1)S(1)}, u32[]{:S(2)}, u32[]{:S(2)}) collective-permute-start(bf16[128,4096]{1,0:T(8,128)(2,1)S(1)} %get-tuple-element.48), channel_id=1, source_target_pairs={{0,32},{32,64},{64,96},{96,0},{1,33},{33,65},{65,97},{97,1},{2,34}... | collective-permute-start | bytes 3145736 | tf_op jit(solution)/shard_map/ppermute | solution.py:406
  179.3 21.5 %collective-permute-start.14 = (bf16[128,4096]{1,0:T(8,128)(2,1)S(1)}, bf16[128,4096]{1,0:T(8,128)(2,1)S(1)}, u32[]{:S(2)}, u32[]{:S(2)}) collective-permute-start(bf16[128,4096]{1,0:T(8,128)(2,1)S(1)} %get-tuple-element.54), channel_id=1, source_target_pairs={{0,96},{32,0},{64,32},{96,64},{1,97},{33,1},{65,33},{97,65},{2,98}... | collective-permute-start | bytes 3145736 | tf_op jit(solution)/shard_map/ppermute | solution.py:407
  181.1 23.2 %collective-permute-start.9 = (bf16[128,4096]{1,0:T(8,128)(2,1)S(1)}, bf16[128,4096]{1,0:T(8,128)(2,1)S(1)}, u32[]{:S(2)}, u32[]{:S(2)}) collective-permute-start(bf16[128,4096]{1,0:T(8,128)(2,1)S(1)} %add_convert_fusion.3), channel_id=1, source_target_pairs={{0,32},{32,64},{64,96},{96,0},{1,33},{33,65},{65,97},{97,1},{2,34}... | collective-permute-start | bytes 3145736 | tf_op jit(solution)/shard_map/ppermute | solution.py:406
  201.1 23.8 %collective-permute-start.16 = (bf16[128,4096]{1,0:T(8,128)(2,1)S(1)}, bf16[128,4096]{1,0:T(8,128)(2,1)S(1)}, u32[]{:S(2)}, u32[]{:S(2)}) collective-permute-start(bf16[128,4096]{1,0:T(8,128)(2,1)S(1)} %add_convert_fusion.1), channel_id=1, source_target_pairs={{0,96},{32,0},{64,32},{96,64},{1,97},{33,1},{65,33},{97,65},{2,98}... | collective-permute-start | bytes 3145736 | tf_op jit(solution)/shard_map/ppermute | solution.py:407
  204.4 22.2 %collective-permute-start.15 = (bf16[128,4096]{1,0:T(8,128)(2,1)S(1)}, bf16[128,4096]{1,0:T(8,128)(2,1)S(1)}, u32[]{:S(2)}, u32[]{:S(2)}) collective-permute-start(bf16[128,4096]{1,0:T(8,128)(2,1)S(1)} %get-tuple-element.62), channel_id=1, source_target_pairs={{0,32},{32,64},{64,96},{96,0},{1,33},{33,65},{65,97},{97,1},{2,34}... | collective-permute-start | bytes 3145736 | tf_op jit(solution)/shard_map/ppermute | solution.py:406
  204.9 19.2 %copy-start.10 = (f32[128,2]{0,1:T(2,128)S(1)}, f32[128,2]{0,1:T(2,128)}, u32[]{:S(2)}) copy-start(f32[128,2]{0,1:T(2,128)} %param.21) | copy-start | bytes 3076

commit v7 on v6

--- a/solution.py
+++ b/solution.py
@@ -140,14 +140,29 @@
 
 
 def local_kernel(
+    experts,
+    chunks,
     query_ref,
     key_ref,
     value_ref,
     by_head_ref,
+    index_ref,
+    gate_ref,
+    attention_gain_ref,
     out_ref,
+    since_ref,
+    selector_ref,
+    gate_gain_ref,
 ):
     heads, tokens = by_head_ref.shape
     by_token = by_head_ref[...].T
+    since_ref[...] = jnp.exp(-by_token)
+    slot = places(index_ref, experts)[2]
+    count = selector_ref.shape[0] // chunks
+    for c in range(chunks):
+        masks = chunk_rows(slot, c, count // experts)
+        selector = jnp.concatenate([m.astype(F32) for m in masks], axis=0)
+        selector_ref[c * count : (c + 1) * count, :] = selector.astype(BF16)
     at = lambda dim: lax.broadcasted_iota(jnp.int32, (tokens, tokens), dim)
     causal = at(0) >= at(1)
     for h in range(heads):
@@ -160,6 +175,9 @@
         out_ref[:, lane_block(h)] = jnp.dot(
             weights, value_ref[:, lane_block(h)], preferred_element_type=F32
         )
+        gate = gate_ref[:, lane_block(h)].astype(F32)
+        gain = attention_gain_ref[:, lane_block(h)]
+        gate_gain_ref[:, lane_block(h)] = gain / (1.0 + jnp.exp(-gate))
 
 
 def places(index_ref, experts):
@@ -182,20 +200,19 @@
 def stream_kernel(
     query_ref,
     local_ref,
-    gate_ref,
+    gate_gain_ref,
     residual_ref,
     carried_ref,
-    by_head_ref,
-    attention_gain_ref,
+    since_ref,
     expert_gain_ref,
-    index_ref,
+    selector_ref,
     stream_ref,
     *rest,
 ):
     *bin_refs, attention_ref = rest
     tokens, width = query_ref.shape
     heads = width // HEAD
-    since = jnp.exp(-by_head_ref[...]).T
+    since = since_ref[...]
     total = jnp.zeros((tokens, HEAD), F32)
     for h in range(heads):
         carried_out = jnp.dot(
@@ -207,27 +224,23 @@
     inverse = lax.rsqrt(jnp.sum(total, axis=1, keepdims=True) / width + 1e-05)
     total = jnp.zeros((tokens, HEAD), F32)
     for h in range(heads):
-        gate = gate_ref[:, lane_block(h)].astype(F32)
-        gain = attention_gain_ref[:, lane_block(h)] / (1.0 + jnp.exp(-gate))
-        gated = attention_ref[:, lane_block(h)] * inverse * gain
+        gated = attention_ref[:, lane_block(h)] * inverse * gate_gain_ref[:, lane_block(h)]
         stream = (residual_ref[:, lane_block(h)].astype(F32) + gated).astype(BF16)
         stream_ref[:, lane_block(h)] = stream
         wide = stream.astype(F32)
         total = total + wide * wide
     inverse = lax.rsqrt(jnp.sum(total, axis=1, keepdims=True) / width + 1e-05)
-    experts = bin_refs[0].shape[0]
-    rows = bin_refs[0].shape[1]
-    slot = places(index_ref, experts)[2]
-    selectors = [
-        jnp.concatenate([m.astype(F32) for m in chunk_rows(slot, c, rows)], axis=0).astype(BF16)
-        for c in range(len(bin_refs))
-    ]
-    for h in range(heads):
-        wide = stream_ref[:, lane_block(h)].astype(F32)
-        entry = (wide * inverse * expert_gain_ref[:, lane_block(h)]).astype(BF16)
-        for selector, bin_ref in zip(selectors, bin_refs):
-            picked = jnp.dot(selector, entry, preferred_element_type=F32)
-            bin_ref[:, :, lane_block(h)] = picked.astype(BF16).reshape(experts, rows, HEAD)
+    experts, rows, _ = bin_refs[0].shape
+    count = experts * rows
+    size = 2 * HEAD
+    for start in range(0, width, size):
+        columns = slice(start, start + size)
+        wide = stream_ref[:, columns].astype(F32)
+        entry = (wide * inverse * expert_gain_ref[:, columns]).astype(BF16)
+        picked = jnp.dot(selector_ref[...], entry, preferred_element_type=F32).astype(BF16)
+        for c, bin_ref in enumerate(bin_refs):
+            part = picked[c * count : (c + 1) * count]
+            bin_ref[:, :, columns] = part.reshape(experts, rows, size)
 
 
 def first_mix_kernel(
@@ -433,10 +446,24 @@
         (0, 1, 2),
     )
     arrived = exchange(sent, plane)
-    (local_out,) = whole_call(
-        local_kernel,
-        [shape((tokens, width), F32)],
-        [queries, key_rows, value_rows, by_head],
+    index = expert_index.T
+    local_out, since, selector, gate_gain = whole_call(
+        functools.partial(local_kernel, experts, chunks),
+        [
+            shape((tokens, width), F32),
+            shape((tokens, heads), F32),
+            shape((chunks * count, tokens), BF16),
+            shape((tokens, width), F32),
+        ],
+        [
+            queries,
+            key_rows,
+            value_rows,
+            by_head,
+            index,
+            gate_logits,
+            attention_gain[None, :],
+        ],
         4 * tokens * width * tokens,
         16,
     )
@@ -462,20 +489,18 @@
         8,
     )
     carried_low = exchange(carried, plane)
-    index = expert_index.T
     stream, *bins = whole_call(
         stream_kernel,
         [shape((tokens, width), BF16)] + [shape((experts, rows, width), BF16)] * chunks,
         [
             queries,
             local_out,
-            gate_logits,
+            gate_gain,
             residual_in,
             carried_low,
-            by_head,
-            attention_gain[None, :],
+            since,
             expert_gain[None, :],
-            index,
+            selector,
         ],
         2 * tokens * width * (HEAD + chunks * count),
         8,

time: 248 us -> 247 us (level)
  local copies, waits for them, and re-layouts: 3.78 us -> 7.43 us
    unnamed x26 -> x32, local copies, waits for them, and re-layouts: 3.71 us -> 7.36 us
    all_to_all x1, waiting for transfers between devices: 9.35 us -> 6.62 us  [body(): lax.all_to_all(a, axis, split_axis=0, concat_axis=0, tiled=True)]
where the time goes in v7:
time: 247 us
  blocking collectives  96 us (39%)
  Pallas kernels  55.7 us (23%)
  waiting for transfers between devices  55.1 us (22%)
  starting transfers between devices  30.8 us (12%)
  local copies, waits for them, and re-layouts  7.43 us (3%)
    all_to_all x5, blocking collectives, body(): lax.all_to_all(a, axis, split_axis=0, concat_axis=0, tiled=True)  96 us
    pallas_call x2, Pallas kernels, expert_rows(): pl.pallas_call(expert_kernel, in_specs=vmem(len(blocks)) + in_place, out_...  41.4 us
    ppermute x6, waiting for transfers between devices, body(): lax.ppermute(a, 'x', [(i, (i + 1) % chips) for i in range(chips)])  25.4 us
    ppermute x6, waiting for transfers between devices, body(): lax.ppermute(a, 'x', [(i, (i - 1) % chips) for i in range(chips)])  20.6 us
    pallas_call x7, Pallas kernels, whole_call(): pl.pallas_call(kernel, out_shape=outs, in_specs=[pl.BlockSpec(memory_spac...  14.3 us
    ppermute x6, starting transfers between devices, body(): lax.ppermute(a, 'x', [(i, (i - 1) % chips) for i in range(chips)])  12.7 us
    all_to_all x1, starting transfers between devices, body(): lax.all_to_all(a, axis, split_axis=0, concat_axis=0, tiled=True)  8.43 us
    unnamed x32, local copies, waits for them, and re-layouts  7.36 us
  transfers between devices with their start and end apart: 18, of which 7 were waited for; matrix products, arithmetic and copies ran while one was open for 0% of the time, Pallas kernels for 19%

profile of v7, /device:TPU:0, one launch (start us, length us, event | category | flops | bytes accessed | tf_op | source)
XLA Modules:
  0.0 246.9 jit_solution(4673455098415210003)
XLA Ops:
  0.0 3.9 %shard_map.118 = (bf16[32,136,128]{2,1,0:T(8,128)(2,1)}, f32[32,128]{1,0:T(8,128)}) custom-call(f32[32,128]{1,0:T(8,128)} %bitcast.26, bf16[128,4096]{1,0:T(8,128)(2,1)} %key_ref.1, bf16[128,4096]{1,0:T(8,128)(2,1)} %value_ref.1), custom_call_target="tpu_custom_call" | custom-call | flops 134217728 | bytes 3244032 | tf_op jit(solution)/shard_map/pallas_call | solution.py:25
  3.9 8.4 %all-to-all-start = ((bf16[32,136,128]{2,1,0:T(8,128)(2,1)}), bf16[32,136,128]{2,1,0:T(8,128)(2,1)S(1)}, u32[]{:S(2)}, u32[]{:S(2)}) async-start(bf16[32,136,128]{2,1,0:T(8,128)(2,1)} %get-tuple-element.41), calls=%async_computation | async-start | bytes 2228224 | tf_op jit(solution)/shard_map/all_to_all | solution.py:424
  12.4 1.2 copy-done.1
  13.6 1.2 copy-done.2
  14.9 1.2 copy-done.7
  16.1 5.1 %shard_map.119 = (f32[128,4096]{1,0:T(8,128)S(1)}, f32[128,32]{1,0:T(8,128)S(1)}, bf16[256,128]{1,0:T(8,128)(2,1)S(1)}, f32[128,4096]{1,0:T(8,128)S(1)}) custom-call(bf16[128,4096]{1,0:T(8,128)(2,1)S(1)} %copy-done, bf16[128,4096]{1,0:T(8,128)(2,1)S(1)} %copy-done.1, bf16[128,4096]{1,0:T(8,128)(2,1)S(1)} %copy-done.2, f32[32,128]{1,0:T(8,128)S(1)} %copy-done.11, ...), custom_call_target="tpu_custom_call" | custom-call | flops 268435456 | bytes 8504320 | tf_op jit(solution)/shard_map/pallas_call | solution.py:25
  21.2 1.3 copy-done.3
  22.6 1.3 copy-done.5
  23.9 6.6 %all-to-all-done.arrived_ref = bf16[32,136,128]{2,1,0:T(8,128)(2,1)S(1)} async-done(((bf16[32,136,128]{2,1,0:T(8,128)(2,1)}), bf16[32,136,128]{2,1,0:T(8,128)(2,1)S(1)}, u32[]{:S(2)}, u32[]{:S(2)}) %all-to-all-start) | async-done | bytes 1114144 | tf_op jit(solution)/shard_map/all_to_all | solution.py:424
  30.5 0.3 shard_map.120
  30.8 1.6 collective-permute-start
  32.4 2.7 %collective-permute-start.1 = (bf16[136,128]{1,0:T(8,128)(2,1)S(1)}, bf16[136,128]{1,0:T(8,128)(2,1)S(1)}, u32[]{:S(2)}, u32[]{:S(2)}) collective-permute-start(bf16[136,128]{1,0:T(8,128)(2,1)S(1)} %get-tuple-element.45), channel_id=1, source_target_pairs={{0,64},{32,96},{64,0},{96,32},{1,65},{33,97},{65,1},{97,33},{2,66}... | collective-permute-start | bytes 104456 | tf_op jit(solution)/shard_map/ppermute | solution.py:421
  35.1 1.4 collective-permute-start.2
  36.5 1.3 collective-permute-done.1.rest_1_
  37.8 1.2 collective-permute-done.2.rest_2_
  39.0 0.1 iota.7.earlier_ref
  39.1 0.2 shard_map.121
  39.4 21.0 %all_to_all.30.carried_ref = bf16[32,128,128]{2,1,0:T(8,128)(2,1)S(1)} all-to-all(bf16[32,128,128]{2,1,0:T(8,128)(2,1)S(1)} %shard_map.121), channel_id=1, replica_groups=mesh['x'=4,'core'=2,'seq'=16] {'core','seq'}, dimensions={0} | all-to-all | bytes 2097152 | tf_op jit(solution)/shard_map/all_to_all | solution.py:424
  60.4 2.4 shard_map.122
  62.8 0.1 collective-permute-start.6
  62.9 0.5 collective-permute-start.7
  63.4 20.4 %all_to_all.31 = bf16[16,8,4096]{2,1,0:T(8,128)(2,1)S(1)} all-to-all(bf16[16,8,4096]{2,1,0:T(8,128)(2,1)S(1)} %get-tuple-element.49), channel_id=1, replica_groups=mesh['x'=4,'core'=2,'seq'=16] {'seq'}, dimensions={0} | all-to-all | bytes 2097152 | tf_op jit(solution)/shard_map/all_to_all | solution.py:424
  83.8 0.3 collective-permute-start.3
  84.1 3.0 %collective-permute-start.4 = (bf16[128,4096]{1,0:T(8,128)(2,1)S(1)}, bf16[128,4096]{1,0:T(8,128)(2,1)S(1)}, u32[]{:S(2)}, u32[]{:S(2)}) collective-permute-start(bf16[128,4096]{1,0:T(8,128)(2,1)S(1)} %bitcast.19), channel_id=1, source_target_pairs={{0,96},{32,0},{64,32},{96,64},{1,97},{33,1},{65,33},{97,65},{2,98}... | collective-permute-start | bytes 3145736 | tf_op jit(solution)/shard_map/ppermute | solution.py:420
  87.0 18.9 %all_to_all.32 = bf16[16,8,4096]{2,1,0:T(8,128)(2,1)S(1)} all-to-all(bf16[16,8,4096]{2,1,0:T(8,128)(2,1)S(1)} %get-tuple-element.50), channel_id=1, replica_groups=mesh['x'=4,'core'=2,'seq'=16] {'seq'}, dimensions={0} | all-to-all | bytes 2097152 | tf_op jit(solution)/shard_map/all_to_all | solution.py:424
  106.0 2.5 %collective-permute-done.3.left_ref = bf16[128,4096]{1,0:T(8,128)(2,1)S(1)} collective-permute-done((bf16[128,4096]{1,0:T(8,128)(2,1)S(1)}, bf16[128,4096]{1,0:T(8,128)(2,1)S(1)}, u32[]{:S(2)}, u32[]{:S(2)}) %collective-permute-start.3) | collective-permute-done | bytes 1048608 | tf_op jit(solution)/shard_map/ppermute | solution.py:419
  108.5 3.2 %collective-permute-start.12 = (bf16[128,4096]{1,0:T(8,128)(2,1)S(1)}, bf16[128,4096]{1,0:T(8,128)(2,1)S(1)}, u32[]{:S(2)}, u32[]{:S(2)}) collective-permute-start(bf16[128,4096]{1,0:T(8,128)(2,1)S(1)} %bitcast.15), channel_id=1, source_target_pairs={{0,96},{32,0},{64,32},{96,64},{1,97},{33,1},{65,33},{97,65},{2,98}... | collective-permute-start | bytes 3145736 | tf_op jit(solution)/shard_map/ppermute | solution.py:420
  111.7 20.5 %collective-permute-done.5.far_ref = bf16[128,4096]{1,0:T(8,128)(2,1)S(1)} collective-permute-done((bf16[128,4096]{1,0:T(8,128)(2,1)S(1)}, bf16[128,4096]{1,0:T(8,128)(2,1)S(1)}, u32[]{:S(2)}, u32[]{:S(2)}) %collective-permute-start.5) | collective-permute-done | bytes 1048608 | tf_op jit(solution)/shard_map/ppermute | solution.py:419
  132.3 3.2 %collective-permute-start.13 = (bf16[128,4096]{1,0:T(8,128)(2,1)S(1)}, bf16[128,4096]{1,0:T(8,128)(2,1)S(1)}, u32[]{:S(2)}, u32[]{:S(2)}) collective-permute-start(bf16[128,4096]{1,0:T(8,128)(2,1)S(1)} %collective-permute-done.12.right_ref), channel_id=1, source_target_pairs={{0,96},{32,0},{64,32},{96,64},{1,97},{33,1},{65,33},{97,65},{2,98}... | collective-permute-start | bytes 3145736 | tf_op jit(solution)/shard_map/ppermute | solution.py:420
  135.5 20.7 %shard_map.123 = (bf16[128,4096]{1,0:T(8,128)(2,1)S(1)}, bf16[128,4096]{1,0:T(8,128)(2,1)S(1)}, bf16[128,4096]{1,0:T(8,128)(2,1)S(1)}, bf16[128,4096]{1,0:T(8,128)(2,1)S(1)}) custom-call(bf16[128,4096]{1,0:T(8,128)(2,1)S(1)} %bitcast.20, bf16[128,4096]{1,0:T(8,128)(2,1)S(1)} %collective-permute-done.3.left_ref, ...), custom_call_target="tpu_custom_call" | custom-call | flops 14495514624 | bytes 36700160 | tf_op jit(solution)/shard_map/pallas_call | solution.py:373
  156.2 0.1 collective-permute-start.10
  156.3 2.0 collective-permute-start.8
  158.3 1.0 copy-done.14
  159.3 20.7 %shard_map.124 = (bf16[128,4096]{1,0:T(8,128)(2,1)S(1)}, bf16[128,4096]{1,0:T(8,128)(2,1)S(1)}, bf16[128,4096]{1,0:T(8,128)(2,1)S(1)}, bf16[128,4096]{1,0:T(8,128)(2,1)S(1)}) custom-call(bf16[128,4096]{1,0:T(8,128)(2,1)S(1)} %bitcast.17, bf16[128,4096]{1,0:T(8,128)(2,1)S(1)} %collective-permute-done.11.left_ref, ...), custom_call_target="tpu_custom_call" | custom-call | flops 14495514624 | bytes 36700160 | tf_op jit(solution)/shard_map/pallas_call | solution.py:373
  180.0 1.6 collective-permute-start.14
  181.6 0.2 add_convert_fusion.3
  181.8 0.6 collective-permute-start.9
  182.4 20.6 %collective-permute-done.14 = bf16[128,4096]{1,0:T(8,128)(2,1)S(1)} collective-permute-done((bf16[128,4096]{1,0:T(8,128)(2,1)S(1)}, bf16[128,4096]{1,0:T(8,128)(2,1)S(1)}, u32[]{:S(2)}, u32[]{:S(2)}) %collective-permute-start.14) | collective-permute-done | bytes 1048608 | tf_op jit(solution)/shard_map/ppermute | solution.py:420
  203.0 0.2 add_convert_fusion.1
  203.3 1.6 collective-permute-start.16
  204.9 0.4 collective-permute-start.15
  205.4 0.5 fusion
  205.9 17.3 %all_to_all.33.returned_ref = bf16[16,8,4096]{2,1,0:T(8,128)(2,1)S(1)} all-to-all(bf16[16,8,4096]{2,1,0:T(8,128)(2,1)S(1)} %fusion), channel_id=1, replica_groups=mesh['x'=4,'core'=2,'seq'=16] {'seq'}, dimensions={0} | all-to-all | bytes 2097152 | tf_op jit(solution)/shard_map/all_to_all | solution.py:424
  223.2 0.9 shard_map.125
  224.1 2.3 collective-permute-done.15
  226.3 0.5 fusion.1
  226.8 18.4 %all_to_all.34.returned_ref = bf16[16,8,4096]{2,1,0:T(8,128)(2,1)S(1)} all-to-all(bf16[16,8,4096]{2,1,0:T(8,128)(2,1)S(1)} %fusion.1), channel_id=1, replica_groups=mesh['x'=4,'core'=2,'seq'=16] {'seq'}, dimensions={0} | all-to-all | bytes 2097152 | tf_op jit(solution)/shard_map/all_to_all | solution.py:424
  245.3 1.4 shard_map.126
  (40 shorter events, 0.1 us)
Async XLA Ops:
  0.0 12.4 %copy-start = (bf16[128,4096]{1,0:T(8,128)(2,1)S(1)}, bf16[128,4096]{1,0:T(8,128)(2,1)}, u32[]{:S(2)}) copy-start(bf16[128,4096]{1,0:T(8,128)(2,1)} %query_ref.3) | copy-start | bytes 3145732
  0.0 12.4 %copy-start.9 = (f32[4096]{0:T(1024)S(1)}, f32[4096]{0:T(1024)}, u32[]{:S(2)}) copy-start(f32[4096]{0:T(1024)} %param.18) | copy-start | bytes 49156
  0.0 12.4 %copy-start.12 = (s32[128,2]{0,1:T(2,128)S(1)}, s32[128,2]{0,1:T(2,128)}, u32[]{:S(2)}) copy-start(s32[128,2]{0,1:T(2,128)} %param.20) | copy-start | bytes 3076
  3.9 8.5 %copy-start.11 = (f32[32,128]{1,0:T(8,128)S(1)}, f32[32,128]{1,0:T(8,128)}, u32[]{:S(2)}) copy-start(f32[32,128]{1,0:T(8,128)} %get-tuple-element.38.by_head_ref) | copy-start | bytes 49156
  3.9 26.6 %all-to-all-start = ((bf16[32,136,128]{2,1,0:T(8,128)(2,1)}), bf16[32,136,128]{2,1,0:T(8,128)(2,1)S(1)}, u32[]{:S(2)}, u32[]{:S(2)}) async-start(bf16[32,136,128]{2,1,0:T(8,128)(2,1)} %get-tuple-element.41), calls=%async_computation | async-start | bytes 2228224 | tf_op jit(solution)/shard_map/all_to_all | solution.py:424
  12.4 1.2 copy-start.1
  13.6 1.2 copy-start.2
  14.9 1.2 copy-start.7
  21.2 1.4 copy-start.3
  22.6 1.3 copy-start.5
  30.8 5.7 %collective-permute-start = (bf16[136,128]{1,0:T(8,128)(2,1)S(1)}, bf16[136,128]{1,0:T(8,128)(2,1)S(1)}, u32[]{:S(2)}, u32[]{:S(2)}) collective-permute-start(bf16[136,128]{1,0:T(8,128)(2,1)S(1)} %get-tuple-element.45), channel_id=1, source_target_pairs={{0,32},{32,64},{64,96},{96,0},{1,33},{33,65},{65,97},{97,1},{2,34}... | collective-permute-start | bytes 104456 | tf_op jit(solution)/shard_map/ppermute | solution.py:421
  32.4 5.4 %collective-permute-start.1 = (bf16[136,128]{1,0:T(8,128)(2,1)S(1)}, bf16[136,128]{1,0:T(8,128)(2,1)S(1)}, u32[]{:S(2)}, u32[]{:S(2)}) collective-permute-start(bf16[136,128]{1,0:T(8,128)(2,1)S(1)} %get-tuple-element.45), channel_id=1, source_target_pairs={{0,64},{32,96},{64,0},{96,32},{1,65},{33,97},{65,1},{97,33},{2,66}... | collective-permute-start | bytes 104456 | tf_op jit(solution)/shard_map/ppermute | solution.py:421
  35.1 3.9 %collective-permute-start.2 = (bf16[136,128]{1,0:T(8,128)(2,1)S(1)}, bf16[136,128]{1,0:T(8,128)(2,1)S(1)}, u32[]{:S(2)}, u32[]{:S(2)}) collective-permute-start(bf16[136,128]{1,0:T(8,128)(2,1)S(1)} %get-tuple-element.45), channel_id=1, source_target_pairs={{0,96},{32,0},{64,32},{96,64},{1,97},{33,1},{65,33},{97,65},{2,98}... | collective-permute-start | bytes 104456 | tf_op jit(solution)/shard_map/ppermute | solution.py:421
  39.1 21.3 %copy-start.4 = (f32[128,4096]{1,0:T(8,128)S(1)}, f32[128,4096]{1,0:T(8,128)}, u32[]{:S(2)}) copy-start(f32[128,4096]{1,0:T(8,128)} %copy-done.3) | copy-start | bytes 6291460
  39.1 21.3 %copy-start.6 = (f32[128,4096]{1,0:T(8,128)S(1)}, f32[128,4096]{1,0:T(8,128)}, u32[]{:S(2)}) copy-start(f32[128,4096]{1,0:T(8,128)} %copy-done.5) | copy-start | bytes 6291460
  39.1 21.3 %copy-start.8 = (bf16[128,4096]{1,0:T(8,128)(2,1)S(1)}, bf16[128,4096]{1,0:T(8,128)(2,1)}, u32[]{:S(2)}) copy-start(bf16[128,4096]{1,0:T(8,128)(2,1)} %residual_ref.1) | copy-start | bytes 3145732
  39.1 21.3 %copy-start.10 = (f32[4096]{0:T(1024)S(1)}, f32[4096]{0:T(1024)}, u32[]{:S(2)}) copy-start(f32[4096]{0:T(1024)} %param.19) | copy-start | bytes 49156
  62.8 72.7 %collective-permute-start.6 = (bf16[2,576,4096]{2,1,0:T(8,128)(2,1)}, bf16[2,576,4096]{2,1,0:T(8,128)(2,1)}, u32[]{:S(2)}, u32[]{:S(2)}) collective-permute-start(bf16[2,576,4096]{2,1,0:T(8,128)(2,1)} %bitcast.27), channel_id=1, source_target_pairs={{0,16},{16,0},{1,17},{17,1},{2,18},{18,2},{3,19},{19,3},{4,20},{20... | collective-permute-start | bytes 28311560 | tf_op jit(solution)/shard_map/ppermute | solution.py:418
  62.9 45.6 %collective-permute-start.7 = (bf16[576,4096]{1,0:T(8,128)(2,1)}, bf16[576,4096]{1,0:T(8,128)(2,1)}, u32[]{:S(2)}, u32[]{:S(2)}) collective-permute-start(bf16[576,4096]{1,0:T(8,128)(2,1)} %bitcast.30), channel_id=1, source_target_pairs={{0,16},{16,0},{1,17},{17,1},{2,18},{18,2},{3,19},{19,3},{4,20},{20... | collective-permute-start | bytes 14155784 | tf_op jit(solution)/shard_map/ppermute | solution.py:418
  83.8 24.7 %collective-permute-start.3 = (bf16[128,4096]{1,0:T(8,128)(2,1)S(1)}, bf16[128,4096]{1,0:T(8,128)(2,1)S(1)}, u32[]{:S(2)}, u32[]{:S(2)}) collective-permute-start(bf16[128,4096]{1,0:T(8,128)(2,1)S(1)} %bitcast.18), channel_id=1, source_target_pairs={{0,32},{32,64},{64,96},{96,0},{1,33},{33,65},{65,97},{97,1},{2,34}... | collective-permute-start | bytes 3145736 | tf_op jit(solution)/shard_map/ppermute | solution.py:419
  84.1 24.4 %collective-permute-start.4 = (bf16[128,4096]{1,0:T(8,128)(2,1)S(1)}, bf16[128,4096]{1,0:T(8,128)(2,1)S(1)}, u32[]{:S(2)}, u32[]{:S(2)}) collective-permute-start(bf16[128,4096]{1,0:T(8,128)(2,1)S(1)} %bitcast.19), channel_id=1, source_target_pairs={{0,96},{32,0},{64,32},{96,64},{1,97},{33,1},{65,33},{97,65},{2,98}... | collective-permute-start | bytes 3145736 | tf_op jit(solution)/shard_map/ppermute | solution.py:420
  108.5 23.8 %collective-permute-start.5 = (bf16[128,4096]{1,0:T(8,128)(2,1)S(1)}, bf16[128,4096]{1,0:T(8,128)(2,1)S(1)}, u32[]{:S(2)}, u32[]{:S(2)}) collective-permute-start(bf16[128,4096]{1,0:T(8,128)(2,1)S(1)} %collective-permute-done.3.left_ref), channel_id=1, source_target_pairs={{0,32},{32,64},{64,96},{96,0},{1,33},{33,65},{65,97},{97,1},{2,34}... | collective-permute-start | bytes 3145736 | tf_op jit(solution)/shard_map/ppermute | solution.py:419
  108.5 23.8 %collective-permute-start.12 = (bf16[128,4096]{1,0:T(8,128)(2,1)S(1)}, bf16[128,4096]{1,0:T(8,128)(2,1)S(1)}, u32[]{:S(2)}, u32[]{:S(2)}) collective-permute-start(bf16[128,4096]{1,0:T(8,128)(2,1)S(1)} %bitcast.15), channel_id=1, source_target_pairs={{0,96},{32,0},{64,32},{96,64},{1,97},{33,1},{65,33},{97,65},{2,98}... | collective-permute-start | bytes 3145736 | tf_op jit(solution)/shard_map/ppermute | solution.py:420
  132.2 3.2 %copy-start.15 = (bf16[128,4096]{1,0:T(8,128)(2,1)}, bf16[128,4096]{1,0:T(8,128)(2,1)S(1)}, u32[]{:S(2)}) copy-start(bf16[128,4096]{1,0:T(8,128)(2,1)S(1)} %collective-permute-done.5.far_ref) | copy-start | bytes 3145732
  132.2 26.1 %collective-permute-start.11 = (bf16[128,4096]{1,0:T(8,128)(2,1)S(1)}, bf16[128,4096]{1,0:T(8,128)(2,1)S(1)}, u32[]{:S(2)}, u32[]{:S(2)}) collective-permute-start(bf16[128,4096]{1,0:T(8,128)(2,1)S(1)} %bitcast.16), channel_id=1, source_target_pairs={{0,32},{32,64},{64,96},{96,0},{1,33},{33,65},{65,97},{97,1},{2,34}... | collective-permute-start | bytes 3145736 | tf_op jit(solution)/shard_map/ppermute | solution.py:419
  132.3 26.0 %collective-permute-start.13 = (bf16[128,4096]{1,0:T(8,128)(2,1)S(1)}, bf16[128,4096]{1,0:T(8,128)(2,1)S(1)}, u32[]{:S(2)}, u32[]{:S(2)}) collective-permute-start(bf16[128,4096]{1,0:T(8,128)(2,1)S(1)} %collective-permute-done.12.right_ref), channel_id=1, source_target_pairs={{0,96},{32,0},{64,32},{96,64},{1,97},{33,1},{65,33},{97,65},{2,98}... | collective-permute-start | bytes 3145736 | tf_op jit(solution)/shard_map/ppermute | solution.py:420
  156.2 23.8 %collective-permute-start.10 = (bf16[128,4096]{1,0:T(8,128)(2,1)S(1)}, bf16[128,4096]{1,0:T(8,128)(2,1)S(1)}, u32[]{:S(2)}, u32[]{:S(2)}) collective-permute-start(bf16[128,4096]{1,0:T(8,128)(2,1)S(1)} %get-tuple-element.57), channel_id=1, source_target_pairs={{0,96},{32,0},{64,32},{96,64},{1,97},{33,1},{65,33},{97,65},{2,98}... | collective-permute-start | bytes 3145736 | tf_op jit(solution)/shard_map/ppermute | solution.py:420
  156.3 23.7 %collective-permute-start.8 = (bf16[128,4096]{1,0:T(8,128)(2,1)S(1)}, bf16[128,4096]{1,0:T(8,128)(2,1)S(1)}, u32[]{:S(2)}, u32[]{:S(2)}) collective-permute-start(bf16[128,4096]{1,0:T(8,128)(2,1)S(1)} %get-tuple-element.56), channel_id=1, source_target_pairs={{0,32},{32,64},{64,96},{96,0},{1,33},{33,65},{65,97},{97,1},{2,34}... | collective-permute-start | bytes 3145736 | tf_op jit(solution)/shard_map/ppermute | solution.py:419
  158.3 1.0 copy-start.14
  180.0 23.0 %collective-permute-start.14 = (bf16[128,4096]{1,0:T(8,128)(2,1)S(1)}, bf16[128,4096]{1,0:T(8,128)(2,1)S(1)}, u32[]{:S(2)}, u32[]{:S(2)}) collective-permute-start(bf16[128,4096]{1,0:T(8,128)(2,1)S(1)} %get-tuple-element.62), channel_id=1, source_target_pairs={{0,96},{32,0},{64,32},{96,64},{1,97},{33,1},{65,33},{97,65},{2,98}... | collective-permute-start | bytes 3145736 | tf_op jit(solution)/shard_map/ppermute | solution.py:420
  181.8 23.1 %collective-permute-start.9 = (bf16[128,4096]{1,0:T(8,128)(2,1)S(1)}, bf16[128,4096]{1,0:T(8,128)(2,1)S(1)}, u32[]{:S(2)}, u32[]{:S(2)}) collective-permute-start(bf16[128,4096]{1,0:T(8,128)(2,1)S(1)} %add_convert_fusion.3), channel_id=1, source_target_pairs={{0,32},{32,64},{64,96},{96,0},{1,33},{33,65},{65,97},{97,1},{2,34}... | collective-permute-start | bytes 3145736 | tf_op jit(solution)/shard_map/ppermute | solution.py:419
  203.3 20.8 %collective-permute-start.16 = (bf16[128,4096]{1,0:T(8,128)(2,1)S(1)}, bf16[128,4096]{1,0:T(8,128)(2,1)S(1)}, u32[]{:S(2)}, u32[]{:S(2)}) collective-permute-start(bf16[128,4096]{1,0:T(8,128)(2,1)S(1)} %add_convert_fusion.1), channel_id=1, source_target_pairs={{0,96},{32,0},{64,32},{96,64},{1,97},{33,1},{65,33},{97,65},{2,98}... | collective-permute-start | bytes 3145736 | tf_op jit(solution)/shard_map/ppermute | solution.py:420
  204.9 21.4 %collective-permute-start.15 = (bf16[128,4096]{1,0:T(8,128)(2,1)S(1)}, bf16[128,4096]{1,0:T(8,128)(2,1)S(1)}, u32[]{:S(2)}, u32[]{:S(2)}) collective-permute-start(bf16[128,4096]{1,0:T(8,128)(2,1)S(1)} %get-tuple-element.70), channel_id=1, source_target_pairs={{0,32},{32,64},{64,96},{96,0},{1,33},{33,65},{65,97},{97,1},{2,34}... | collective-permute-start | bytes 3145736 | tf_op jit(solution)/shard_map/ppermute | solution.py:419
  205.9 17.3 %copy-start.13 = (f32[128,2]{0,1:T(2,128)S(1)}, f32[128,2]{0,1:T(2,128)}, u32[]{:S(2)}) copy-start(f32[128,2]{0,1:T(2,128)} %param.21) | copy-start | bytes 3076

commit v8 on v7

--- a/solution.py
+++ b/solution.py
@@ -440,7 +440,7 @@
             pltpu.VMEM((heads, tokens), F32),
             pltpu.VMEM((tokens, width), BF16),
             pltpu.VMEM((tokens, width), BF16),
-            pltpu.SemaphoreType.DMA((2, 4)),
+            pltpu.SemaphoreType.DMA((2, 2)),
             pltpu.SemaphoreType.DMA,
         ],
         (0, 1, 2),

time: 247 us -> 247 us (level)
  no operation moved by 1% of the time
where the time goes in v8:
time: 247 us; the launch traced here: 246 us
  blocking collectives  96 us (39%)
  Pallas kernels  55.2 us (22%)
  waiting for transfers between devices  55.1 us (22%)
  starting transfers between devices  30.8 us (12%)
  local copies, waits for them, and re-layouts  7.43 us (3%)
    all_to_all x5, blocking collectives, body(): lax.all_to_all(a, axis, split_axis=0, concat_axis=0, tiled=True)  96 us
    pallas_call x2, Pallas kernels, expert_rows(): pl.pallas_call(expert_kernel, in_specs=vmem(len(blocks)) + in_place, out_...  41.4 us
    ppermute x6, waiting for transfers between devices, body(): lax.ppermute(a, 'x', [(i, (i + 1) % chips) for i in range(chips)])  25.3 us
    ppermute x6, waiting for transfers between devices, body(): lax.ppermute(a, 'x', [(i, (i - 1) % chips) for i in range(chips)])  20.7 us
    pallas_call x7, Pallas kernels, whole_call(): pl.pallas_call(kernel, out_shape=outs, in_specs=[pl.BlockSpec(memory_spac...  13.8 us
    ppermute x6, starting transfers between devices, body(): lax.ppermute(a, 'x', [(i, (i - 1) % chips) for i in range(chips)])  12.7 us
    all_to_all x1, starting transfers between devices, body(): lax.all_to_all(a, axis, split_axis=0, concat_axis=0, tiled=True)  8.43 us
    unnamed x32, local copies, waits for them, and re-layouts  7.36 us
  transfers between devices with their start and end apart: 18, of which 7 were waited for; matrix products, arithmetic and copies ran while one was open for 0% of the time, Pallas kernels for 19%

profile of v8, /device:TPU:0, one launch (start us, length us, event | category | flops | bytes accessed | tf_op | source)
XLA Modules:
  0.0 246.4 jit_solution(1324805115316589103)
XLA Ops:
  0.0 3.4 %shard_map.118 = (bf16[32,136,128]{2,1,0:T(8,128)(2,1)}, f32[32,128]{1,0:T(8,128)}) custom-call(f32[32,128]{1,0:T(8,128)} %bitcast.26, bf16[128,4096]{1,0:T(8,128)(2,1)} %key_ref.1, bf16[128,4096]{1,0:T(8,128)(2,1)} %value_ref.1), custom_call_target="tpu_custom_call" | custom-call | flops 134217728 | bytes 3244032 | tf_op jit(solution)/shard_map/pallas_call | solution.py:25
  3.4 8.4 %all-to-all-start = ((bf16[32,136,128]{2,1,0:T(8,128)(2,1)}), bf16[32,136,128]{2,1,0:T(8,128)(2,1)S(1)}, u32[]{:S(2)}, u32[]{:S(2)}) async-start(bf16[32,136,128]{2,1,0:T(8,128)(2,1)} %get-tuple-element.41), calls=%async_computation | async-start | bytes 2228224 | tf_op jit(solution)/shard_map/all_to_all | solution.py:424
  11.9 1.2 copy-done.1
  13.1 1.2 copy-done.2
  14.3 1.2 copy-done.7
  15.6 5.1 %shard_map.119 = (f32[128,4096]{1,0:T(8,128)S(1)}, f32[128,32]{1,0:T(8,128)S(1)}, bf16[256,128]{1,0:T(8,128)(2,1)S(1)}, f32[128,4096]{1,0:T(8,128)S(1)}) custom-call(bf16[128,4096]{1,0:T(8,128)(2,1)S(1)} %copy-done, bf16[128,4096]{1,0:T(8,128)(2,1)S(1)} %copy-done.1, bf16[128,4096]{1,0:T(8,128)(2,1)S(1)} %copy-done.2, f32[32,128]{1,0:T(8,128)S(1)} %copy-done.11, ...), custom_call_target="tpu_custom_call" | custom-call | flops 268435456 | bytes 8504320 | tf_op jit(solution)/shard_map/pallas_call | solution.py:25
  20.7 1.3 copy-done.3
  22.0 1.3 copy-done.5
  23.4 6.6 %all-to-all-done.arrived_ref = bf16[32,136,128]{2,1,0:T(8,128)(2,1)S(1)} async-done(((bf16[32,136,128]{2,1,0:T(8,128)(2,1)}), bf16[32,136,128]{2,1,0:T(8,128)(2,1)S(1)}, u32[]{:S(2)}, u32[]{:S(2)}) %all-to-all-start) | async-done | bytes 1114144 | tf_op jit(solution)/shard_map/all_to_all | solution.py:424
  30.0 0.3 shard_map.120
  30.3 1.6 collective-permute-start
  31.8 2.7 %collective-permute-start.1 = (bf16[136,128]{1,0:T(8,128)(2,1)S(1)}, bf16[136,128]{1,0:T(8,128)(2,1)S(1)}, u32[]{:S(2)}, u32[]{:S(2)}) collective-permute-start(bf16[136,128]{1,0:T(8,128)(2,1)S(1)} %get-tuple-element.45), channel_id=1, source_target_pairs={{0,64},{32,96},{64,0},{96,32},{1,65},{33,97},{65,1},{97,33},{2,66}... | collective-permute-start | bytes 104456 | tf_op jit(solution)/shard_map/ppermute | solution.py:421
  34.6 1.4 collective-permute-start.2
  36.0 1.3 collective-permute-done.1.rest_1_
  37.3 1.2 collective-permute-done.2.rest_2_
  38.5 0.1 iota.7.earlier_ref
  38.6 0.2 shard_map.121
  38.8 21.0 %all_to_all.30.carried_ref = bf16[32,128,128]{2,1,0:T(8,128)(2,1)S(1)} all-to-all(bf16[32,128,128]{2,1,0:T(8,128)(2,1)S(1)} %shard_map.121), channel_id=1, replica_groups=mesh['x'=4,'core'=2,'seq'=16] {'core','seq'}, dimensions={0} | all-to-all | bytes 2097152 | tf_op jit(solution)/shard_map/all_to_all | solution.py:424
  59.9 2.4 shard_map.122
  62.3 0.1 collective-permute-start.6
  62.4 0.5 collective-permute-start.7
  62.9 20.4 %all_to_all.31 = bf16[16,8,4096]{2,1,0:T(8,128)(2,1)S(1)} all-to-all(bf16[16,8,4096]{2,1,0:T(8,128)(2,1)S(1)} %get-tuple-element.49), channel_id=1, replica_groups=mesh['x'=4,'core'=2,'seq'=16] {'seq'}, dimensions={0} | all-to-all | bytes 2097152 | tf_op jit(solution)/shard_map/all_to_all | solution.py:424
  83.3 0.3 collective-permute-start.3
  83.5 3.0 %collective-permute-start.4 = (bf16[128,4096]{1,0:T(8,128)(2,1)S(1)}, bf16[128,4096]{1,0:T(8,128)(2,1)S(1)}, u32[]{:S(2)}, u32[]{:S(2)}) collective-permute-start(bf16[128,4096]{1,0:T(8,128)(2,1)S(1)} %bitcast.19), channel_id=1, source_target_pairs={{0,96},{32,0},{64,32},{96,64},{1,97},{33,1},{65,33},{97,65},{2,98}... | collective-permute-start | bytes 3145736 | tf_op jit(solution)/shard_map/ppermute | solution.py:420
  86.5 18.9 %all_to_all.32 = bf16[16,8,4096]{2,1,0:T(8,128)(2,1)S(1)} all-to-all(bf16[16,8,4096]{2,1,0:T(8,128)(2,1)S(1)} %get-tuple-element.50), channel_id=1, replica_groups=mesh['x'=4,'core'=2,'seq'=16] {'seq'}, dimensions={0} | all-to-all | bytes 2097152 | tf_op jit(solution)/shard_map/all_to_all | solution.py:424
  105.4 2.5 %collective-permute-done.3.left_ref = bf16[128,4096]{1,0:T(8,128)(2,1)S(1)} collective-permute-done((bf16[128,4096]{1,0:T(8,128)(2,1)S(1)}, bf16[128,4096]{1,0:T(8,128)(2,1)S(1)}, u32[]{:S(2)}, u32[]{:S(2)}) %collective-permute-start.3) | collective-permute-done | bytes 1048608 | tf_op jit(solution)/shard_map/ppermute | solution.py:419
  108.0 3.2 %collective-permute-start.12 = (bf16[128,4096]{1,0:T(8,128)(2,1)S(1)}, bf16[128,4096]{1,0:T(8,128)(2,1)S(1)}, u32[]{:S(2)}, u32[]{:S(2)}) collective-permute-start(bf16[128,4096]{1,0:T(8,128)(2,1)S(1)} %bitcast.15), channel_id=1, source_target_pairs={{0,96},{32,0},{64,32},{96,64},{1,97},{33,1},{65,33},{97,65},{2,98}... | collective-permute-start | bytes 3145736 | tf_op jit(solution)/shard_map/ppermute | solution.py:420
  111.2 20.5 %collective-permute-done.5.far_ref = bf16[128,4096]{1,0:T(8,128)(2,1)S(1)} collective-permute-done((bf16[128,4096]{1,0:T(8,128)(2,1)S(1)}, bf16[128,4096]{1,0:T(8,128)(2,1)S(1)}, u32[]{:S(2)}, u32[]{:S(2)}) %collective-permute-start.5) | collective-permute-done | bytes 1048608 | tf_op jit(solution)/shard_map/ppermute | solution.py:419
  131.7 3.2 %collective-permute-start.13 = (bf16[128,4096]{1,0:T(8,128)(2,1)S(1)}, bf16[128,4096]{1,0:T(8,128)(2,1)S(1)}, u32[]{:S(2)}, u32[]{:S(2)}) collective-permute-start(bf16[128,4096]{1,0:T(8,128)(2,1)S(1)} %collective-permute-done.12.right_ref), channel_id=1, source_target_pairs={{0,96},{32,0},{64,32},{96,64},{1,97},{33,1},{65,33},{97,65},{2,98}... | collective-permute-start | bytes 3145736 | tf_op jit(solution)/shard_map/ppermute | solution.py:420
  135.0 20.7 %shard_map.123 = (bf16[128,4096]{1,0:T(8,128)(2,1)S(1)}, bf16[128,4096]{1,0:T(8,128)(2,1)S(1)}, bf16[128,4096]{1,0:T(8,128)(2,1)S(1)}, bf16[128,4096]{1,0:T(8,128)(2,1)S(1)}) custom-call(bf16[128,4096]{1,0:T(8,128)(2,1)S(1)} %bitcast.20, bf16[128,4096]{1,0:T(8,128)(2,1)S(1)} %collective-permute-done.3.left_ref, ...), custom_call_target="tpu_custom_call" | custom-call | flops 14495514624 | bytes 36700160 | tf_op jit(solution)/shard_map/pallas_call | solution.py:373
  155.7 0.1 collective-permute-start.10
  155.8 2.0 collective-permute-start.8
  157.8 1.0 copy-done.14
  158.8 20.7 %shard_map.124 = (bf16[128,4096]{1,0:T(8,128)(2,1)S(1)}, bf16[128,4096]{1,0:T(8,128)(2,1)S(1)}, bf16[128,4096]{1,0:T(8,128)(2,1)S(1)}, bf16[128,4096]{1,0:T(8,128)(2,1)S(1)}) custom-call(bf16[128,4096]{1,0:T(8,128)(2,1)S(1)} %bitcast.17, bf16[128,4096]{1,0:T(8,128)(2,1)S(1)} %collective-permute-done.11.left_ref, ...), custom_call_target="tpu_custom_call" | custom-call | flops 14495514624 | bytes 36700160 | tf_op jit(solution)/shard_map/pallas_call | solution.py:373
  179.5 1.6 collective-permute-start.14
  181.1 0.2 add_convert_fusion.3
  181.3 0.6 collective-permute-start.9
  181.9 20.7 %collective-permute-done.14 = bf16[128,4096]{1,0:T(8,128)(2,1)S(1)} collective-permute-done((bf16[128,4096]{1,0:T(8,128)(2,1)S(1)}, bf16[128,4096]{1,0:T(8,128)(2,1)S(1)}, u32[]{:S(2)}, u32[]{:S(2)}) %collective-permute-start.14) | collective-permute-done | bytes 1048608 | tf_op jit(solution)/shard_map/ppermute | solution.py:420
  202.6 0.2 add_convert_fusion.1
  202.8 1.6 collective-permute-start.16
  204.4 0.5 collective-permute-start.15
  204.9 0.5 fusion
  205.4 17.2 %all_to_all.33.returned_ref = bf16[16,8,4096]{2,1,0:T(8,128)(2,1)S(1)} all-to-all(bf16[16,8,4096]{2,1,0:T(8,128)(2,1)S(1)} %fusion), channel_id=1, replica_groups=mesh['x'=4,'core'=2,'seq'=16] {'seq'}, dimensions={0} | all-to-all | bytes 2097152 | tf_op jit(solution)/shard_map/all_to_all | solution.py:424
  222.6 0.9 shard_map.125
  223.5 2.3 collective-permute-done.15
  225.8 0.5 fusion.1
  226.3 18.5 %all_to_all.34.returned_ref = bf16[16,8,4096]{2,1,0:T(8,128)(2,1)S(1)} all-to-all(bf16[16,8,4096]{2,1,0:T(8,128)(2,1)S(1)} %fusion.1), channel_id=1, replica_groups=mesh['x'=4,'core'=2,'seq'=16] {'seq'}, dimensions={0} | all-to-all | bytes 2097152 | tf_op jit(solution)/shard_map/all_to_all | solution.py:424
  244.7 1.4 shard_map.126
  (40 shorter events, 0.1 us)
Async XLA Ops:
  0.0 11.8 %copy-start = (bf16[128,4096]{1,0:T(8,128)(2,1)S(1)}, bf16[128,4096]{1,0:T(8,128)(2,1)}, u32[]{:S(2)}) copy-start(bf16[128,4096]{1,0:T(8,128)(2,1)} %query_ref.3) | copy-start | bytes 3145732
  0.0 11.9 %copy-start.9 = (f32[4096]{0:T(1024)S(1)}, f32[4096]{0:T(1024)}, u32[]{:S(2)}) copy-start(f32[4096]{0:T(1024)} %param.18) | copy-start | bytes 49156
  0.0 11.9 %copy-start.12 = (s32[128,2]{0,1:T(2,128)S(1)}, s32[128,2]{0,1:T(2,128)}, u32[]{:S(2)}) copy-start(s32[128,2]{0,1:T(2,128)} %param.20) | copy-start | bytes 3076
  3.4 8.5 %copy-start.11 = (f32[32,128]{1,0:T(8,128)S(1)}, f32[32,128]{1,0:T(8,128)}, u32[]{:S(2)}) copy-start(f32[32,128]{1,0:T(8,128)} %get-tuple-element.38.by_head_ref) | copy-start | bytes 49156
  3.4 26.6 %all-to-all-start = ((bf16[32,136,128]{2,1,0:T(8,128)(2,1)}), bf16[32,136,128]{2,1,0:T(8,128)(2,1)S(1)}, u32[]{:S(2)}, u32[]{:S(2)}) async-start(bf16[32,136,128]{2,1,0:T(8,128)(2,1)} %get-tuple-element.41), calls=%async_computation | async-start | bytes 2228224 | tf_op jit(solution)/shard_map/all_to_all | solution.py:424
  11.9 1.2 copy-start.1
  13.1 1.2 copy-start.2
  14.3 1.2 copy-start.7
  20.7 1.4 copy-start.3
  22.0 1.3 copy-start.5
  30.3 5.7 %collective-permute-start = (bf16[136,128]{1,0:T(8,128)(2,1)S(1)}, bf16[136,128]{1,0:T(8,128)(2,1)S(1)}, u32[]{:S(2)}, u32[]{:S(2)}) collective-permute-start(bf16[136,128]{1,0:T(8,128)(2,1)S(1)} %get-tuple-element.45), channel_id=1, source_target_pairs={{0,32},{32,64},{64,96},{96,0},{1,33},{33,65},{65,97},{97,1},{2,34}... | collective-permute-start | bytes 104456 | tf_op jit(solution)/shard_map/ppermute | solution.py:421
  31.8 5.4 %collective-permute-start.1 = (bf16[136,128]{1,0:T(8,128)(2,1)S(1)}, bf16[136,128]{1,0:T(8,128)(2,1)S(1)}, u32[]{:S(2)}, u32[]{:S(2)}) collective-permute-start(bf16[136,128]{1,0:T(8,128)(2,1)S(1)} %get-tuple-element.45), channel_id=1, source_target_pairs={{0,64},{32,96},{64,0},{96,32},{1,65},{33,97},{65,1},{97,33},{2,66}... | collective-permute-start | bytes 104456 | tf_op jit(solution)/shard_map/ppermute | solution.py:421
  34.6 3.9 %collective-permute-start.2 = (bf16[136,128]{1,0:T(8,128)(2,1)S(1)}, bf16[136,128]{1,0:T(8,128)(2,1)S(1)}, u32[]{:S(2)}, u32[]{:S(2)}) collective-permute-start(bf16[136,128]{1,0:T(8,128)(2,1)S(1)} %get-tuple-element.45), channel_id=1, source_target_pairs={{0,96},{32,0},{64,32},{96,64},{1,97},{33,1},{65,33},{97,65},{2,98}... | collective-permute-start | bytes 104456 | tf_op jit(solution)/shard_map/ppermute | solution.py:421
  38.6 21.3 %copy-start.4 = (f32[128,4096]{1,0:T(8,128)S(1)}, f32[128,4096]{1,0:T(8,128)}, u32[]{:S(2)}) copy-start(f32[128,4096]{1,0:T(8,128)} %copy-done.3) | copy-start | bytes 6291460
  38.6 21.3 %copy-start.6 = (f32[128,4096]{1,0:T(8,128)S(1)}, f32[128,4096]{1,0:T(8,128)}, u32[]{:S(2)}) copy-start(f32[128,4096]{1,0:T(8,128)} %copy-done.5) | copy-start | bytes 6291460
  38.6 21.3 %copy-start.8 = (bf16[128,4096]{1,0:T(8,128)(2,1)S(1)}, bf16[128,4096]{1,0:T(8,128)(2,1)}, u32[]{:S(2)}) copy-start(bf16[128,4096]{1,0:T(8,128)(2,1)} %residual_ref.1) | copy-start | bytes 3145732
  38.6 21.3 %copy-start.10 = (f32[4096]{0:T(1024)S(1)}, f32[4096]{0:T(1024)}, u32[]{:S(2)}) copy-start(f32[4096]{0:T(1024)} %param.19) | copy-start | bytes 49156
  62.3 72.7 %collective-permute-start.6 = (bf16[2,576,4096]{2,1,0:T(8,128)(2,1)}, bf16[2,576,4096]{2,1,0:T(8,128)(2,1)}, u32[]{:S(2)}, u32[]{:S(2)}) collective-permute-start(bf16[2,576,4096]{2,1,0:T(8,128)(2,1)} %bitcast.27), channel_id=1, source_target_pairs={{0,16},{16,0},{1,17},{17,1},{2,18},{18,2},{3,19},{19,3},{4,20},{20... | collective-permute-start | bytes 28311560 | tf_op jit(solution)/shard_map/ppermute | solution.py:418
  62.4 45.6 %collective-permute-start.7 = (bf16[576,4096]{1,0:T(8,128)(2,1)}, bf16[576,4096]{1,0:T(8,128)(2,1)}, u32[]{:S(2)}, u32[]{:S(2)}) collective-permute-start(bf16[576,4096]{1,0:T(8,128)(2,1)} %bitcast.30), channel_id=1, source_target_pairs={{0,16},{16,0},{1,17},{17,1},{2,18},{18,2},{3,19},{19,3},{4,20},{20... | collective-permute-start | bytes 14155784 | tf_op jit(solution)/shard_map/ppermute | solution.py:418
  83.3 24.7 %collective-permute-start.3 = (bf16[128,4096]{1,0:T(8,128)(2,1)S(1)}, bf16[128,4096]{1,0:T(8,128)(2,1)S(1)}, u32[]{:S(2)}, u32[]{:S(2)}) collective-permute-start(bf16[128,4096]{1,0:T(8,128)(2,1)S(1)} %bitcast.18), channel_id=1, source_target_pairs={{0,32},{32,64},{64,96},{96,0},{1,33},{33,65},{65,97},{97,1},{2,34}... | collective-permute-start | bytes 3145736 | tf_op jit(solution)/shard_map/ppermute | solution.py:419
  83.5 24.4 %collective-permute-start.4 = (bf16[128,4096]{1,0:T(8,128)(2,1)S(1)}, bf16[128,4096]{1,0:T(8,128)(2,1)S(1)}, u32[]{:S(2)}, u32[]{:S(2)}) collective-permute-start(bf16[128,4096]{1,0:T(8,128)(2,1)S(1)} %bitcast.19), channel_id=1, source_target_pairs={{0,96},{32,0},{64,32},{96,64},{1,97},{33,1},{65,33},{97,65},{2,98}... | collective-permute-start | bytes 3145736 | tf_op jit(solution)/shard_map/ppermute | solution.py:420
  108.0 23.8 %collective-permute-start.5 = (bf16[128,4096]{1,0:T(8,128)(2,1)S(1)}, bf16[128,4096]{1,0:T(8,128)(2,1)S(1)}, u32[]{:S(2)}, u32[]{:S(2)}) collective-permute-start(bf16[128,4096]{1,0:T(8,128)(2,1)S(1)} %collective-permute-done.3.left_ref), channel_id=1, source_target_pairs={{0,32},{32,64},{64,96},{96,0},{1,33},{33,65},{65,97},{97,1},{2,34}... | collective-permute-start | bytes 3145736 | tf_op jit(solution)/shard_map/ppermute | solution.py:419
  108.0 23.8 %collective-permute-start.12 = (bf16[128,4096]{1,0:T(8,128)(2,1)S(1)}, bf16[128,4096]{1,0:T(8,128)(2,1)S(1)}, u32[]{:S(2)}, u32[]{:S(2)}) collective-permute-start(bf16[128,4096]{1,0:T(8,128)(2,1)S(1)} %bitcast.15), channel_id=1, source_target_pairs={{0,96},{32,0},{64,32},{96,64},{1,97},{33,1},{65,33},{97,65},{2,98}... | collective-permute-start | bytes 3145736 | tf_op jit(solution)/shard_map/ppermute | solution.py:420
  131.7 3.2 %copy-start.15 = (bf16[128,4096]{1,0:T(8,128)(2,1)}, bf16[128,4096]{1,0:T(8,128)(2,1)S(1)}, u32[]{:S(2)}) copy-start(bf16[128,4096]{1,0:T(8,128)(2,1)S(1)} %collective-permute-done.5.far_ref) | copy-start | bytes 3145732
  131.7 26.1 %collective-permute-start.11 = (bf16[128,4096]{1,0:T(8,128)(2,1)S(1)}, bf16[128,4096]{1,0:T(8,128)(2,1)S(1)}, u32[]{:S(2)}, u32[]{:S(2)}) collective-permute-start(bf16[128,4096]{1,0:T(8,128)(2,1)S(1)} %bitcast.16), channel_id=1, source_target_pairs={{0,32},{32,64},{64,96},{96,0},{1,33},{33,65},{65,97},{97,1},{2,34}... | collective-permute-start | bytes 3145736 | tf_op jit(solution)/shard_map/ppermute | solution.py:419
  131.7 26.1 %collective-permute-start.13 = (bf16[128,4096]{1,0:T(8,128)(2,1)S(1)}, bf16[128,4096]{1,0:T(8,128)(2,1)S(1)}, u32[]{:S(2)}, u32[]{:S(2)}) collective-permute-start(bf16[128,4096]{1,0:T(8,128)(2,1)S(1)} %collective-permute-done.12.right_ref), channel_id=1, source_target_pairs={{0,96},{32,0},{64,32},{96,64},{1,97},{33,1},{65,33},{97,65},{2,98}... | collective-permute-start | bytes 3145736 | tf_op jit(solution)/shard_map/ppermute | solution.py:420
  155.7 23.8 %collective-permute-start.10 = (bf16[128,4096]{1,0:T(8,128)(2,1)S(1)}, bf16[128,4096]{1,0:T(8,128)(2,1)S(1)}, u32[]{:S(2)}, u32[]{:S(2)}) collective-permute-start(bf16[128,4096]{1,0:T(8,128)(2,1)S(1)} %get-tuple-element.57), channel_id=1, source_target_pairs={{0,96},{32,0},{64,32},{96,64},{1,97},{33,1},{65,33},{97,65},{2,98}... | collective-permute-start | bytes 3145736 | tf_op jit(solution)/shard_map/ppermute | solution.py:420
  155.8 23.7 %collective-permute-start.8 = (bf16[128,4096]{1,0:T(8,128)(2,1)S(1)}, bf16[128,4096]{1,0:T(8,128)(2,1)S(1)}, u32[]{:S(2)}, u32[]{:S(2)}) collective-permute-start(bf16[128,4096]{1,0:T(8,128)(2,1)S(1)} %get-tuple-element.56), channel_id=1, source_target_pairs={{0,32},{32,64},{64,96},{96,0},{1,33},{33,65},{65,97},{97,1},{2,34}... | collective-permute-start | bytes 3145736 | tf_op jit(solution)/shard_map/ppermute | solution.py:419
  157.8 1.0 copy-start.14
  179.5 23.1 %collective-permute-start.14 = (bf16[128,4096]{1,0:T(8,128)(2,1)S(1)}, bf16[128,4096]{1,0:T(8,128)(2,1)S(1)}, u32[]{:S(2)}, u32[]{:S(2)}) collective-permute-start(bf16[128,4096]{1,0:T(8,128)(2,1)S(1)} %get-tuple-element.62), channel_id=1, source_target_pairs={{0,96},{32,0},{64,32},{96,64},{1,97},{33,1},{65,33},{97,65},{2,98}... | collective-permute-start | bytes 3145736 | tf_op jit(solution)/shard_map/ppermute | solution.py:420
  181.3 23.1 %collective-permute-start.9 = (bf16[128,4096]{1,0:T(8,128)(2,1)S(1)}, bf16[128,4096]{1,0:T(8,128)(2,1)S(1)}, u32[]{:S(2)}, u32[]{:S(2)}) collective-permute-start(bf16[128,4096]{1,0:T(8,128)(2,1)S(1)} %add_convert_fusion.3), channel_id=1, source_target_pairs={{0,32},{32,64},{64,96},{96,0},{1,33},{33,65},{65,97},{97,1},{2,34}... | collective-permute-start | bytes 3145736 | tf_op jit(solution)/shard_map/ppermute | solution.py:419
  202.8 20.7 %collective-permute-start.16 = (bf16[128,4096]{1,0:T(8,128)(2,1)S(1)}, bf16[128,4096]{1,0:T(8,128)(2,1)S(1)}, u32[]{:S(2)}, u32[]{:S(2)}) collective-permute-start(bf16[128,4096]{1,0:T(8,128)(2,1)S(1)} %add_convert_fusion.1), channel_id=1, source_target_pairs={{0,96},{32,0},{64,32},{96,64},{1,97},{33,1},{65,33},{97,65},{2,98}... | collective-permute-start | bytes 3145736 | tf_op jit(solution)/shard_map/ppermute | solution.py:420
  204.4 21.4 %collective-permute-start.15 = (bf16[128,4096]{1,0:T(8,128)(2,1)S(1)}, bf16[128,4096]{1,0:T(8,128)(2,1)S(1)}, u32[]{:S(2)}, u32[]{:S(2)}) collective-permute-start(bf16[128,4096]{1,0:T(8,128)(2,1)S(1)} %get-tuple-element.70), channel_id=1, source_target_pairs={{0,32},{32,64},{64,96},{96,0},{1,33},{33,65},{65,97},{97,1},{2,34}... | collective-permute-start | bytes 3145736 | tf_op jit(solution)/shard_map/ppermute | solution.py:419
  205.4 17.2 %copy-start.13 = (f32[128,2]{0,1:T(2,128)S(1)}, f32[128,2]{0,1:T(2,128)}, u32[]{:S(2)}) copy-start(f32[128,2]{0,1:T(2,128)} %param.21) | copy-start | bytes 3076
